TPU v7x, 128 devices: a whole 4x4x4 slice. The times are simulated.
128 devices in a mesh: snap: 2 (over core), tile: 64 (over z, y, x).
Axes of the slice: x: 4, y: 4, z: 4, core: 2. Of those that a mesh axis runs over, the one named last changes fastest.
Arguments:
- velocity: float32 [256, 2, 4096, 256], P('snap', None, 'tile'), may hold values from -48 to 48
- offsets: int32 [256, 2], P('snap'), may hold values from -16 to 16
- phase: int32 [256], P('snap'), may hold values from 0 to 71
Outputs:
- phase_mean: float32 [72, 2, 4096, 256], P('snap', None, 'tile')
- phase_moment: float32 [72, 3, 4096, 256], P('snap', None, 'tile')
Inputs may be any that keep to these rules, and one draw needn't show every extreme that they name: `offsets`: column 0 shifts rows and column 1 shifts columns.
All inputs are finite; a program needn't handle non-finite values.
Results may differ from a plain program's by a relative error of at most 0.0003.
Values sent between devices are 32-bit elements; how exact they have to be, the bound alone decides.
A program may use at most 256 MiB of HBM per device.

v0:
```python
import jax
import jax.numpy as jnp
from jax import lax
from jax.sharding import PartitionSpec as P

PHASES = 72
RAD = 8
HALO = 24


def extended(array, sides, width):
    for axis, dim in sides:
        size, length = (lax.axis_size(axis), array.shape[dim])
        up = [(i, (i + 1) % size) for i in range(size - 1)]
        down = [(j, i) for i, j in up]
        last = lax.slice_in_dim(array, length - width, length, axis=dim)
        initial = lax.slice_in_dim(array, 0, width, axis=dim)
        before = lax.ppermute(last, axis, up)
        after = lax.ppermute(initial, axis, down)
        array = jnp.concatenate([before, array, after], axis=dim)
    return array


def gauss_total():
    steps = jnp.arange(2 * RAD + 1, dtype=jnp.float32) - RAD
    sigma = RAD / 2.0
    return jnp.sum(jnp.exp(-steps * steps / (2.0 * sigma * sigma)))


def tap_weight(distance, total):
    sigma = RAD / 2.0
    spread = distance.astype(jnp.float32)
    inside = (distance >= -RAD) & (distance <= RAD)
    value = jnp.exp(-spread * spread / (2.0 * sigma * sigma)) / total
    return jnp.where(inside, value, jnp.float32(0.0))


def row_operator(shift_rows, first_row, out_rows, padded_rows, total_rows, total):
    target = jnp.arange(out_rows, dtype=jnp.int32)[None, :, None]
    source = jnp.arange(padded_rows, dtype=jnp.int32)[None, None, :]
    tap = source - HALO - shift_rows[:, None, None] - target
    seen = first_row + target + tap
    valid = (seen >= 0) & (seen < total_rows)
    return jnp.where(valid, tap_weight(tap, total), jnp.float32(0.0))


def column_operator(shift_cols, width, total):
    source = jnp.arange(width, dtype=jnp.int32)[None, :, None]
    target = jnp.arange(width, dtype=jnp.int32)[None, None, :]
    moved = source - shift_cols[:, None, None]
    tap = moved - target
    valid = (moved >= 0) & (moved < width)
    return jnp.where(valid, tap_weight(tap, total), jnp.float32(0.0))


def smooth_all(padded, shift_rows, shift_cols, first_row, out_rows, total_rows, total):
    width = padded.shape[3]
    rows_op = row_operator(shift_rows, first_row, out_rows, padded.shape[2], total_rows, total)
    cols_op = column_operator(shift_cols, width, total)
    vertical = jnp.einsum("nir,ncrw->nciw", rows_op, padded, precision=lax.Precision.HIGHEST)
    return jnp.einsum("nciw,nwj->ncij", vertical, cols_op, precision=lax.Precision.HIGHEST)


def per_device(velocity, offsets, phase):
    total = gauss_total()
    local_rows = velocity.shape[2]
    tiles = lax.axis_size("tile")
    total_rows = local_rows * tiles
    wide = extended(velocity, (("tile", 2),), HALO)
    first = lax.axis_index("tile") * local_rows
    smooth = smooth_all(wide, offsets[:, 0], offsets[:, 1], first, local_rows, total_rows, total)
    fields = jnp.concatenate(
        [
            smooth,
            smooth[:, 0:1] * smooth[:, 0:1],
            smooth[:, 1:2] * smooth[:, 1:2],
            smooth[:, 0:1] * smooth[:, 1:2],
        ],
        axis=1,
    )
    onehot = (phase[:, None] == jnp.arange(PHASES, dtype=jnp.int32)[None, :]).astype(jnp.float32)
    partial_sums = jnp.einsum("sp,scrw->pcrw", onehot, fields, precision=lax.Precision.HIGHEST)
    partial_count = jnp.sum(onehot, axis=0)
    sums, count = (
        lax.psum_scatter(partial_sums, "snap", scatter_dimension=0, tiled=True),
        lax.psum_scatter(partial_count, "snap", scatter_dimension=0, tiled=True),
    )
    scale = 1.0 / jnp.maximum(count, 1.0)
    phase_mean = sums[:, 0:2] * scale[:, None, None, None]
    phase_moment = sums[:, 2:5] * scale[:, None, None, None]
    return (phase_mean, phase_moment)


def solution(mesh):
    in_specs = (P("snap", None, "tile", None), P("snap", None), P("snap"))
    out_specs = (P("snap", None, "tile", None), P("snap", None, "tile", None))
    return jax.shard_map(
        per_device, mesh=mesh, in_specs=in_specs, out_specs=out_specs, check_vma=False
    )
```

profile of v0, /device:TPU:97, one launch (start us, length us, event | category | flops | bytes accessed | tf_op | source)
XLA Modules:
  0.0 403.2 jit_solution(14071226564511086696)
XLA Ops:
  7.2 0.0 copy-start
  7.2 0.0 reduce-scatter.2.cloned.1.call-start
  7.2 10.8 %fusion.75 = (f32[128,2,24,256]{3,2,1,0:T(8,128)}, f32[128,2,24,256]{3,2,1,0:T(8,128)}) fusion(f32[128,2,64,256]{3,2,1,0:T(8,128)} %param.3), kind=kLoop, calls=%fused_computation.88 | loop fusion | bytes 25165824 | tf_op jit(solution)/shard_map/slice | solution.py:16
  18.0 3.1 collective-permute-start
  21.1 6.4 %collective-permute-start.1 = (f32[128,2,24,256]{3,2,1,0:T(8,128)}, f32[128,2,24,256]{3,2,1,0:T(8,128)}, u32[]{:S(2)}, u32[]{:S(2)}) collective-permute-start(f32[128,2,24,256]{3,2,1,0:T(8,128)} %get-tuple-element.8), channel_id=1, source_target_pairs={{1,0},{2,1},{3,2},{4,3},{5,4},{6,5},{7,6},{8,7},{9,8},{10,9},{11,1... | collective-permute-start | bytes 18874376 | tf_op jit(solution)/shard_map/ppermute | solution.py:19
  27.5 0.6 fusion.62
  28.1 0.0 copy-done
  28.2 0.1 compare_and_fusion
  28.3 0.1 broadcast_subtract_fusion
  28.3 0.1 iota_subtract_fusion.4
  28.4 132.4 %collective-permute-done = f32[128,2,24,256]{3,2,1,0:T(8,128)} collective-permute-done((f32[128,2,24,256]{3,2,1,0:T(8,128)}, f32[128,2,24,256]{3,2,1,0:T(8,128)}, u32[]{:S(2)}, u32[]{:S(2)}) %collective-permute-start) | collective-permute-done | bytes 6291488 | tf_op jit(solution)/shard_map/ppermute | solution.py:18
  160.8 0.9 collective-permute-done.1
  161.7 26.2 %fusion.16 = f32[128,2,256,64]{2,3,1,0:T(8,128)} fusion(f32[128,2,24,256]{3,2,1,0:T(8,128)} %collective-permute-done.1, f32[128,2,64,256]{3,2,1,0:T(8,128)} %param.3, f32[128,2,24,256]{3,2,1,0:T(8,128)} %collective-permute-done, f32[]{:T(128)} %fusion.62, s32[128,112]{1,0:T(8,128)S(1)} %broadcast_subtract_fusion, s32[64]{0:T(128)S(1)} %iota_add_fusion.1), kind=kOutput, calls=%fused_computation.16 | convolution fusion | flops 5665587200 | bytes 46194948 | tf_op jit(solution)/shard_map/nir,ncrw->nciw/dot_general | solution.py:60
  187.8 44.9 %fusion.8 = f32[128,2,64,256]{3,2,1,0:T(8,128)} fusion(f32[128,2,256,64]{2,3,1,0:T(8,128)} %fusion.16, f32[]{:T(128)} %fusion.62, s32[128,256]{1,0:T(8,128)S(1)} %iota_subtract_fusion.4, pred[128,256]{1,0:T(8,128)(4,1)S(1)} %compare_and_fusion), kind=kOutput, calls=%fused_computation.10 | convolution fusion | flops 12977176576 | bytes 33718276 | tf_op jit(solution)/shard_map/nciw,nwj->ncij/dot_general | solution.py:61
  232.8 11.1 %slice_multiply_fusion.2 = (f32[128,1,64,256]{3,2,1,0:T(8,128)S(1)}, f32[128,1,64,256]{3,2,1,0:T(8,128)}, f32[128,1,64,256]{3,2,1,0:T(8,128)}) fusion(f32[128,2,64,256]{3,2,1,0:T(8,128)} %fusion.8), kind=kLoop, calls=%fused_computation.32 | loop fusion | flops 6291456 | bytes 41943040 | tf_op jit(solution)/shard_map/mul | solution.py:75
  243.9 0.0 copy-start.1
  243.9 26.8 %pad_maximum_fusion = f32[128,5,64,256]{3,2,1,0:T(8,128)} fusion(f32[128,1,64,256]{3,2,1,0:T(8,128)} %get-tuple-element.5, f32[128,1,64,256]{3,2,1,0:T(8,128)} %get-tuple-element.6, f32[128,1,64,256]{3,2,1,0:T(8,128)S(1)} %get-tuple-element.4, f32[128,2,64,256]{3,2,1,0:T(8,128)} %fusion.8), kind=kLoop, calls=%fused_computation.1 | loop fusion | flops 31457280 | bytes 83886080 | tf_op jit(solution)/shard_map/concatenate | solution.py:72
  270.7 0.0 copy-done.1
  270.7 50.5 %fusion = f32[72,5,64,256]{3,0,2,1:T(8,128)} fusion(f32[128,5,64,256]{3,2,1,0:T(8,128)} %pad_maximum_fusion, s32[128]{0:T(128)S(1)} %copy-done.1), kind=kOutput, calls=%fused_computation.2 | convolution fusion | flops 9059705856 | bytes 65536512 | tf_op jit(solution)/shard_map/sp,scrw->pcrw/dot_general | solution.py:82
  321.2 22.0 %copy.9 = f32[72,5,64,256]{3,2,1,0:T(8,128)} copy(f32[72,5,64,256]{3,0,2,1:T(8,128)} %fusion) | data formatting | bytes 47185920 | tf_op jit(solution)/shard_map/sp,scrw->pcrw/dot_general | solution.py:82
  343.3 0.0 copy-start.2
  343.3 0.0 reduce-scatter.2.cloned.1.call-update
  343.3 0.6 copy-done.2
  343.9 0.6 dynamic-slice
  345.2 0.1 convert_reduce_fusion
  345.3 4.0 all-reduce
  349.3 0.1 fusion.63
  349.3 34.4 %reduce-scatter.2.cloned.1.call-done = f32[36,5,64,256]{3,2,1,0:T(8,128)} async-done(((f32[72,5,64,256]{3,2,1,0:T(8,128)}), f32[36,5,64,256]{3,2,1,0:T(8,128)}) %reduce-scatter.2.cloned.1.call-update) | async-done | bytes 11796496 | tf_op jit(solution)/shard_map/reduce_scatter | solution.py:85
  383.8 7.3 %slice_multiply_fusion.3 = f32[36,3,64,256]{3,2,1,0:T(8,128)} fusion(f32[36,5,64,256]{3,2,1,0:T(8,128)} %reduce-scatter.2.cloned.1.call-done, f32[36]{0:T(128)S(1)} %fusion.63), kind=kLoop, calls=%fused_computation.33 | loop fusion | flops 1769472 | bytes 14155920 | tf_op jit(solution)/shard_map/mul | solution.py:90
  391.1 5.3 %slice_multiply_fusion.4 = f32[36,2,64,256]{3,2,1,0:T(8,128)} fusion(f32[36,5,64,256]{3,2,1,0:T(8,128)} %reduce-scatter.2.cloned.1.call-done, f32[36]{0:T(128)S(1)} %fusion.63), kind=kLoop, calls=%fused_computation.35 | loop fusion | flops 1179648 | bytes 9437328 | tf_op jit(solution)/shard_map/mul | solution.py:89
  (3 shorter events, 0.0 us)
Async XLA Ops:
  7.2 21.0 %copy-start = (s32[128,2]{0,1:T(2,128)S(1)}, s32[128,2]{0,1:T(2,128)}, u32[]{:S(2)}) copy-start(s32[128,2]{0,1:T(2,128)} %param.4) | copy-start | bytes 3076
  7.2 376.6 %reduce-scatter.2.cloned.1.call-start = ((), (), s32[]{:S(2)}) async-start(), calls=%async_computation.1 | async-start | bytes 35389440 | tf_op jit(solution)/shard_map/reduce_scatter | solution.py:85
  18.0 142.8 %collective-permute-start = (f32[128,2,24,256]{3,2,1,0:T(8,128)}, f32[128,2,24,256]{3,2,1,0:T(8,128)}, u32[]{:S(2)}, u32[]{:S(2)}) collective-permute-start(f32[128,2,24,256]{3,2,1,0:T(8,128)} %get-tuple-element.7), channel_id=1, source_target_pairs={{0,1},{1,2},{2,3},{3,4},{4,5},{5,6},{6,7},{7,8},{8,9},{9,10},{10,1... | collective-permute-start | bytes 18874376 | tf_op jit(solution)/shard_map/ppermute | solution.py:18
  21.1 140.5 %collective-permute-start.1 = (f32[128,2,24,256]{3,2,1,0:T(8,128)}, f32[128,2,24,256]{3,2,1,0:T(8,128)}, u32[]{:S(2)}, u32[]{:S(2)}) collective-permute-start(f32[128,2,24,256]{3,2,1,0:T(8,128)} %get-tuple-element.8), channel_id=1, source_target_pairs={{1,0},{2,1},{3,2},{4,3},{5,4},{6,5},{7,6},{8,7},{9,8},{10,9},{11,1... | collective-permute-start | bytes 18874376 | tf_op jit(solution)/shard_map/ppermute | solution.py:19
  243.9 26.8 %copy-start.1 = (s32[128]{0:T(128)S(1)}, s32[128]{0:T(128)}, u32[]{:S(2)}) copy-start(s32[128]{0:T(128)} %param.5) | copy-start | bytes 1540
  343.3 0.7 copy-start.2
Sparse Core Ops, SparseCore 0:
  343.4 40.3 reduce-scatter.1
where the time goes:
time: 405 us; the launch traced here: 403 us
  waiting for transfers between devices  168 us (41%)
  matrix products  122 us (30%)
  other arithmetic  51.6 us (13%)
  local copies, waits for them, and re-layouts  34 us (8%)
  between operations  14.8 us (4%)
  starting transfers between devices  9.53 us (2%)
    ppermute x1, waiting for transfers between devices, extended(): before = lax.ppermute(last, axis, up)  132 us
    dot_general x1, matrix products, per_device(): jnp.einsum('sp,scrw->pcrw', onehot, fields, precision=lax.Precision.HIGHEST)  50.5 us
    dot_general x1, matrix products, smooth_all(): jnp.einsum('nciw,nwj->ncij', vertical, cols_op, precision=lax.Precision.H...  44.9 us
    reduce_scatter x1, waiting for transfers between devices, per_device(): lax.psum_scatter(partial_sums, 'snap', scatter_dimension=0, tiled=True)  34.4 us
    concatenate x1, other arithmetic, per_device(): jnp.concatenate([smooth, smooth[:, 0:1] * smooth[:, 0:1], smooth[:, 1:2]...  26.8 us
    dot_general x1, matrix products, smooth_all(): jnp.einsum('nir,ncrw->nciw', rows_op, padded, precision=lax.Precision.HIG...  26.2 us
    dot_general x1, local copies, waits for them, and re-layouts, per_device(): jnp.einsum('sp,scrw->pcrw', onehot, fields, precision=lax.Precision.HIGHEST)  22 us
    mul x1, other arithmetic, per_device(): smooth[:, 0:1] * smooth[:, 0:1]  11.1 us
  transfers between devices with their start and end apart: 3, of which 3 were waited for; matrix products, arithmetic and copies ran while one was open for 0% of the time, Pallas kernels for 0%

commit v1 on v0

v1 whole, which is shorter than its diff:
```python
import functools

import jax
import jax.numpy as jnp
import numpy as np
from jax import lax
from jax.experimental import pallas as pl
from jax.experimental.pallas import tpu as pltpu
from jax.sharding import PartitionSpec as P

PHASES = 72
HALF = PHASES // 2
RAD = 8
MAXS = 16
HALO = RAD + MAXS
ROWS = 64
WIDTH = 256
SNAPS = 128
EXT = ROWS + 2 * HALO
STEP = 4
GAP = 16
VMEM_BYTES = 56 * 1024 * 1024
FIRST = 32
FIRST_CUTS = (480,)
REST_CUTS = (608, 1016, 1184)
F32 = jnp.float32
BF16 = jnp.bfloat16
I32 = jnp.int32


def taps():
    steps = np.arange(2 * RAD + 1, dtype=np.float64) - RAD
    sigma = RAD / 2.0
    values = np.exp(-steps * steps / (2.0 * sigma * sigma))
    return values / values.sum()


def split_const(values):
    high = values.astype(BF16)
    low = (values - high.astype(np.float64)).astype(BF16)
    return high, low


def column_constant():
    weight = taps()
    source = np.arange(WIDTH)[:, None]
    target = np.arange(WIDTH)[None, :]
    distance = source - target
    band = np.where(np.abs(distance) <= RAD, weight[np.clip(distance + RAD, 0, 2 * RAD)], 0.0)
    return np.stack(split_const(band))


def row_constant():
    weight = taps()
    target = np.arange(EXT)[None, :, None] - HALO
    source = np.arange(ROWS)[None, None, :]
    shift = np.arange(-MAXS, MAXS + 1)[:, None, None]
    distance = source - shift - target
    band = np.where(np.abs(distance) <= RAD, weight[np.clip(distance + RAD, 0, 2 * RAD)], 0.0)
    seen = source - shift
    kinds = []
    for kind in range(3):
        keep = np.ones_like(seen, dtype=bool)
        if kind == 0:
            keep = seen >= 0
        if kind == 2:
            keep = seen < ROWS
        high, low = split_const(np.where(keep, band, 0.0))
        kinds.append(np.concatenate([high, low, high], axis=2))
    return np.stack(kinds)


def level_rows(need, level):
    return jnp.clip(need - 8 * level, 0, 8)


def needs(dy):
    return jnp.clip(RAD + dy, 0, HALO), jnp.clip(RAD - dy, 0, HALO)


def next_start(end):
    return end // 8 * 8 + 16


def split(value):
    high = value.astype(BF16)
    return high, (value - high.astype(F32)).astype(BF16)


def smooth_kernel(first, count, cuts, step, meta, vel, colop, rowop, *refs):
    pieces = len(cuts)
    y_refs, refs = refs[:3], refs[3:]
    out_up, out_dn = refs[:pieces], refs[pieces:2 * pieces]
    pos_ref = refs[2 * pieces]
    acc_out = refs[2 * pieces + 1]
    xs_hi, xs_lo, stack, ext, acc, up, dn, cursor, sem = refs[2 * pieces + 2:]
    at = pl.program_id(0)
    last = pl.num_programs(0) - 1

    @pl.when(at == 0)
    def _():
        def count_rows(n, sums):
            dy = meta[first + n]
            out = list(sums)
            for side, need in enumerate(needs(dy)):
                for level in range(3):
                    out[3 * side + level] += level_rows(need, level)
            return tuple(out)

        sums = lax.fori_loop(0, count, count_rows, (I32(0),) * 6)
        for side in range(2):
            start = I32(0)
            for level in range(3):
                cursor[3 * side + level] = start
                start = next_start(start + sums[3 * side + level])
        acc[...] = jnp.zeros_like(acc)

    lane = lax.broadcasted_iota(I32, (1, WIDTH), 1)
    for b in range(step):
        n = first + at * step + b
        dx = meta[SNAPS + n]
        rolled = pltpu.roll(vel[b].reshape(2 * ROWS, WIDTH), lax.rem(WIDTH - dx, WIDTH), 1)
        moved = lane + dx
        high, low = split(jnp.where((moved >= 0) & (moved < WIDTH), rolled, 0.0))
        xs_hi[2 * ROWS * b:2 * ROWS * (b + 1)] = high
        xs_lo[2 * ROWS * b:2 * ROWS * (b + 1)] = low
    dot = functools.partial(jnp.dot, preferred_element_type=F32)
    for b in range(step):
        part = slice(2 * ROWS * b, 2 * ROWS * (b + 1))
        horizontal = dot(xs_hi[part], colop[0]) + dot(xs_hi[part], colop[1]) + dot(xs_lo[part], colop[0])
        high, low = split(horizontal)
        for comp in range(2):
            rows = slice(ROWS * comp, ROWS * (comp + 1))
            stack[b, comp, 0:ROWS] = high[rows]
            stack[b, comp, ROWS:2 * ROWS] = high[rows]
            stack[b, comp, 2 * ROWS:3 * ROWS] = low[rows]
    for b in range(step):
        n = first + at * step + b
        oper = rowop[0, meta[n] + MAXS]
        for comp in range(2):
            ext[b, comp] = dot(oper, stack[b, comp])
    row = lax.broadcasted_iota(I32, (8, WIDTH), 0)
    for b in range(step):
        local = at * step + b
        n = first + local
        for level in range(3):
            top = HALO + 8 * level
            bottom = HALO + ROWS - 8 - 8 * level
            y_refs[level][b, 0] = ext[b, :, top:top + 8]
            y_refs[level][b, 1] = ext[b, :, bottom:bottom + 8]
        phase = meta[2 * SNAPS + n]
        u = ext[b, 0, 2 * HALO:2 * HALO + 16]
        v = ext[b, 1, 2 * HALO:2 * HALO + 16]
        for at_field, field in enumerate((u, v, u * u, v * v, u * v)):
            acc[phase, at_field, 0] += field[0:8]
            acc[phase, at_field, 1] += field[8:16]
        for side, need in enumerate(needs(meta[n])):
            buffer = (up, dn)[side]
            for level in range(3):
                slot = 3 * side + level
                have = level_rows(need, level)
                pos = cursor[slot]
                cursor[slot] = pos + have
                pos_ref[6 * local + slot] = pos
                skew = lax.rem(pos, 8)
                base = pl.multiple_of(pos - skew, 8)
                source = 16 - 8 * level if side == 0 else HALO + ROWS + 8 * level
                turn = lax.rem(skew + have, 8) if side == 0 else skew
                for comp in range(2):
                    tile = pltpu.roll(ext[b, comp, source:source + 8], turn, 0)
                    old = buffer[comp, pl.ds(base, 8)]
                    buffer[comp, pl.ds(base, 8)] = jnp.where(row < skew, old, tile)
                    buffer[comp, pl.ds(base + 8, 8)] = tile

    @pl.when(at == last)
    def _():
        copies = [pltpu.make_async_copy(acc, acc_out, sem.at[0])]
        low = 0
        for piece, high in enumerate(cuts):
            for side in range(2):
                copies.append(pltpu.make_async_copy(
                    (up, dn)[side].at[:, low:high], (out_up, out_dn)[side][piece], sem.at[1 + 2 * piece + side]))
            low = high
        for copy in copies:
            copy.start()
        for copy in copies:
            copy.wait()


def smooth_part(meta, velocity, colop, rowop, kind_at, first, count, cuts):
    pieces = len(cuts)
    sizes = [high - low for low, high in zip((0,) + cuts[:-1], cuts)]
    any_space = pl.BlockSpec(memory_space=pl.ANY)
    steps = count // STEP
    piece_shapes = [jax.ShapeDtypeStruct((2, size, WIDTH), F32) for size in sizes]
    strip = jax.ShapeDtypeStruct((count, 2, 2, 8, WIDTH), F32)
    room = cuts[-1] + GAP
    out = pl.pallas_call(
        functools.partial(smooth_kernel, first, count, cuts, STEP),
        grid_spec=pltpu.PrefetchScalarGridSpec(
            num_scalar_prefetch=1,
            grid=(steps,),
            in_specs=[
                pl.BlockSpec((STEP, 2, ROWS, WIDTH), lambda i, m: (first // STEP + i, 0, 0, 0)),
                pl.BlockSpec((2, WIDTH, WIDTH), lambda i, m: (0, 0, 0)),
                pl.BlockSpec((1, 2 * MAXS + 1, EXT, 3 * ROWS), lambda i, m: (m[kind_at], 0, 0, 0)),
            ],
            out_specs=[pl.BlockSpec((STEP, 2, 2, 8, WIDTH), lambda i, m: (i, 0, 0, 0, 0))] * 3
            + [any_space] * (2 * pieces)
            + [pl.BlockSpec(memory_space=pltpu.SMEM), any_space],
            scratch_shapes=[
                pltpu.VMEM((STEP * 2 * ROWS, WIDTH), BF16),
                pltpu.VMEM((STEP * 2 * ROWS, WIDTH), BF16),
                pltpu.VMEM((STEP, 2, 3 * ROWS, WIDTH), BF16),
                pltpu.VMEM((STEP, 2, EXT, WIDTH), F32),
                pltpu.VMEM((PHASES, 5, 2, 8, WIDTH), F32),
                pltpu.VMEM((2, room, WIDTH), F32),
                pltpu.VMEM((2, room, WIDTH), F32),
                pltpu.SMEM((8,), I32),
                pltpu.SemaphoreType.DMA((1 + 2 * pieces,)),
            ],
        ),
        out_shape=[strip] * 3 + piece_shapes * 2
        + [jax.ShapeDtypeStruct((count * 6,), I32), jax.ShapeDtypeStruct((PHASES, 5, 2, 8, WIDTH), F32)],
        compiler_params=pltpu.CompilerParams(vmem_limit_bytes=VMEM_BYTES),
        name="smooth_part",
    )(meta, velocity, colop, rowop)
    return out[:3], out[3:3 + pieces], out[3 + pieces:3 + 2 * pieces], out[-2], out[-1]


def finish_kernel(level, parts, meta, *refs):
    count = len(parts)
    pos_refs, refs = refs[:count], refs[count:]
    y_refs, refs = refs[:count], refs[count:]
    piece_refs = []
    for _, _, cuts in parts:
        piece_refs.append((refs[:len(cuts)], refs[len(cuts):2 * len(cuts)]))
        refs = refs[2 * len(cuts):]
    mine, theirs, refs = refs[0], refs[1], refs[2:]
    acc, refs = refs[0], refs[1:]
    y_bufs, refs = refs[:count], refs[count:]
    buffers, refs = [refs[2 * k:2 * k + 2] for k in range(count)], refs[2 * count:]
    sem = refs[0]
    loads = []
    for k, (_, _, cuts) in enumerate(parts):
        loads.append(pltpu.make_async_copy(y_refs[k], y_bufs[k], sem.at[len(loads)]))
        low = 0
        for piece, high in enumerate(cuts):
            for side in range(2):
                loads.append(pltpu.make_async_copy(
                    piece_refs[k][side][piece], buffers[k][side].at[:, low:high], sem.at[len(loads)]))
            low = high
    for copy in loads:
        copy.start()
    acc[...] = jnp.zeros_like(acc)
    for copy in loads:
        copy.wait()
    row = lax.broadcasted_iota(I32, (8, WIDTH), 0)
    for k, (first, size, _) in enumerate(parts):
        def one(local, k=k, first=first):
            n = first + local
            phase = meta[2 * SNAPS + n]
            for place in range(2):
                side = 1 - place
                have = level_rows(needs(meta[n])[side], level)
                pos = pos_refs[k][6 * local + 3 * side + level]
                skew = lax.rem(pos, 8)
                base = pl.multiple_of(pos - skew, 8)
                fields = []
                for comp in range(2):
                    window = buffers[k][side][comp, pl.ds(base, 16)]
                    if place == 0:
                        tile = pltpu.roll(window, lax.rem(16 - skew, 16), 0)[0:8]
                        keep = row < have
                    else:
                        tile = pltpu.roll(window, lax.rem(24 - skew - have, 16), 0)[0:8]
                        keep = row >= 8 - have
                    fields.append(y_bufs[k][local, place, comp] + jnp.where(keep, tile, 0.0))
                u, v = fields
                for at_field, field in enumerate((u, v, u * u, v * v, u * v)):
                    acc[phase, at_field, place] += field

        def several(i, carry, one=one):
            for b in range(4):
                one(4 * i + b)
            return carry

        lax.fori_loop(0, size // 4, several, 0)
    stores = [pltpu.make_async_copy(acc.at[HALF:PHASES], theirs, sem.at[0]),
              pltpu.make_async_copy(acc.at[0:HALF], mine, sem.at[1])]
    for copy in stores:
        copy.start()
    for copy in stores:
        copy.wait()


def finish_level(level, meta, parts):
    any_space = pl.BlockSpec(memory_space=pl.ANY)
    smem = pl.BlockSpec(memory_space=pltpu.SMEM)
    shape = jax.ShapeDtypeStruct((HALF, 5, 2, 8, WIDTH), F32)
    plan = [(first, count, level_cuts(cuts, level)) for first, count, cuts, *_ in parts]
    positions = [part[3] for part in parts]
    strips = [part[4][level] for part in parts]
    packs = [piece for part in parts for side in part[5:7] for piece in side[:len(level_cuts(part[2], level))]]
    scratch = [pltpu.VMEM((PHASES, 5, 2, 8, WIDTH), F32)]
    scratch += [pltpu.VMEM((count, 2, 2, 8, WIDTH), F32) for _, count, _ in plan]
    for _, _, cuts in plan:
        scratch += [pltpu.VMEM((2, cuts[-1] + GAP, WIDTH), F32)] * 2
    scratch.append(pltpu.SemaphoreType.DMA((len(strips) + len(packs) + 2,)))
    return pl.pallas_call(
        functools.partial(finish_kernel, level, plan),
        in_specs=[smem] * (1 + len(positions)) + [any_space] * (len(strips) + len(packs)),
        out_specs=[any_space] * 2,
        out_shape=[shape] * 2,
        scratch_shapes=scratch,
        compiler_params=pltpu.CompilerParams(vmem_limit_bytes=VMEM_BYTES),
        name="finish_level",
    )(meta, *positions, *strips, *packs)


def scale_kernel(block, scale, mine, other, *refs):
    mean, moment = refs[-2:]
    start = pl.program_id(0) * block

    def one(p, carry):
        factor = scale[start + p]
        total = (mine[p, :, 0] + other[p, :, 0]) * factor
        mean[p] = total[0:2]
        moment[p] = total[2:5]
        return carry

    lax.fori_loop(0, block, one, 0)


def scale_level(level, scale, mine, other, before):
    block = 18
    any_space = pl.BlockSpec(memory_space=pl.ANY)
    total = pl.BlockSpec((block, 5, 1, 8, WIDTH), lambda i, side, s: (i, 0, side, 0, 0))

    def place(i, side, s):
        return (i, 0, level + side * (7 - 2 * level), 0)

    return pl.pallas_call(
        functools.partial(scale_kernel, block),
        grid_spec=pltpu.PrefetchScalarGridSpec(
            num_scalar_prefetch=1,
            grid=(HALF // block, 2),
            in_specs=[total, total] + [any_space] * len(before),
            out_specs=[pl.BlockSpec((block, 2, 8, WIDTH), place), pl.BlockSpec((block, 3, 8, WIDTH), place)],
        ),
        out_shape=[jax.ShapeDtypeStruct((HALF, 2, ROWS, WIDTH), F32), jax.ShapeDtypeStruct((HALF, 3, ROWS, WIDTH), F32)],
        input_output_aliases={3: 0, 4: 1} if before else {},
        compiler_params=pltpu.CompilerParams(vmem_limit_bytes=VMEM_BYTES),
        name="scale_level",
    )(scale, mine, other, *before)


def to_partner(value):
    return lax.ppermute(value, "snap", [(0, 1), (1, 0)])


def to_above(value):
    size = lax.axis_size("tile")
    return lax.ppermute(value, "tile", [(i + 1, i) for i in range(size - 1)])


def to_below(value):
    size = lax.axis_size("tile")
    return lax.ppermute(value, "tile", [(i, i + 1) for i in range(size - 1)])


def level_cuts(cuts, level):
    return cuts[:level + 1] if len(cuts) == 3 else cuts


def all_fit(dy, first, cuts, count):
    good = True
    for need in needs(dy[first:first + count]):
        end = I32(0)
        for level in range(3):
            end = next_start(end + jnp.sum(level_rows(need, level)))
            good &= end <= level_cuts(cuts, level)[-1]
    return good


def send(up_pieces, dn_pieces):
    from_below = [to_above(piece) for piece in up_pieces]
    from_above = [to_below(piece) for piece in dn_pieces]
    return from_below, from_above


def per_device(velocity, offsets, phase):
    snap = lax.axis_index("snap")
    tile = lax.axis_index("tile")
    dy, dx = offsets[:, 0].astype(I32), offsets[:, 1].astype(I32)
    turned = lax.rem(phase.astype(I32) + PHASES - HALF * snap, PHASES)
    kind = jnp.where(tile == 0, 0, jnp.where(tile == lax.axis_size("tile") - 1, 2, 1)).astype(I32)
    meta = jnp.concatenate([dy, dx, turned, kind[None]])
    colop = jnp.asarray(column_constant())
    rowop = jnp.asarray(row_constant())
    smooth = functools.partial(smooth_part, meta, velocity, colop, rowop, 3 * SNAPS)

    onehot = (turned[:, None] == jnp.arange(PHASES, dtype=I32)[None, :]).astype(I32)
    own = jnp.sum(onehot, axis=0)
    fits = all_fit(dy, 0, FIRST_CUTS, FIRST) & all_fit(dy, FIRST, REST_CUTS, SNAPS - FIRST)
    message = jnp.concatenate([own[HALF:], fits.astype(I32)[None]])
    reply = to_partner(message)
    scale = 1.0 / jnp.maximum((own[:HALF] + reply[:HALF]).astype(F32), 1.0)
    fits = fits & (reply[HALF] > 0)

    strips_a, up_a, dn_a, pos_a, middle_a = smooth(0, FIRST, FIRST_CUTS)
    below_a, above_a = send(up_a, dn_a)
    strips_b, up_b, dn_b, pos_b, middle_b = smooth(FIRST, SNAPS - FIRST, REST_CUTS)

    def tail(parts, middles, scale):
        mine = sum(middle[:HALF] for middle in middles)
        theirs = sum(middle[HALF:] for middle in middles)
        before = scale_level(3, scale, mine, to_partner(theirs), ())
        for level in range(3):
            mine, theirs = finish_level(level, meta, parts)
            before = scale_level(level, scale, mine, to_partner(theirs), before)
        return tuple(before)

    def fast(scale, middle_a, middle_b, strips_a, pos_a, below_a, above_a, strips_b, pos_b, up_b, dn_b):
        below_b, above_b = send(up_b, dn_b)
        parts = [(0, FIRST, FIRST_CUTS, pos_a, strips_a, below_a, above_a),
                 (FIRST, SNAPS - FIRST, REST_CUTS, pos_b, strips_b, below_b, above_b)]
        return tail(parts, [middle_a, middle_b], scale)

    def full(scale, *_):
        cuts = (HALO * SNAPS + 4 * GAP,)
        strips, up, dn, pos, middle = smooth(0, SNAPS, cuts)
        below, above = send(up, dn)
        return tail([(0, SNAPS, cuts, pos, strips, below, above)], [middle], scale)

    return lax.cond(fits, fast, full, scale, middle_a, middle_b, strips_a, pos_a, below_a, above_a, strips_b, pos_b, up_b, dn_b)


def solution(mesh):
    in_specs = (P("snap", None, "tile", None), P("snap", None), P("snap"))
    out_specs = (P("snap", None, "tile", None), P("snap", None, "tile", None))
    return jax.shard_map(
        per_device, mesh=mesh, in_specs=in_specs, out_specs=out_specs, check_vma=False
    )
```

time: 405 us -> 184 us (0.45)
  waiting for transfers between devices: 168 us -> 11.9 us
  matrix products: 122 us -> 0 us
  Pallas kernels: 0 us -> 94 us
  other arithmetic: 51.6 us -> 10.9 us
  starting transfers between devices: 9.53 us -> 42.7 us
  local copies, waits for them, and re-layouts: 34 us -> 6.39 us
    dot_general x3 -> x0, matrix products: 122 us -> none  [the longest x1 50.5 us: per_device(): jnp.einsum('sp,scrw->pcrw', onehot, fields, precision=lax.Precision.HIGHEST)]
    ppermute x2 -> x13, waiting for transfers between devices: 133 us -> 11.9 us  [the longest x4 8.05 us: to_above(): return lax.ppermute(value, 'tile', [(i + 1, i) for i in range(size - 1)])]
    pallas_call x0 -> x9, Pallas kernels: none -> 94 us  [the longest x2 43.1 us: smooth_part(): pl.pallas_call(functools.partial(smooth_kernel, first, count, cuts, STEP)...]
    reduce_scatter x1 -> x0, waiting for transfers between devices: 34.4 us -> none  [per_device(): lax.psum_scatter(partial_sums, 'snap', scatter_dimension=0, tiled=True)]
    ppermute x2 -> x13, starting transfers between devices: 9.49 us -> 42.7 us  [the longest x4 29.7 us: to_above(): return lax.ppermute(value, 'tile', [(i + 1, i) for i in range(size - 1)])]
    concatenate x1 -> x2, other arithmetic: 26.8 us -> 0.09 us  [the longest x1 0.08 us: per_device(): message = jnp.concatenate([own[HALF:], fits.astype(I32)[None]])]
    mul x3 -> x0, other arithmetic: 23.7 us -> none  [the longest x1 11.1 us: per_device(): smooth[:, 0:1] * smooth[:, 0:1]]
    dot_general x1 -> x0, local copies, waits for them, and re-layouts: 22 us -> none  [per_device(): jnp.einsum('sp,scrw->pcrw', onehot, fields, precision=lax.Precision.HIGHEST)]
  transfers between devices with their start and end apart: 3 -> 13, of which waited for: 3 -> 2; matrix products, arithmetic and copies ran while one was open for 0% -> 6% of each run, Pallas kernels for 0% -> 41%
where the time goes in v1:
time: 184 us; the launch traced here: 183 us
  Pallas kernels  94 us (51%)
  starting transfers between devices  42.7 us (23%)
  between operations  16.6 us (9%)
  waiting for transfers between devices  11.9 us (6%)
  other arithmetic  10.9 us (6%)
  local copies, waits for them, and re-layouts  6.39 us (3%)
    pallas_call x2, Pallas kernels, smooth_part(): pl.pallas_call(functools.partial(smooth_kernel, first, count, cuts, STEP)...  43.1 us
    ppermute x4, starting transfers between devices, to_above(): return lax.ppermute(value, 'tile', [(i + 1, i) for i in range(size - 1)])  29.7 us
    pallas_call x3, Pallas kernels, finish_level(): pl.pallas_call(functools.partial(finish_kernel, level, plan), in_specs=[s...  29.1 us
    pallas_call x4, Pallas kernels, scale_level(): pl.pallas_call(functools.partial(scale_kernel, block), grid_spec=pltpu.Pr...  21.8 us
    add x1, other arithmetic, tail(): theirs = sum((middle[HALF:] for middle in middles))  8.45 us
    ppermute x4, waiting for transfers between devices, to_above(): return lax.ppermute(value, 'tile', [(i + 1, i) for i in range(size - 1)])  8.05 us
    ppermute x4, starting transfers between devices, to_below(): return lax.ppermute(value, 'tile', [(i, i + 1) for i in range(size - 1)])  7.67 us
    ppermute x5, starting transfers between devices, to_partner(): return lax.ppermute(value, 'snap', [(0, 1), (1, 0)])  5.35 us
  transfers between devices with their start and end apart: 13, of which 2 were waited for; matrix products, arithmetic and copies ran while one was open for 6% of the time, Pallas kernels for 41%

profile of v1, /device:TPU:97, one launch (start us, length us, event | category | flops | bytes accessed | tf_op | source)
XLA Modules:
  0.0 182.6 jit_solution(5242431038262601846)
XLA Ops:
  0.6 0.8 slice_bitcast_fusion.1
  1.4 0.7 subtract_remainder_fusion
  2.1 0.0 copy-start.9
  2.1 13.7 %smooth_part.5 = (f32[32,2,2,8,256]{4,3,2,1,0:T(8,128)}, f32[32,2,2,8,256]{4,3,2,1,0:T(8,128)}, f32[32,2,2,8,256]{4,3,2,1,0:T(8,128)}, f32[2,480,256]{2,1,0:T(8,...) custom-call(s32[385]{0:T(512)S(1)} %pad_add_fusion.meta, f32[128,2,64,256]{3,2,1,0:T(8,128)} %vel.3, ...), custom_call_target="tpu_custom_call" | custom-call | tf_op jit(solution)/shard_map/smooth_part/pallas_call | solution.py:198
  15.8 6.7 %collective-permute-start.17 = (f32[2,480,256]{2,1,0:T(8,128)}, f32[2,480,256]{2,1,0:T(8,128)S(1)}, u32[]{:S(2)}, u32[]{:S(2)}) collective-permute-start(f32[2,480,256]{2,1,0:T(8,128)} %get-tuple-element.136), channel_id=1, source_target_pairs={{1,0},{2,1},{3,2},{4,3},{5,4},{6,5},{7,6},{8,7},{9,8},{10,9},{11,1... | collective-permute-start | bytes 2949128 | tf_op jit(solution)/shard_map/ppermute | solution.py:364
  22.4 1.9 %collective-permute-start.18 = (f32[2,480,256]{2,1,0:T(8,128)}, f32[2,480,256]{2,1,0:T(8,128)S(1)}, u32[]{:S(2)}, u32[]{:S(2)}) collective-permute-start(f32[2,480,256]{2,1,0:T(8,128)} %get-tuple-element.137), channel_id=1, source_target_pairs={{0,1},{1,2},{2,3},{3,4},{4,5},{5,6},{6,7},{7,8},{8,9},{9,10},{10,1... | collective-permute-start | bytes 2949128 | tf_op jit(solution)/shard_map/ppermute | solution.py:369
  24.4 0.8 clamp_reduce_fusion.4
  32.7 0.8 clamp_reduce_fusion
  41.3 0.1 convert_reduce_fusion
  41.4 0.1 slice.48
  41.4 0.1 pad_add_fusion.1
  41.5 1.0 collective-permute-start.16
  42.5 29.4 %smooth_part.4 = (f32[96,2,2,8,256]{4,3,2,1,0:T(8,128)}, f32[96,2,2,8,256]{4,3,2,1,0:T(8,128)}, f32[96,2,2,8,256]{4,3,2,1,0:T(8,128)}, f32[2,608,256]{2,1,0:T(8,...) custom-call(s32[385]{0:T(512)S(1)} %pad_add_fusion.meta, ...), custom_call_target="tpu_custom_call" | custom-call | tf_op jit(solution)/shard_map/smooth_part/pallas_call | solution.py:198
  71.9 0.6 slice.49
  73.1 0.0 collective-permute-done.17
  73.1 0.0 collective-permute-done.18
  73.1 109.6 %conditional.1 = ((f32[36,2,64,256]{3,2,1,0:T(8,128)}, f32[36,3,64,256]{3,2,1,0:T(8,128)})) conditional(s32[]{:T(128)} %convert_element_type.11, (s32[385]{0:T(512)S(1)}, f32[128,2,64,256]{3,2,1,0:T(8,128)}, bf16[2,256,256]{2,1,0:T(8,128)(2,1)S(1)}, bf16[3,33,112,192]{3,2,1,0:T(8,128)(2,1)}, f32[36]{0:T(128)S(1)}) %tuple.36, ...), branch_computations={%region_13.14_spmd, %region_14.15_spmd} | conditional | flops 1474560 | bytes 159646016 | solution.py:436
  73.1 7.9 %collective-permute-start = (f32[2,608,256]{2,1,0:T(8,128)}, f32[2,608,256]{2,1,0:T(8,128)S(1)}, u32[]{:S(2)}, u32[]{:S(2)}) collective-permute-start(f32[2,608,256]{2,1,0:T(8,128)} %get-tuple-element.82), channel_id=1, source_target_pairs={{1,0},{2,1},{3,2},{4,3},{5,4},{6,5},{7,6},{8,7},{9,8},{10,9},{11,1... | collective-permute-start | bytes 3735560 | tf_op jit(solution)/shard_map/cond/branch_1_fun/ppermute | solution.py:364
  81.0 1.9 %collective-permute-start.3 = (f32[2,608,256]{2,1,0:T(8,128)}, f32[2,608,256]{2,1,0:T(8,128)S(1)}, u32[]{:S(2)}, u32[]{:S(2)}) collective-permute-start(f32[2,608,256]{2,1,0:T(8,128)} %get-tuple-element.85), channel_id=1, source_target_pairs={{0,1},{1,2},{2,3},{3,4},{4,5},{5,6},{6,7},{7,8},{8,9},{9,10},{10,1... | collective-permute-start | bytes 3735560 | tf_op jit(solution)/shard_map/cond/branch_1_fun/ppermute | solution.py:369
  82.9 7.6 %collective-permute-start.1 = (f32[2,408,256]{2,1,0:T(8,128)}, f32[2,408,256]{2,1,0:T(8,128)S(1)}, u32[]{:S(2)}, u32[]{:S(2)}) collective-permute-start(f32[2,408,256]{2,1,0:T(8,128)} %get-tuple-element.83), channel_id=1, source_target_pairs={{1,0},{2,1},{3,2},{4,3},{5,4},{6,5},{7,6},{8,7},{9,8},{10,9},{11,1... | collective-permute-start | bytes 2506760 | tf_op jit(solution)/shard_map/cond/branch_1_fun/ppermute | solution.py:364
  90.5 1.9 %collective-permute-start.4 = (f32[2,408,256]{2,1,0:T(8,128)}, f32[2,408,256]{2,1,0:T(8,128)S(1)}, u32[]{:S(2)}, u32[]{:S(2)}) collective-permute-start(f32[2,408,256]{2,1,0:T(8,128)} %get-tuple-element.86), channel_id=1, source_target_pairs={{0,1},{1,2},{2,3},{3,4},{4,5},{5,6},{6,7},{7,8},{8,9},{9,10},{10,1... | collective-permute-start | bytes 2506760 | tf_op jit(solution)/shard_map/cond/branch_1_fun/ppermute | solution.py:369
  92.4 7.6 %collective-permute-start.2 = (f32[2,168,256]{2,1,0:T(8,128)S(1)}, f32[2,168,256]{2,1,0:T(8,128)S(1)}, u32[]{:S(2)}, u32[]{:S(2)}) collective-permute-start(f32[2,168,256]{2,1,0:T(8,128)S(1)} %get-tuple-element.84), channel_id=1, source_target_pairs={{1,0},{2,1},{3,2},{4,3},{5,4},{6,5},{7,6},{8,7},{9,8},{10,9},{11,1... | collective-permute-start | bytes 1032200 | tf_op jit(solution)/shard_map/cond/branch_1_fun/ppermute | solution.py:364
  100.0 8.0 %collective-permute-done.refs_6_ = f32[2,608,256]{2,1,0:T(8,128)S(1)} collective-permute-done((f32[2,608,256]{2,1,0:T(8,128)}, f32[2,608,256]{2,1,0:T(8,128)S(1)}, u32[]{:S(2)}, u32[]{:S(2)}) %collective-permute-start) | collective-permute-done | bytes 1245216 | tf_op jit(solution)/shard_map/cond/branch_1_fun/ppermute | solution.py:364
  108.0 1.9 %collective-permute-start.5 = (f32[2,168,256]{2,1,0:T(8,128)}, f32[2,168,256]{2,1,0:T(8,128)S(1)}, u32[]{:S(2)}, u32[]{:S(2)}) collective-permute-start(f32[2,168,256]{2,1,0:T(8,128)} %get-tuple-element.87), channel_id=1, source_target_pairs={{0,1},{1,2},{2,3},{3,4},{4,5},{5,6},{6,7},{7,8},{8,9},{9,10},{10,1... | collective-permute-start | bytes 1032200 | tf_op jit(solution)/shard_map/cond/branch_1_fun/ppermute | solution.py:369
  110.0 8.5 %slice_add_fusion = (f32[36,5,2,8,256]{4,3,2,1,0:T(8,128)}, f32[36,5,2,8,256]{4,3,2,1,0:T(8,128)}) fusion(f32[72,5,2,8,256]{4,3,2,1,0:T(8,128)} %get-tuple-element.99, f32[72,5,2,8,256]{4,3,2,1,0:T(8,128)} %get-tuple-element.98), kind=kLoop, calls=%fused_computation | loop fusion | flops 1474560 | bytes 17694720 | tf_op jit(solution)/shard_map/cond/branch_1_fun/add | solution.py:417
  118.4 1.5 collective-permute-start.9
  119.9 9.2 %finish_level.11 = (f32[36,5,2,8,256]{4,3,2,1,0:T(8,128)}, f32[36,5,2,8,256]{4,3,2,1,0:T(8,128)}) custom-call(s32[385]{0:T(512)S(1)} %get-tuple-element.75.meta, s32[192]{0:T(256)S(1)} %get-tuple-element.76.refs_0_, s32[576]{0:T(1024)S(1)} %get-tuple-element.77.refs_1_, f32[32,2,2,8,256]{4,3,2,1,0:T(8,128)} %get-tuple-element.94.refs_2_, ...), custom_call_target="tpu_custom_call" | custom-call | tf_op jit(solution)/shard_map/cond/branch_1_fun/finish_level/pallas_call | solution.py:310
  129.1 0.0 collective-permute-done.1.refs_7_
  129.1 0.9 collective-permute-start.8
  130.1 3.8 %collective-permute-done.4.refs_10_.refs_9_ = f32[2,408,256]{2,1,0:T(8,128)S(1)} collective-permute-done((f32[2,408,256]{2,1,0:T(8,128)}, f32[2,408,256]{2,1,0:T(8,128)S(1)}, u32[]{:S(2)}, u32[]{:S(2)}) %collective-permute-start.4) | collective-permute-done | bytes 835616 | tf_op jit(solution)/shard_map/cond/branch_1_fun/ppermute | solution.py:369
  133.9 0.9 copy-done.4
  134.8 9.9 %finish_level.10 = (f32[36,5,2,8,256]{4,3,2,1,0:T(8,128)}, f32[36,5,2,8,256]{4,3,2,1,0:T(8,128)}) custom-call(s32[385]{0:T(512)S(1)} %get-tuple-element.75.meta, s32[192]{0:T(256)S(1)} %get-tuple-element.76.refs_0_, s32[576]{0:T(1024)S(1)} %get-tuple-element.77.refs_1_, f32[32,2,2,8,256]{4,3,2,1,0:T(8,128)S(1)} %copy-done.10, ...), custom_call_target="tpu_custom_call" | custom-call | tf_op jit(solution)/shard_map/cond/branch_1_fun/finish_level/pallas_call | solution.py:310
  144.7 1.9 %collective-permute-start.7 = (f32[36,5,2,8,256]{4,3,2,1,0:T(8,128)}, f32[36,5,2,8,256]{4,3,2,1,0:T(8,128)S(1)}, u32[]{:S(2)}, u32[]{:S(2)}) collective-permute-start(f32[36,5,2,8,256]{4,3,2,1,0:T(8,128)} %get-tuple-element.93), channel_id=1, source_target_pairs={{0,64},{64,0},{1,65},{65,1},{2,66},{66,2},{3,67},{67,3},{4,68},{68... | collective-permute-start | bytes 8847368 | tf_op jit(solution)/shard_map/cond/branch_1_fun/ppermute | solution.py:359
  146.6 0.0 collective-permute-done.2.refs_8_
  146.6 0.0 collective-permute-done.5.refs_11_
  146.6 0.7 copy-done.11
  147.3 0.1 copy-done.12
  147.4 10.0 %finish_level.9 = (f32[36,5,2,8,256]{4,3,2,1,0:T(8,128)}, f32[36,5,2,8,256]{4,3,2,1,0:T(8,128)}) custom-call(s32[385]{0:T(512)S(1)} %get-tuple-element.75.meta, s32[192]{0:T(256)S(1)} %get-tuple-element.76.refs_0_, s32[576]{0:T(1024)S(1)} %get-tuple-element.77.refs_1_, f32[32,2,2,8,256]{4,3,2,1,0:T(8,128)} %get-tuple-element.78.refs_2_, ...), custom_call_target="tpu_custom_call" | custom-call | tf_op jit(solution)/shard_map/cond/branch_1_fun/finish_level/pallas_call | solution.py:310
  157.4 0.1 collective-permute-start.6
  157.5 0.0 collective-permute-done.9.other
  157.5 5.5 %scale_level.12 = (f32[36,2,64,256]{3,2,1,0:T(8,128)}, f32[36,3,64,256]{3,2,1,0:T(8,128)}) custom-call(f32[36]{0:T(128)S(1)} %get-tuple-element.74.scale, f32[36,5,2,8,256]{4,3,2,1,0:T(8,128)} %get-tuple-element.165.mine, f32[36,5,2,8,256]{4,3,2,1,0:T(8,128)} %collective-permute-done.9.other), custom_call_target="tpu_custom_call" | custom-call | tf_op jit(solution)/shard_map/cond/branch_1_fun/scale_level/pallas_call | solution.py:343
  163.0 0.0 collective-permute-done.8.other
  163.0 5.5 %scale_level.13 = (f32[36,2,64,256]{3,2,1,0:T(8,128)}, f32[36,3,64,256]{3,2,1,0:T(8,128)}) custom-call(f32[36]{0:T(128)S(1)} %get-tuple-element.74.scale, f32[36,5,2,8,256]{4,3,2,1,0:T(8,128)} %get-tuple-element.96.mine, f32[36,5,2,8,256]{4,3,2,1,0:T(8,128)} %collective-permute-done.8.other, ...), custom_call_target="tpu_custom_call", output_to_operand_aliasing={{0}: (3, {}), {1}: (4, {})} | custom-call | tf_op jit(solution)/shard_map/cond/branch_1_fun/scale_level/pallas_call | solution.py:343
  168.4 0.0 collective-permute-done.7.other
  168.5 1.5 copy-done.5
  170.0 5.5 %scale_level.14 = (f32[36,2,64,256]{3,2,1,0:T(8,128)}, f32[36,3,64,256]{3,2,1,0:T(8,128)}) custom-call(f32[36]{0:T(128)S(1)} %get-tuple-element.74.scale, f32[36,5,2,8,256]{4,3,2,1,0:T(8,128)} %get-tuple-element.92.mine, f32[36,5,2,8,256]{4,3,2,1,0:T(8,128)} %copy-done.5, ...), custom_call_target="tpu_custom_call", output_to_operand_aliasing={{0}: (3, {}), {1}: (4, {})} | custom-call | tf_op jit(solution)/shard_map/cond/branch_1_fun/scale_level/pallas_call | solution.py:343
  175.5 1.7 copy-done.7
  177.2 5.5 %scale_level.15 = (f32[36,2,64,256]{3,2,1,0:T(8,128)}, f32[36,3,64,256]{3,2,1,0:T(8,128)}) custom-call(f32[36]{0:T(128)S(1)} %get-tuple-element.74.scale, f32[36,5,2,8,256]{4,3,2,1,0:T(8,128)} %get-tuple-element.88.mine, f32[36,5,2,8,256]{4,3,2,1,0:T(8,128)} %copy-done.7, ...), custom_call_target="tpu_custom_call", output_to_operand_aliasing={{0}: (3, {}), {1}: (4, {})} | custom-call | tf_op jit(solution)/shard_map/cond/branch_1_fun/scale_level/pallas_call | solution.py:343
  (21 shorter events, 0.1 us)
Async XLA Ops:
  2.1 22.3 %copy-start.13 = (s32[128,2]{0,1:T(2,128)S(1)}, s32[128,2]{0,1:T(2,128)}, u32[]{:S(2)}) copy-start(s32[128,2]{0,1:T(2,128)} %param.8) | copy-start | bytes 3076
  2.1 40.4 %copy-start.9 = (bf16[2,256,256]{2,1,0:T(8,128)(2,1)S(1)}, bf16[2,256,256]{2,1,0:T(8,128)(2,1)}, u32[]{:S(2)}) copy-start(bf16[2,256,256]{2,1,0:T(8,128)(2,1)} %constant.147.clone.colop) | copy-start | bytes 786436
  15.8 57.3 %collective-permute-start.17 = (f32[2,480,256]{2,1,0:T(8,128)}, f32[2,480,256]{2,1,0:T(8,128)S(1)}, u32[]{:S(2)}, u32[]{:S(2)}) collective-permute-start(f32[2,480,256]{2,1,0:T(8,128)} %get-tuple-element.136), channel_id=1, source_target_pairs={{1,0},{2,1},{3,2},{4,3},{5,4},{6,5},{7,6},{8,7},{9,8},{10,9},{11,1... | collective-permute-start | bytes 2949128 | tf_op jit(solution)/shard_map/ppermute | solution.py:364
  22.4 50.6 %collective-permute-start.18 = (f32[2,480,256]{2,1,0:T(8,128)}, f32[2,480,256]{2,1,0:T(8,128)S(1)}, u32[]{:S(2)}, u32[]{:S(2)}) collective-permute-start(f32[2,480,256]{2,1,0:T(8,128)} %get-tuple-element.137), channel_id=1, source_target_pairs={{0,1},{1,2},{2,3},{3,4},{4,5},{5,6},{6,7},{7,8},{8,9},{9,10},{10,1... | collective-permute-start | bytes 2949128 | tf_op jit(solution)/shard_map/ppermute | solution.py:369
  41.5 30.4 %collective-permute-start.16 = (s32[37]{0:T(128)S(1)}, s32[37]{0:T(128)S(1)}, u32[]{:S(2)}, u32[]{:S(2)}) collective-permute-start(s32[37]{0:T(128)S(1)} %pad_add_fusion.1), channel_id=1, source_target_pairs={{0,64},{64,0},{1,65},{65,1},{2,66},{66,2},{3,67},{67,3},{4,68},{68... | collective-permute-start | bytes 452 | tf_op jit(solution)/shard_map/ppermute | solution.py:359
  73.1 34.9 %collective-permute-start = (f32[2,608,256]{2,1,0:T(8,128)}, f32[2,608,256]{2,1,0:T(8,128)S(1)}, u32[]{:S(2)}, u32[]{:S(2)}) collective-permute-start(f32[2,608,256]{2,1,0:T(8,128)} %get-tuple-element.82), channel_id=1, source_target_pairs={{1,0},{2,1},{3,2},{4,3},{5,4},{6,5},{7,6},{8,7},{9,8},{10,9},{11,1... | collective-permute-start | bytes 3735560 | tf_op jit(solution)/shard_map/cond/branch_1_fun/ppermute | solution.py:364
  81.0 37.5 %collective-permute-start.3 = (f32[2,608,256]{2,1,0:T(8,128)}, f32[2,608,256]{2,1,0:T(8,128)S(1)}, u32[]{:S(2)}, u32[]{:S(2)}) collective-permute-start(f32[2,608,256]{2,1,0:T(8,128)} %get-tuple-element.85), channel_id=1, source_target_pairs={{0,1},{1,2},{2,3},{3,4},{4,5},{5,6},{6,7},{7,8},{8,9},{9,10},{10,1... | collective-permute-start | bytes 3735560 | tf_op jit(solution)/shard_map/cond/branch_1_fun/ppermute | solution.py:369
  82.9 46.2 %collective-permute-start.1 = (f32[2,408,256]{2,1,0:T(8,128)}, f32[2,408,256]{2,1,0:T(8,128)S(1)}, u32[]{:S(2)}, u32[]{:S(2)}) collective-permute-start(f32[2,408,256]{2,1,0:T(8,128)} %get-tuple-element.83), channel_id=1, source_target_pairs={{1,0},{2,1},{3,2},{4,3},{5,4},{6,5},{7,6},{8,7},{9,8},{10,9},{11,1... | collective-permute-start | bytes 2506760 | tf_op jit(solution)/shard_map/cond/branch_1_fun/ppermute | solution.py:364
  90.5 43.4 %collective-permute-start.4 = (f32[2,408,256]{2,1,0:T(8,128)}, f32[2,408,256]{2,1,0:T(8,128)S(1)}, u32[]{:S(2)}, u32[]{:S(2)}) collective-permute-start(f32[2,408,256]{2,1,0:T(8,128)} %get-tuple-element.86), channel_id=1, source_target_pairs={{0,1},{1,2},{2,3},{3,4},{4,5},{5,6},{6,7},{7,8},{8,9},{9,10},{10,1... | collective-permute-start | bytes 2506760 | tf_op jit(solution)/shard_map/cond/branch_1_fun/ppermute | solution.py:369
  92.4 54.2 %collective-permute-start.2 = (f32[2,168,256]{2,1,0:T(8,128)S(1)}, f32[2,168,256]{2,1,0:T(8,128)S(1)}, u32[]{:S(2)}, u32[]{:S(2)}) collective-permute-start(f32[2,168,256]{2,1,0:T(8,128)S(1)} %get-tuple-element.84), channel_id=1, source_target_pairs={{1,0},{2,1},{3,2},{4,3},{5,4},{6,5},{7,6},{8,7},{9,8},{10,9},{11,1... | collective-permute-start | bytes 1032200 | tf_op jit(solution)/shard_map/cond/branch_1_fun/ppermute | solution.py:364
  108.0 10.4 %copy-start.1 = (f32[2,608,256]{2,1,0:T(8,128)}, f32[2,608,256]{2,1,0:T(8,128)S(1)}, u32[]{:S(2)}) copy-start(f32[2,608,256]{2,1,0:T(8,128)S(1)} %collective-permute-done.refs_6_) | copy-start | bytes 3735556 | tf_op jit(solution)/shard_map/cond
  108.0 38.6 %collective-permute-start.5 = (f32[2,168,256]{2,1,0:T(8,128)}, f32[2,168,256]{2,1,0:T(8,128)S(1)}, u32[]{:S(2)}, u32[]{:S(2)}) collective-permute-start(f32[2,168,256]{2,1,0:T(8,128)} %get-tuple-element.87), channel_id=1, source_target_pairs={{0,1},{1,2},{2,3},{3,4},{4,5},{5,6},{6,7},{7,8},{8,9},{9,10},{10,1... | collective-permute-start | bytes 1032200 | tf_op jit(solution)/shard_map/cond/branch_1_fun/ppermute | solution.py:369
  118.4 1.5 copy-start.2
  118.4 39.1 %collective-permute-start.9 = (f32[36,5,2,8,256]{4,3,2,1,0:T(8,128)}, f32[36,5,2,8,256]{4,3,2,1,0:T(8,128)}, u32[]{:S(2)}, u32[]{:S(2)}) collective-permute-start(f32[36,5,2,8,256]{4,3,2,1,0:T(8,128)} %get-tuple-element.164), channel_id=1, source_target_pairs={{0,64},{64,0},{1,65},{65,1},{2,66},{66,2},{3,67},{67,3},{4,68},{68... | collective-permute-start | bytes 8847368 | tf_op jit(solution)/shard_map/cond/branch_1_fun/ppermute | solution.py:359
  119.9 14.9 %copy-start.10 = (f32[32,2,2,8,256]{4,3,2,1,0:T(8,128)S(1)}, f32[32,2,2,8,256]{4,3,2,1,0:T(8,128)}, u32[]{:S(2)}) copy-start(f32[32,2,2,8,256]{4,3,2,1,0:T(8,128)} %get-tuple-element.90.refs_2_) | copy-start | bytes 3145732 | tf_op jit(solution)/shard_map/cond
  129.1 4.7 %copy-start.3 = (f32[2,408,256]{2,1,0:T(8,128)}, f32[2,408,256]{2,1,0:T(8,128)S(1)}, u32[]{:S(2)}) copy-start(f32[2,408,256]{2,1,0:T(8,128)S(1)} %collective-permute-done.1.refs_7_) | copy-start | bytes 2506756 | tf_op jit(solution)/shard_map/cond
  129.1 33.8 %collective-permute-start.8 = (f32[36,5,2,8,256]{4,3,2,1,0:T(8,128)}, f32[36,5,2,8,256]{4,3,2,1,0:T(8,128)}, u32[]{:S(2)}, u32[]{:S(2)}) collective-permute-start(f32[36,5,2,8,256]{4,3,2,1,0:T(8,128)} %get-tuple-element.97), channel_id=1, source_target_pairs={{0,64},{64,0},{1,65},{65,1},{2,66},{66,2},{3,67},{67,3},{4,68},{68... | collective-permute-start | bytes 8847368 | tf_op jit(solution)/shard_map/cond/branch_1_fun/ppermute | solution.py:359
  133.9 0.9 copy-start.4
  144.7 23.8 %collective-permute-start.7 = (f32[36,5,2,8,256]{4,3,2,1,0:T(8,128)}, f32[36,5,2,8,256]{4,3,2,1,0:T(8,128)S(1)}, u32[]{:S(2)}, u32[]{:S(2)}) collective-permute-start(f32[36,5,2,8,256]{4,3,2,1,0:T(8,128)} %get-tuple-element.93), channel_id=1, source_target_pairs={{0,64},{64,0},{1,65},{65,1},{2,66},{66,2},{3,67},{67,3},{4,68},{68... | collective-permute-start | bytes 8847368 | tf_op jit(solution)/shard_map/cond/branch_1_fun/ppermute | solution.py:359
  146.6 0.7 copy-start.11
  146.6 0.8 copy-start.12
  157.4 18.0 %collective-permute-start.6 = (f32[36,5,2,8,256]{4,3,2,1,0:T(8,128)}, f32[36,5,2,8,256]{4,3,2,1,0:T(8,128)S(1)}, u32[]{:S(2)}, u32[]{:S(2)}) collective-permute-start(f32[36,5,2,8,256]{4,3,2,1,0:T(8,128)} %get-tuple-element.89), channel_id=1, source_target_pairs={{0,64},{64,0},{1,65},{65,1},{2,66},{66,2},{3,67},{67,3},{4,68},{68... | collective-permute-start | bytes 8847368 | tf_op jit(solution)/shard_map/cond/branch_1_fun/ppermute | solution.py:359
  168.5 1.5 copy-start.5
  175.5 1.7 copy-start.7

commit v2 on v1

v2 whole, which is shorter than its diff:
```python
import functools

import jax
import jax.numpy as jnp
import numpy as np
from jax import lax
from jax.experimental import pallas as pl
from jax.experimental.pallas import tpu as pltpu
from jax.sharding import PartitionSpec as P

PHASES = 72
HALF = PHASES // 2
RAD = 8
MAXS = 16
HALO = RAD + MAXS
ROWS = 64
WIDTH = 256
SNAPS = 128
EXT = ROWS + 2 * HALO
GROUP = 4
FIRST_STEP = 8
REST_STEP = 16
GAP = 16
VMEM_BYTES = 56 * 1024 * 1024
FIRST = 32
FIRST_CUTS = (480,)
REST_CUTS = (608, 1016, 1184)
F32 = jnp.float32
BF16 = jnp.bfloat16
I32 = jnp.int32


def taps():
    steps = np.arange(2 * RAD + 1, dtype=np.float64) - RAD
    sigma = RAD / 2.0
    values = np.exp(-steps * steps / (2.0 * sigma * sigma))
    return values / values.sum()


def split_const(values):
    high = values.astype(BF16)
    low = (values - high.astype(np.float64)).astype(BF16)
    return high, low


def column_constant():
    weight = taps()
    source = np.arange(WIDTH)[:, None]
    target = np.arange(WIDTH)[None, :]
    distance = source - target
    band = np.where(np.abs(distance) <= RAD, weight[np.clip(distance + RAD, 0, 2 * RAD)], 0.0)
    return np.stack(split_const(band))


def row_constant():
    weight = taps()
    target = np.arange(EXT)[None, :, None] - HALO
    source = np.arange(ROWS)[None, None, :]
    shift = np.arange(-MAXS, MAXS + 1)[:, None, None]
    distance = source - shift - target
    band = np.where(np.abs(distance) <= RAD, weight[np.clip(distance + RAD, 0, 2 * RAD)], 0.0)
    seen = source - shift
    kinds = []
    for kind in range(3):
        keep = np.ones_like(seen, dtype=bool)
        if kind == 0:
            keep = seen >= 0
        if kind == 2:
            keep = seen < ROWS
        high, low = split_const(np.where(keep, band, 0.0))
        kinds.append(np.concatenate([high, low, high], axis=2))
    return np.stack(kinds)


def level_rows(need, level):
    return jnp.clip(need - 8 * level, 0, 8)


def needs(dy):
    return jnp.clip(RAD + dy, 0, HALO), jnp.clip(RAD - dy, 0, HALO)


def next_start(end):
    return end // 8 * 8 + 16


def split(value):
    high = value.astype(BF16)
    return high, (value - high.astype(F32)).astype(BF16)


def smooth_kernel(first, count, cuts, step, earlier, meta, *refs):
    pieces = len(cuts)
    vel, colop, rowop, refs = *refs[:3], refs[3:]
    if earlier is not None:
        early_strip, refs = refs[0], refs[1:]
    strips = 3 if earlier is not None else 4
    y_refs, refs = refs[:strips], refs[strips:]
    out_up, out_dn = refs[:pieces], refs[pieces:2 * pieces]
    pos_ref, refs = refs[2 * pieces], refs[2 * pieces + 1:]
    if earlier is not None:
        mine, theirs, early_buf, acc, refs = *refs[:4], refs[4:]
    xs_hi, xs_lo, stack, ext, up, dn, cursor, sem = refs
    at = pl.program_id(0)
    last = pl.num_programs(0) - 1
    row = lax.broadcasted_iota(I32, (8, WIDTH), 0)
    lane = lax.broadcasted_iota(I32, (1, WIDTH), 1)
    dot = functools.partial(jnp.dot, preferred_element_type=F32)

    def add_fields(phase, place, u, v):
        for at_field, field in enumerate((u, v, u * u, v * v, u * v)):
            acc[phase, at_field, place] += field

    @pl.when(at == 0)
    def _():
        def count_rows(n, sums):
            dy = meta[first + n]
            out = list(sums)
            for side, need in enumerate(needs(dy)):
                for level in range(3):
                    out[3 * side + level] += level_rows(need, level)
            return tuple(out)

        sums = lax.fori_loop(0, count, count_rows, (I32(0),) * 6)
        for side in range(2):
            start = I32(0)
            for level in range(3):
                cursor[3 * side + level] = start
                start = next_start(start + sums[3 * side + level])
        if earlier is not None:
            load = pltpu.make_async_copy(early_strip, early_buf, sem.at[0])
            load.start()
            acc[...] = jnp.zeros_like(acc)
            load.wait()

            def one_early(n, carry):
                phase = meta[2 * SNAPS + earlier + n]
                for place in range(2):
                    add_fields(phase, place, early_buf[n, place, 0], early_buf[n, place, 1])
                return carry

            lax.fori_loop(0, first - earlier, one_early, 0)

    def group(g, carry):
        for b in range(GROUP):
            n = first + at * step + GROUP * g + b
            dx = meta[SNAPS + n]
            rolled = pltpu.roll(vel[GROUP * g + b].reshape(2 * ROWS, WIDTH), lax.rem(WIDTH - dx, WIDTH), 1)
            moved = lane + dx
            high, low = split(jnp.where((moved >= 0) & (moved < WIDTH), rolled, 0.0))
            xs_hi[2 * ROWS * b:2 * ROWS * (b + 1)] = high
            xs_lo[2 * ROWS * b:2 * ROWS * (b + 1)] = low
        horizontal = dot(xs_hi[...], colop[0]) + dot(xs_hi[...], colop[1]) + dot(xs_lo[...], colop[0])
        high, low = split(horizontal)
        for b in range(GROUP):
            for comp in range(2):
                rows = slice(ROWS * (2 * b + comp), ROWS * (2 * b + comp + 1))
                stack[b, comp, 0:ROWS] = high[rows]
                stack[b, comp, ROWS:2 * ROWS] = high[rows]
                stack[b, comp, 2 * ROWS:3 * ROWS] = low[rows]
        for b in range(GROUP):
            n = first + at * step + GROUP * g + b
            oper = rowop[0, meta[n] + MAXS]
            for comp in range(2):
                ext[b, comp] = dot(oper, stack[b, comp])
        for b in range(GROUP):
            inner = GROUP * g + b
            local = at * step + inner
            n = first + local
            for level in range(strips):
                top = HALO + 8 * level
                bottom = HALO + ROWS - 8 - 8 * level
                y_refs[level][inner, 0] = ext[b, :, top:top + 8]
                y_refs[level][inner, 1] = ext[b, :, bottom:bottom + 8]
            if earlier is not None:
                phase = meta[2 * SNAPS + n]
                for place in range(2):
                    rows = slice(2 * HALO + 8 * place, 2 * HALO + 8 * place + 8)
                    add_fields(phase, place, ext[b, 0, rows], ext[b, 1, rows])
            for side, need in enumerate(needs(meta[n])):
                buffer = (up, dn)[side]
                for level in range(3):
                    slot = 3 * side + level
                    have = level_rows(need, level)
                    pos = cursor[slot]
                    cursor[slot] = pos + have
                    pos_ref[6 * local + slot] = pos
                    skew = lax.rem(pos, 8)
                    base = pl.multiple_of(pos - skew, 8)
                    source = 16 - 8 * level if side == 0 else HALO + ROWS + 8 * level
                    turn = lax.rem(skew + have, 8) if side == 0 else skew
                    for comp in range(2):
                        tile = pltpu.roll(ext[b, comp, source:source + 8], turn, 0)
                        old = buffer[comp, pl.ds(base, 8)]
                        buffer[comp, pl.ds(base, 8)] = jnp.where(row < skew, old, tile)
                        buffer[comp, pl.ds(base + 8, 8)] = tile
        return carry

    lax.fori_loop(0, step // GROUP, group, 0)

    @pl.when(at == last)
    def _():
        copies = []
        low = 0
        for piece, high in enumerate(cuts):
            for side in range(2):
                copies.append(pltpu.make_async_copy(
                    (up, dn)[side].at[:, low:high], (out_up, out_dn)[side][piece], sem.at[len(copies)]))
            low = high
        if earlier is not None:
            copies.append(pltpu.make_async_copy(acc.at[0:HALF], mine, sem.at[len(copies)]))
            copies.append(pltpu.make_async_copy(acc.at[HALF:PHASES], theirs, sem.at[len(copies)]))
        for copy in copies:
            copy.start()
        for copy in copies:
            copy.wait()


def smooth_part(meta, velocity, colop, rowop, first, count, cuts, step, earlier, early_strip):
    pieces = len(cuts)
    sizes = [high - low for low, high in zip((0,) + cuts[:-1], cuts)]
    any_space = pl.BlockSpec(memory_space=pl.ANY)
    piece_shapes = [jax.ShapeDtypeStruct((2, size, WIDTH), F32) for size in sizes]
    strip = jax.ShapeDtypeStruct((count, 2, 2, 8, WIDTH), F32)
    total = jax.ShapeDtypeStruct((HALF, 5, 2, 8, WIDTH), F32)
    room = cuts[-1] + GAP
    strips = 3 if earlier is not None else 4
    sums = earlier is not None
    sum_scratch = [pltpu.VMEM((max(first - earlier, 1), 2, 2, 8, WIDTH), F32),
                   pltpu.VMEM((PHASES, 5, 2, 8, WIDTH), F32)] if sums else []
    out = pl.pallas_call(
        functools.partial(smooth_kernel, first, count, cuts, step, earlier),
        grid_spec=pltpu.PrefetchScalarGridSpec(
            num_scalar_prefetch=1,
            grid=(count // step,),
            in_specs=[
                pl.BlockSpec((step, 2, ROWS, WIDTH), lambda i, m: (first // step + i, 0, 0, 0)),
                pl.BlockSpec((2, WIDTH, WIDTH), lambda i, m: (0, 0, 0)),
                pl.BlockSpec((1, 2 * MAXS + 1, EXT, 3 * ROWS), lambda i, m: (m[3 * SNAPS], 0, 0, 0)),
            ] + [any_space] * sums,
            out_specs=[pl.BlockSpec((step, 2, 2, 8, WIDTH), lambda i, m: (i, 0, 0, 0, 0))] * strips
            + [any_space] * (2 * pieces)
            + [pl.BlockSpec(memory_space=pltpu.SMEM)] + [any_space] * (2 * sums),
            scratch_shapes=sum_scratch + [
                pltpu.VMEM((GROUP * 2 * ROWS, WIDTH), BF16),
                pltpu.VMEM((GROUP * 2 * ROWS, WIDTH), BF16),
                pltpu.VMEM((GROUP, 2, 3 * ROWS, WIDTH), BF16),
                pltpu.VMEM((GROUP, 2, EXT, WIDTH), F32),
                pltpu.VMEM((2, room, WIDTH), F32),
                pltpu.VMEM((2, room, WIDTH), F32),
                pltpu.SMEM((8,), I32),
                pltpu.SemaphoreType.DMA((2 + 2 * pieces,)),
            ],
        ),
        out_shape=[strip] * strips + piece_shapes * 2
        + [jax.ShapeDtypeStruct((count * 6,), I32)] + [total] * (2 * sums),
        compiler_params=pltpu.CompilerParams(vmem_limit_bytes=VMEM_BYTES),
        name="smooth_part",
    )(meta, velocity, colop, rowop, *([early_strip] if sums else []))
    up, dn = out[strips:strips + pieces], out[strips + pieces:strips + 2 * pieces]
    return out[:strips], up, dn, out[strips + 2 * pieces], out[strips + 2 * pieces + 1:]


def finish_kernel(level, parts, meta, *refs):
    count = len(parts)
    pos_refs, refs = refs[:count], refs[count:]
    y_refs, refs = refs[:count], refs[count:]
    piece_refs = []
    for _, _, cuts in parts:
        piece_refs.append((refs[:len(cuts)], refs[len(cuts):2 * len(cuts)]))
        refs = refs[2 * len(cuts):]
    mine, theirs, refs = refs[0], refs[1], refs[2:]
    acc, refs = refs[0], refs[1:]
    y_bufs, refs = refs[:count], refs[count:]
    buffers, refs = [refs[2 * k:2 * k + 2] for k in range(count)], refs[2 * count:]
    sem = refs[0]
    chunk = 32
    loads, waits = [], []
    for k, (_, size, cuts) in enumerate(parts):
        here = []
        low = 0
        for piece, high in enumerate(cuts):
            for side in range(2):
                here.append((piece_refs[k][side][piece], buffers[k][side].at[:, low:high]))
            low = high
        for start in range(0, size, chunk):
            here.append((y_refs[k].at[start:start + chunk], y_bufs[k].at[start:start + chunk]))
            group = []
            for source, target in here:
                group.append(pltpu.make_async_copy(source, target, sem.at[len(loads)]))
                loads.append(group[-1])
            waits.append((k, start, group))
            here = []
    for copy in loads:
        copy.start()
    acc[...] = jnp.zeros_like(acc)
    row = lax.broadcasted_iota(I32, (8, WIDTH), 0)
    for k, start, group in waits:
        for copy in group:
            copy.wait()

        def one(local, k=k):
            n = parts[k][0] + local
            phase = meta[2 * SNAPS + n]
            for place in range(2):
                side = 1 - place
                have = level_rows(needs(meta[n])[side], level)
                pos = pos_refs[k][6 * local + 3 * side + level]
                skew = lax.rem(pos, 8)
                base = pl.multiple_of(pos - skew, 8)
                fields = []
                for comp in range(2):
                    window = buffers[k][side][comp, pl.ds(base, 16)]
                    if place == 0:
                        tile = pltpu.roll(window, lax.rem(16 - skew, 16), 0)[0:8]
                        keep = row < have
                    else:
                        tile = pltpu.roll(window, lax.rem(24 - skew - have, 16), 0)[0:8]
                        keep = row >= 8 - have
                    fields.append(y_bufs[k][local, place, comp] + jnp.where(keep, tile, 0.0))
                u, v = fields
                for at_field, field in enumerate((u, v, u * u, v * v, u * v)):
                    acc[phase, at_field, place] += field

        def several(i, carry, one=one, start=start):
            for b in range(4):
                one(start + 4 * i + b)
            return carry

        lax.fori_loop(0, chunk // 4, several, 0)
    stores = [pltpu.make_async_copy(acc.at[HALF:PHASES], theirs, sem.at[0]),
              pltpu.make_async_copy(acc.at[0:HALF], mine, sem.at[1])]
    for copy in stores:
        copy.start()
    for copy in stores:
        copy.wait()


def finish_level(level, meta, parts):
    any_space = pl.BlockSpec(memory_space=pl.ANY)
    smem = pl.BlockSpec(memory_space=pltpu.SMEM)
    shape = jax.ShapeDtypeStruct((HALF, 5, 2, 8, WIDTH), F32)
    plan = [(first, count, level_cuts(cuts, level)) for first, count, cuts, *_ in parts]
    positions = [part[3] for part in parts]
    strips = [part[4][level] for part in parts]
    packs = [piece for part in parts for side in part[5:7] for piece in side[:len(level_cuts(part[2], level))]]
    scratch = [pltpu.VMEM((PHASES, 5, 2, 8, WIDTH), F32)]
    scratch += [pltpu.VMEM((count, 2, 2, 8, WIDTH), F32) for _, count, _ in plan]
    for _, _, cuts in plan:
        scratch += [pltpu.VMEM((2, cuts[-1] + GAP, WIDTH), F32)] * 2
    scratch.append(pltpu.SemaphoreType.DMA((SNAPS // 32 + len(packs) + 2,)))
    return pl.pallas_call(
        functools.partial(finish_kernel, level, plan),
        in_specs=[smem] * (1 + len(positions)) + [any_space] * (len(strips) + len(packs)),
        out_specs=[any_space] * 2,
        out_shape=[shape] * 2,
        scratch_shapes=scratch,
        compiler_params=pltpu.CompilerParams(vmem_limit_bytes=VMEM_BYTES),
        name="finish_level",
    )(meta, *positions, *strips, *packs)


def scale_kernel(block, scale, mine, other, *refs):
    mean, moment = refs[-2:]
    start = pl.program_id(0) * block

    def one(p, carry):
        factor = scale[start + p]
        total = (mine[p, :, 0] + other[p, :, 0]) * factor
        mean[p] = total[0:2]
        moment[p] = total[2:5]
        return carry

    lax.fori_loop(0, block, one, 0)


def scale_level(level, scale, mine, other, before):
    block = 6
    any_space = pl.BlockSpec(memory_space=pl.ANY)
    total = pl.BlockSpec((block, 5, 1, 8, WIDTH), lambda i, side, s: (i, 0, side, 0, 0))

    def place(i, side, s):
        return (i, 0, level + side * (7 - 2 * level), 0)

    return pl.pallas_call(
        functools.partial(scale_kernel, block),
        grid_spec=pltpu.PrefetchScalarGridSpec(
            num_scalar_prefetch=1,
            grid=(HALF // block, 2),
            in_specs=[total, total] + [any_space] * len(before),
            out_specs=[pl.BlockSpec((block, 2, 8, WIDTH), place), pl.BlockSpec((block, 3, 8, WIDTH), place)],
        ),
        out_shape=[jax.ShapeDtypeStruct((HALF, 2, ROWS, WIDTH), F32), jax.ShapeDtypeStruct((HALF, 3, ROWS, WIDTH), F32)],
        input_output_aliases={3: 0, 4: 1} if before else {},
        compiler_params=pltpu.CompilerParams(vmem_limit_bytes=VMEM_BYTES),
        name="scale_level",
    )(scale, mine, other, *before)


def to_partner(value):
    return lax.ppermute(value, "snap", [(0, 1), (1, 0)])


def to_above(value):
    size = lax.axis_size("tile")
    return lax.ppermute(value, "tile", [(i + 1, i) for i in range(size - 1)])


def to_below(value):
    size = lax.axis_size("tile")
    return lax.ppermute(value, "tile", [(i, i + 1) for i in range(size - 1)])


def level_cuts(cuts, level):
    return cuts[:level + 1] if len(cuts) == 3 else cuts


def excess(dy, first, cuts, count):
    need = jnp.stack(needs(dy[first:first + count]))
    over = []
    end = jnp.zeros((2,), I32)
    for level in range(3):
        end = next_start(end + jnp.sum(level_rows(need, level), axis=1))
        over.append(end - level_cuts(cuts, level)[-1])
    return jnp.concatenate(over)


def send(up_pieces, dn_pieces):
    from_below = [to_above(piece) for piece in up_pieces]
    from_above = [to_below(piece) for piece in dn_pieces]
    return from_below, from_above


def per_device(velocity, offsets, phase):
    snap = lax.axis_index("snap")
    tile = lax.axis_index("tile")
    dy, dx = offsets[:, 0].astype(I32), offsets[:, 1].astype(I32)
    turned = lax.rem(phase.astype(I32) + PHASES - HALF * snap, PHASES)
    kind = jnp.where(tile == 0, 0, jnp.where(tile == lax.axis_size("tile") - 1, 2, 1)).astype(I32)
    meta = jnp.concatenate([dy, dx, turned, kind[None]])
    colop = jnp.asarray(column_constant())
    rowop = jnp.asarray(row_constant())
    smooth = functools.partial(smooth_part, meta, velocity, colop, rowop)
    strips_a, up_a, dn_a, pos_a, _ = smooth(0, FIRST, FIRST_CUTS, FIRST_STEP, None, None)
    below_a, above_a = send(up_a, dn_a)

    onehot = (turned[:, None] == jnp.arange(PHASES, dtype=I32)[None, :]).astype(I32)
    own = jnp.sum(onehot, axis=0)
    over = jnp.max(jnp.concatenate([excess(dy, 0, FIRST_CUTS, FIRST), excess(dy, FIRST, REST_CUTS, SNAPS - FIRST)]))
    message = jnp.concatenate([own, jnp.full((8,), over, I32)])
    reply = to_partner(message)
    scale = 1.0 / jnp.maximum((message[:HALF] + reply[HALF:PHASES]).astype(F32), 1.0)
    over = jnp.max(jnp.maximum(message[PHASES:], reply[PHASES:]))

    strips_b, up_b, dn_b, pos_b, sums_b = smooth(FIRST, SNAPS - FIRST, REST_CUTS, REST_STEP, 0, strips_a[3])

    def tail(parts, sums, scale):
        before, waiting = (), [(3, sums[0], to_partner(sums[1]))]
        here = meta
        for level in range(3):
            if level:
                at, mine, other = waiting.pop(0)
                before = scale_level(at, scale, mine, other, before)
                here, before = lax.optimization_barrier((here, before))
            mine, theirs = finish_level(level, here, parts)
            waiting.append((level, mine, to_partner(theirs)))
        for at, mine, other in waiting:
            before = scale_level(at, scale, mine, other, before)
        return tuple(before)

    def fast(scale, sums_b, strips_a, pos_a, below_a, above_a, strips_b, pos_b, up_b, dn_b):
        below_b, above_b = send(up_b, dn_b)
        parts = [(0, FIRST, FIRST_CUTS, pos_a, strips_a, below_a, above_a),
                 (FIRST, SNAPS - FIRST, REST_CUTS, pos_b, strips_b, below_b, above_b)]
        return tail(parts, sums_b, scale)

    def full(scale, *_):
        cuts = (HALO * SNAPS + 4 * GAP,)
        empty = jnp.zeros((1, 2, 2, 8, WIDTH), F32)
        strips, up, dn, pos, sums = smooth(0, SNAPS, cuts, FIRST_STEP, 0, empty)
        below, above = send(up, dn)
        return tail([(0, SNAPS, cuts, pos, strips, below, above)], sums, scale)

    return lax.cond(over <= 0, fast, full, scale, sums_b, strips_a, pos_a, below_a, above_a, strips_b, pos_b, up_b, dn_b)


def solution(mesh):
    in_specs = (P("snap", None, "tile", None), P("snap", None), P("snap"))
    out_specs = (P("snap", None, "tile", None), P("snap", None, "tile", None))
    return jax.shard_map(
        per_device, mesh=mesh, in_specs=in_specs, out_specs=out_specs, check_vma=False
    )
```

time: 184 us -> 194 us (1.054)
  waiting for transfers between devices: 11.9 us -> 38.2 us
  between operations: 16.6 us -> 5.29 us
  Pallas kernels: 94 us -> 103 us
  other arithmetic: 10.9 us -> 3.46 us
  starting transfers between devices: 42.7 us -> 35.9 us
    ppermute x4, waiting for transfers between devices: 8.05 us -> 24.7 us  [to_above(): return lax.ppermute(value, 'tile', [(i + 1, i) for i in range(size - 1)])]
    pallas_call x4, Pallas kernels: 21.8 us -> 37.5 us  [scale_level(): pl.pallas_call(functools.partial(scale_kernel, block), grid_spec=pltpu.Pr...]
    ppermute x4, waiting for transfers between devices: 3.82 us -> 13.5 us  [to_below(): return lax.ppermute(value, 'tile', [(i, i + 1) for i in range(size - 1)])]
    add x1 -> x0, other arithmetic: 8.45 us -> none  [tail(): theirs = sum((middle[HALF:] for middle in middles))]
    ppermute x4, starting transfers between devices: 29.7 us -> 22.6 us  [to_above(): return lax.ppermute(value, 'tile', [(i + 1, i) for i in range(size - 1)])]
    pallas_call x3, Pallas kernels: 29.1 us -> 24.9 us  [finish_level(): pl.pallas_call(functools.partial(finish_kernel, level, plan), in_specs=[s...]
    pallas_call x2, Pallas kernels: 43.1 us -> 40.1 us  [smooth_part(): pl.pallas_call(functools.partial(smooth_kernel, first, count, cuts, step,...]
    reduce_max x0 -> x3, other arithmetic: none -> 2.16 us  [the longest x2 1.45 us: per_device(): jnp.max(jnp.concatenate([excess(dy, 0, FIRST_CUTS, FIRST), excess(dy, FIR...]
  transfers between devices with their start and end apart: 13 -> 13, of which waited for: 2 -> 3; matrix products, arithmetic and copies ran while one was open for 6% -> 1% of each run, Pallas kernels for 41% -> 43%
where the time goes in v2:
time: 194 us; the launch traced here: 192 us
  Pallas kernels  103 us (53%)
  waiting for transfers between devices  38.2 us (20%)
  starting transfers between devices  35.9 us (19%)
  local copies, waits for them, and re-layouts  6.89 us (4%)
  between operations  5.29 us (3%)
  other arithmetic  3.46 us (2%)
    pallas_call x2, Pallas kernels, smooth_part(): pl.pallas_call(functools.partial(smooth_kernel, first, count, cuts, step,...  40.1 us
    pallas_call x4, Pallas kernels, scale_level(): pl.pallas_call(functools.partial(scale_kernel, block), grid_spec=pltpu.Pr...  37.5 us
    pallas_call x3, Pallas kernels, finish_level(): pl.pallas_call(functools.partial(finish_kernel, level, plan), in_specs=[s...  24.9 us
    ppermute x4, waiting for transfers between devices, to_above(): return lax.ppermute(value, 'tile', [(i + 1, i) for i in range(size - 1)])  24.7 us
    ppermute x4, starting transfers between devices, to_above(): return lax.ppermute(value, 'tile', [(i + 1, i) for i in range(size - 1)])  22.6 us
    ppermute x4, waiting for transfers between devices, to_below(): return lax.ppermute(value, 'tile', [(i, i + 1) for i in range(size - 1)])  13.5 us
    ppermute x4, starting transfers between devices, to_below(): return lax.ppermute(value, 'tile', [(i, i + 1) for i in range(size - 1)])  9.3 us
    cond x20, local copies, waits for them, and re-layouts  6.11 us
  transfers between devices with their start and end apart: 13, of which 3 were waited for; matrix products, arithmetic and copies ran while one was open for 1% of the time, Pallas kernels for 43%

profile of v2, /device:TPU:97, one launch (start us, length us, event | category | flops | bytes accessed | tf_op | source)
XLA Modules:
  0.0 192.5 jit_solution(17711690252097646272)
XLA Ops:
  0.6 0.8 slice_bitcast_fusion.1
  1.4 0.7 subtract_remainder_fusion
  2.1 0.0 copy-start.11
  2.1 11.3 %smooth_part.4 = (f32[32,2,2,8,256]{4,3,2,1,0:T(8,128)}, f32[32,2,2,8,256]{4,3,2,1,0:T(8,128)}, f32[32,2,2,8,256]{4,3,2,1,0:T(8,128)}, f32[32,2,2,8,256]{4,3,2,1...) custom-call(s32[385]{0:T(512)S(1)} %pad_add_fusion.meta, ...), custom_call_target="tpu_custom_call" | custom-call | tf_op jit(solution)/shard_map/smooth_part/pallas_call | solution.py:231
  13.4 6.7 %collective-permute-start.17 = (f32[2,480,256]{2,1,0:T(8,128)}, f32[2,480,256]{2,1,0:T(8,128)S(1)}, u32[]{:S(2)}, u32[]{:S(2)}) collective-permute-start(f32[2,480,256]{2,1,0:T(8,128)} %get-tuple-element.149), channel_id=1, source_target_pairs={{1,0},{2,1},{3,2},{4,3},{5,4},{6,5},{7,6},{8,7},{9,8},{10,9},{11,1... | collective-permute-start | bytes 2949128 | tf_op jit(solution)/shard_map/ppermute | solution.py:406
  20.1 1.9 collective-permute-start.18
  22.1 0.2 clamp_reduce_fusion.3
  22.2 0.7 add_reduce_fusion.3
  24.9 0.1 clamp_bitcast_fusion.1
  25.0 0.2 clamp_reduce_fusion
  25.2 0.7 add_reduce_fusion
  27.9 0.1 convert_reduce_fusion
  28.0 1.0 collective-permute-start.16
  29.0 28.8 %smooth_part.5 = (f32[96,2,2,8,256]{4,3,2,1,0:T(8,128)}, f32[96,2,2,8,256]{4,3,2,1,0:T(8,128)}, f32[96,2,2,8,256]{4,3,2,1,0:T(8,128)}, f32[2,608,256]{2,1,0:T(8,...) custom-call(s32[385]{0:T(512)S(1)} %pad_add_fusion.meta, ...), custom_call_target="tpu_custom_call" | custom-call | tf_op jit(solution)/shard_map/smooth_part/pallas_call | solution.py:231
  57.8 0.0 collective-permute-done.16
  57.8 0.7 maximum_reduce_fusion
  59.2 0.1 maximum_divide_fusion
  59.3 0.0 collective-permute-done.18
  59.3 133.2 %conditional.1 = ((f32[36,2,64,256]{3,2,1,0:T(8,128)}, f32[36,3,64,256]{3,2,1,0:T(8,128)})) conditional(s32[]{:T(128)} %convert_element_type.10, (s32[385]{0:T(512)S(1)}, f32[128,2,64,256]{3,2,1,0:T(8,128)}, bf16[2,256,256]{2,1,0:T(8,128)(2,1)S(1)}, bf16[3,33,112,192]{3,2,1,0:T(8,128)(2,1)}, f32[36]{0:T(128)S(1)}) %tuple.40, ...), branch_computations={%region_14.15_spmd, %region_15.16_spmd} | conditional | bytes 159678816 | solution.py:484
  59.3 7.9 %collective-permute-start.7 = (f32[2,608,256]{2,1,0:T(8,128)}, f32[2,608,256]{2,1,0:T(8,128)S(1)}, u32[]{:S(2)}, u32[]{:S(2)}) collective-permute-start(f32[2,608,256]{2,1,0:T(8,128)} %get-tuple-element.94), channel_id=1, source_target_pairs={{1,0},{2,1},{3,2},{4,3},{5,4},{6,5},{7,6},{8,7},{9,8},{10,9},{11,1... | collective-permute-start | bytes 3735560 | tf_op jit(solution)/shard_map/cond/branch_1_fun/ppermute | solution.py:406
  67.2 1.9 collective-permute-start.8
  69.1 0.4 collective-permute-start.6
  69.5 24.7 %collective-permute-done.7.refs_6_ = f32[2,608,256]{2,1,0:T(8,128)S(1)} collective-permute-done((f32[2,608,256]{2,1,0:T(8,128)}, f32[2,608,256]{2,1,0:T(8,128)S(1)}, u32[]{:S(2)}, u32[]{:S(2)}) %collective-permute-start.7) | collective-permute-done | bytes 1245216 | tf_op jit(solution)/shard_map/cond/branch_1_fun/ppermute | solution.py:406
  94.2 7.9 %collective-permute-done.8.refs_7_.refs_9_.refs_8_ = f32[2,608,256]{2,1,0:T(8,128)S(1)} collective-permute-done((f32[2,608,256]{2,1,0:T(8,128)}, f32[2,608,256]{2,1,0:T(8,128)S(1)}, u32[]{:S(2)}, u32[]{:S(2)}) %collective-permute-start.8) | collective-permute-done | bytes 1245216 | tf_op jit(solution)/shard_map/cond/branch_1_fun/ppermute | solution.py:411
  102.2 1.1 copy-done.2
  103.3 8.0 %finish_level.9 = (f32[36,5,2,8,256]{4,3,2,1,0:T(8,128)}, f32[36,5,2,8,256]{4,3,2,1,0:T(8,128)}) custom-call(s32[385]{0:T(512)S(1)} %get-tuple-element.102.meta, s32[192]{0:T(256)S(1)} %get-tuple-element.88.refs_0_, s32[576]{0:T(1024)S(1)} %get-tuple-element.89.refs_1_, f32[32,2,2,8,256]{4,3,2,1,0:T(8,128)} %get-tuple-element.90.refs_2_, ...), custom_call_target="tpu_custom_call" | custom-call | tf_op jit(solution)/shard_map/cond/branch_1_fun/finish_level/pallas_call | solution.py:352
  111.3 1.2 collective-permute-start.9
  112.5 1.9 collective-permute-start.10
  114.5 3.4 %collective-permute-start.12 = (f32[2,408,256]{2,1,0:T(8,128)}, f32[2,408,256]{2,1,0:T(8,128)S(1)}, u32[]{:S(2)}, u32[]{:S(2)}) collective-permute-start(f32[2,408,256]{2,1,0:T(8,128)} %get-tuple-element.107), channel_id=1, source_target_pairs={{0,1},{1,2},{2,3},{3,4},{4,5},{5,6},{6,7},{7,8},{8,9},{9,10},{10,1... | collective-permute-start | bytes 2506760 | tf_op jit(solution)/shard_map/cond/branch_1_fun/ppermute | solution.py:411
  117.8 6.1 %collective-permute-start.11 = (f32[2,168,256]{2,1,0:T(8,128)S(1)}, f32[2,168,256]{2,1,0:T(8,128)S(1)}, u32[]{:S(2)}, u32[]{:S(2)}) collective-permute-start(f32[2,168,256]{2,1,0:T(8,128)S(1)} %get-tuple-element.106), channel_id=1, source_target_pairs={{1,0},{2,1},{3,2},{4,3},{5,4},{6,5},{7,6},{8,7},{9,8},{10,9},{11,1... | collective-permute-start | bytes 1032200 | tf_op jit(solution)/shard_map/cond/branch_1_fun/ppermute | solution.py:406
  124.0 0.0 collective-permute-done.6.other
  124.0 2.1 %collective-permute-start.13 = (f32[2,168,256]{2,1,0:T(8,128)}, f32[2,168,256]{2,1,0:T(8,128)S(1)}, u32[]{:S(2)}, u32[]{:S(2)}) collective-permute-start(f32[2,168,256]{2,1,0:T(8,128)} %get-tuple-element.108), channel_id=1, source_target_pairs={{0,1},{1,2},{2,3},{3,4},{4,5},{5,6},{6,7},{7,8},{8,9},{9,10},{10,1... | collective-permute-start | bytes 1032200 | tf_op jit(solution)/shard_map/cond/branch_1_fun/ppermute | solution.py:411
  126.1 9.3 %scale_level.12 = (f32[36,2,64,256]{3,2,1,0:T(8,128)}, f32[36,3,64,256]{3,2,1,0:T(8,128)}) custom-call(f32[36]{0:T(128)S(1)} %get-tuple-element.81.scale, f32[36,5,2,8,256]{4,3,2,1,0:T(8,128)} %get-tuple-element.83.mine, f32[36,5,2,8,256]{4,3,2,1,0:T(8,128)} %collective-permute-done.6.other), custom_call_target="tpu_custom_call" | custom-call | tf_op jit(solution)/shard_map/cond/branch_1_fun/scale_level/pallas_call | solution.py:385
  135.4 5.6 %collective-permute-done.12.refs_10_.refs_9_ = f32[2,408,256]{2,1,0:T(8,128)S(1)} collective-permute-done((f32[2,408,256]{2,1,0:T(8,128)}, f32[2,408,256]{2,1,0:T(8,128)S(1)}, u32[]{:S(2)}, u32[]{:S(2)}) %collective-permute-start.12) | collective-permute-done | bytes 835616 | tf_op jit(solution)/shard_map/cond/branch_1_fun/ppermute | solution.py:411
  141.0 0.9 copy-done.4
  141.9 8.6 %finish_level.11 = (f32[36,5,2,8,256]{4,3,2,1,0:T(8,128)}, f32[36,5,2,8,256]{4,3,2,1,0:T(8,128)}) custom-call(s32[385]{0:T(512)S(1)} %get-tuple-element.102.meta, s32[192]{0:T(256)S(1)} %get-tuple-element.88.refs_0_, s32[576]{0:T(1024)S(1)} %get-tuple-element.89.refs_1_, f32[32,2,2,8,256]{4,3,2,1,0:T(8,128)} %get-tuple-element.111.refs_2_, ...), custom_call_target="tpu_custom_call" | custom-call | tf_op jit(solution)/shard_map/cond/branch_1_fun/finish_level/pallas_call | solution.py:352
  150.5 1.3 collective-permute-start.15
  151.8 0.0 collective-permute-done.9.other
  151.8 1.6 copy-done.6
  153.4 9.6 %scale_level.13 = (f32[36,2,64,256]{3,2,1,0:T(8,128)}, f32[36,3,64,256]{3,2,1,0:T(8,128)}) custom-call(f32[36]{0:T(128)S(1)} %get-tuple-element.81.scale, f32[36,5,2,8,256]{4,3,2,1,0:T(8,128)} %get-tuple-element.96.mine, f32[36,5,2,8,256]{4,3,2,1,0:T(8,128)} %copy-done.6, ...), custom_call_target="tpu_custom_call", output_to_operand_aliasing={{0}: (3, {}), {1}: (4, {})} | custom-call | tf_op jit(solution)/shard_map/cond/branch_1_fun/scale_level/pallas_call | solution.py:385
  163.0 0.0 collective-permute-done.13.refs_11_
  163.0 0.7 copy-done.13
  163.8 0.1 copy-done.14
  163.9 8.2 %finish_level.10 = (f32[36,5,2,8,256]{4,3,2,1,0:T(8,128)}, f32[36,5,2,8,256]{4,3,2,1,0:T(8,128)}) custom-call(s32[385]{0:T(512)S(1)} %get-tuple-element.102.meta, s32[192]{0:T(256)S(1)} %get-tuple-element.88.refs_0_, s32[576]{0:T(1024)S(1)} %get-tuple-element.89.refs_1_, f32[32,2,2,8,256]{4,3,2,1,0:T(8,128)S(1)} %copy-done.12, ...), custom_call_target="tpu_custom_call" | custom-call | tf_op jit(solution)/shard_map/cond/branch_1_fun/finish_level/pallas_call | solution.py:352
  172.1 0.1 collective-permute-start.14
  172.2 9.3 %scale_level.14 = (f32[36,2,64,256]{3,2,1,0:T(8,128)}, f32[36,3,64,256]{3,2,1,0:T(8,128)}) custom-call(f32[36]{0:T(128)S(1)} %get-tuple-element.81.scale, f32[36,5,2,8,256]{4,3,2,1,0:T(8,128)} %get-tuple-element.113.mine, f32[36,5,2,8,256]{4,3,2,1,0:T(8,128)} %collective-permute-done.15.other, ...), custom_call_target="tpu_custom_call", output_to_operand_aliasing={{0}: (3, {}), {1}: (4, {})} | custom-call | tf_op jit(solution)/shard_map/cond/branch_1_fun/scale_level/pallas_call | solution.py:385
  181.5 1.6 copy-done.10
  183.2 9.3 %scale_level.15 = (f32[36,2,64,256]{3,2,1,0:T(8,128)}, f32[36,3,64,256]{3,2,1,0:T(8,128)}) custom-call(f32[36]{0:T(128)S(1)} %get-tuple-element.81.scale, f32[36,5,2,8,256]{4,3,2,1,0:T(8,128)} %get-tuple-element.109.mine, f32[36,5,2,8,256]{4,3,2,1,0:T(8,128)} %copy-done.10, ...), custom_call_target="tpu_custom_call", output_to_operand_aliasing={{0}: (3, {}), {1}: (4, {})} | custom-call | tf_op jit(solution)/shard_map/cond/branch_1_fun/scale_level/pallas_call | solution.py:385
  (27 shorter events, 0.1 us)
Async XLA Ops:
  2.1 20.0 %copy-start.15 = (s32[128,2]{0,1:T(2,128)S(1)}, s32[128,2]{0,1:T(2,128)}, u32[]{:S(2)}) copy-start(s32[128,2]{0,1:T(2,128)} %param.8) | copy-start | bytes 3076
  2.1 26.9 %copy-start.11 = (bf16[2,256,256]{2,1,0:T(8,128)(2,1)S(1)}, bf16[2,256,256]{2,1,0:T(8,128)(2,1)}, u32[]{:S(2)}) copy-start(bf16[2,256,256]{2,1,0:T(8,128)(2,1)} %constant.118.clone.refs_1_) | copy-start | bytes 786436
  13.4 45.9 %collective-permute-start.17 = (f32[2,480,256]{2,1,0:T(8,128)}, f32[2,480,256]{2,1,0:T(8,128)S(1)}, u32[]{:S(2)}, u32[]{:S(2)}) collective-permute-start(f32[2,480,256]{2,1,0:T(8,128)} %get-tuple-element.149), channel_id=1, source_target_pairs={{1,0},{2,1},{3,2},{4,3},{5,4},{6,5},{7,6},{8,7},{9,8},{10,9},{11,1... | collective-permute-start | bytes 2949128 | tf_op jit(solution)/shard_map/ppermute | solution.py:406
  20.1 39.2 %collective-permute-start.18 = (f32[2,480,256]{2,1,0:T(8,128)}, f32[2,480,256]{2,1,0:T(8,128)S(1)}, u32[]{:S(2)}, u32[]{:S(2)}) collective-permute-start(f32[2,480,256]{2,1,0:T(8,128)} %get-tuple-element.150), channel_id=1, source_target_pairs={{0,1},{1,2},{2,3},{3,4},{4,5},{5,6},{6,7},{7,8},{8,9},{9,10},{10,1... | collective-permute-start | bytes 2949128 | tf_op jit(solution)/shard_map/ppermute | solution.py:411
  28.0 29.9 %collective-permute-start.16 = (s32[80]{0:T(128)S(1)}, s32[80]{0:T(128)S(1)}, u32[]{:S(2)}, u32[]{:S(2)}) collective-permute-start(s32[80]{0:T(128)S(1)} %concatenate.7), channel_id=1, source_target_pairs={{0,64},{64,0},{1,65},{65,1},{2,66},{66,2},{3,67},{67,3},{4,68},{68... | collective-permute-start | bytes 968 | tf_op jit(solution)/shard_map/ppermute | solution.py:401
  59.3 34.9 %collective-permute-start.7 = (f32[2,608,256]{2,1,0:T(8,128)}, f32[2,608,256]{2,1,0:T(8,128)S(1)}, u32[]{:S(2)}, u32[]{:S(2)}) collective-permute-start(f32[2,608,256]{2,1,0:T(8,128)} %get-tuple-element.94), channel_id=1, source_target_pairs={{1,0},{2,1},{3,2},{4,3},{5,4},{6,5},{7,6},{8,7},{9,8},{10,9},{11,1... | collective-permute-start | bytes 3735560 | tf_op jit(solution)/shard_map/cond/branch_1_fun/ppermute | solution.py:406
  67.2 35.0 %collective-permute-start.8 = (f32[2,608,256]{2,1,0:T(8,128)}, f32[2,608,256]{2,1,0:T(8,128)S(1)}, u32[]{:S(2)}, u32[]{:S(2)}) collective-permute-start(f32[2,608,256]{2,1,0:T(8,128)} %get-tuple-element.95), channel_id=1, source_target_pairs={{0,1},{1,2},{2,3},{3,4},{4,5},{5,6},{6,7},{7,8},{8,9},{9,10},{10,1... | collective-permute-start | bytes 3735560 | tf_op jit(solution)/shard_map/cond/branch_1_fun/ppermute | solution.py:411
  69.1 54.9 %collective-permute-start.6 = (f32[36,5,2,8,256]{4,3,2,1,0:T(8,128)}, f32[36,5,2,8,256]{4,3,2,1,0:T(8,128)}, u32[]{:S(2)}, u32[]{:S(2)}) collective-permute-start(f32[36,5,2,8,256]{4,3,2,1,0:T(8,128)} %get-tuple-element.84), channel_id=1, source_target_pairs={{0,64},{64,0},{1,65},{65,1},{2,66},{66,2},{3,67},{67,3},{4,68},{68... | collective-permute-start | bytes 8847368 | tf_op jit(solution)/shard_map/cond/branch_1_fun/ppermute | solution.py:401
  94.2 7.9 %copy-start.1 = (f32[2,608,256]{2,1,0:T(8,128)}, f32[2,608,256]{2,1,0:T(8,128)S(1)}, u32[]{:S(2)}) copy-start(f32[2,608,256]{2,1,0:T(8,128)S(1)} %collective-permute-done.7.refs_6_) | copy-start | bytes 3735556 | tf_op jit(solution)/shard_map/cond
  102.2 1.1 copy-start.2
  111.3 40.5 %collective-permute-start.9 = (f32[36,5,2,8,256]{4,3,2,1,0:T(8,128)}, f32[36,5,2,8,256]{4,3,2,1,0:T(8,128)S(1)}, u32[]{:S(2)}, u32[]{:S(2)}) collective-permute-start(f32[36,5,2,8,256]{4,3,2,1,0:T(8,128)} %get-tuple-element.97), channel_id=1, source_target_pairs={{0,64},{64,0},{1,65},{65,1},{2,66},{66,2},{3,67},{67,3},{4,68},{68... | collective-permute-start | bytes 8847368 | tf_op jit(solution)/shard_map/cond/branch_1_fun/ppermute | solution.py:401
  112.5 22.9 %collective-permute-start.10 = (f32[2,408,256]{2,1,0:T(8,128)}, f32[2,408,256]{2,1,0:T(8,128)S(1)}, u32[]{:S(2)}, u32[]{:S(2)}) collective-permute-start(f32[2,408,256]{2,1,0:T(8,128)} %get-tuple-element.105), channel_id=1, source_target_pairs={{1,0},{2,1},{3,2},{4,3},{5,4},{6,5},{7,6},{8,7},{9,8},{10,9},{11,1... | collective-permute-start | bytes 2506760 | tf_op jit(solution)/shard_map/cond/branch_1_fun/ppermute | solution.py:406
  114.5 26.5 %collective-permute-start.12 = (f32[2,408,256]{2,1,0:T(8,128)}, f32[2,408,256]{2,1,0:T(8,128)S(1)}, u32[]{:S(2)}, u32[]{:S(2)}) collective-permute-start(f32[2,408,256]{2,1,0:T(8,128)} %get-tuple-element.107), channel_id=1, source_target_pairs={{0,1},{1,2},{2,3},{3,4},{4,5},{5,6},{6,7},{7,8},{8,9},{9,10},{10,1... | collective-permute-start | bytes 2506760 | tf_op jit(solution)/shard_map/cond/branch_1_fun/ppermute | solution.py:411
  117.8 45.2 %collective-permute-start.11 = (f32[2,168,256]{2,1,0:T(8,128)S(1)}, f32[2,168,256]{2,1,0:T(8,128)S(1)}, u32[]{:S(2)}, u32[]{:S(2)}) collective-permute-start(f32[2,168,256]{2,1,0:T(8,128)S(1)} %get-tuple-element.106), channel_id=1, source_target_pairs={{1,0},{2,1},{3,2},{4,3},{5,4},{6,5},{7,6},{8,7},{9,8},{10,9},{11,1... | collective-permute-start | bytes 1032200 | tf_op jit(solution)/shard_map/cond/branch_1_fun/ppermute | solution.py:406
  124.0 39.0 %collective-permute-start.13 = (f32[2,168,256]{2,1,0:T(8,128)}, f32[2,168,256]{2,1,0:T(8,128)S(1)}, u32[]{:S(2)}, u32[]{:S(2)}) collective-permute-start(f32[2,168,256]{2,1,0:T(8,128)} %get-tuple-element.108), channel_id=1, source_target_pairs={{0,1},{1,2},{2,3},{3,4},{4,5},{5,6},{6,7},{7,8},{8,9},{9,10},{10,1... | collective-permute-start | bytes 1032200 | tf_op jit(solution)/shard_map/cond/branch_1_fun/ppermute | solution.py:411
  135.4 5.6 %copy-start.3 = (f32[2,408,256]{2,1,0:T(8,128)}, f32[2,408,256]{2,1,0:T(8,128)S(1)}, u32[]{:S(2)}) copy-start(f32[2,408,256]{2,1,0:T(8,128)S(1)} %collective-permute-done.10.refs_7_) | copy-start | bytes 2506756 | tf_op jit(solution)/shard_map/cond
  141.0 0.9 copy-start.4
  150.5 21.7 %collective-permute-start.15 = (f32[36,5,2,8,256]{4,3,2,1,0:T(8,128)}, f32[36,5,2,8,256]{4,3,2,1,0:T(8,128)}, u32[]{:S(2)}, u32[]{:S(2)}) collective-permute-start(f32[36,5,2,8,256]{4,3,2,1,0:T(8,128)} %get-tuple-element.114), channel_id=1, source_target_pairs={{0,64},{64,0},{1,65},{65,1},{2,66},{66,2},{3,67},{67,3},{4,68},{68... | collective-permute-start | bytes 8847368 | tf_op jit(solution)/shard_map/cond/branch_1_fun/ppermute | solution.py:401
  151.8 1.6 copy-start.6
  153.4 10.5 %copy-start.5 = (f32[96,2,2,8,256]{4,3,2,1,0:T(8,128)S(1)}, f32[96,2,2,8,256]{4,3,2,1,0:T(8,128)}, u32[]{:S(2)}) copy-start(f32[96,2,2,8,256]{4,3,2,1,0:T(8,128)} %get-tuple-element.104.refs_3_) | copy-start | bytes 9437188 | tf_op jit(solution)/shard_map/cond
  153.4 10.5 %copy-start.12 = (f32[32,2,2,8,256]{4,3,2,1,0:T(8,128)S(1)}, f32[32,2,2,8,256]{4,3,2,1,0:T(8,128)}, u32[]{:S(2)}) copy-start(f32[32,2,2,8,256]{4,3,2,1,0:T(8,128)} %get-tuple-element.103.refs_2_) | copy-start | bytes 3145732 | tf_op jit(solution)/shard_map/cond
  163.0 0.8 copy-start.13
  163.0 0.8 copy-start.14
  172.1 9.4 %collective-permute-start.14 = (f32[36,5,2,8,256]{4,3,2,1,0:T(8,128)}, f32[36,5,2,8,256]{4,3,2,1,0:T(8,128)S(1)}, u32[]{:S(2)}, u32[]{:S(2)}) collective-permute-start(f32[36,5,2,8,256]{4,3,2,1,0:T(8,128)} %get-tuple-element.110), channel_id=1, source_target_pairs={{0,64},{64,0},{1,65},{65,1},{2,66},{66,2},{3,67},{67,3},{4,68},{68... | collective-permute-start | bytes 8847368 | tf_op jit(solution)/shard_map/cond/branch_1_fun/ppermute | solution.py:401
  181.5 1.6 copy-start.10

commit v3 on v2

v3 whole, which is shorter than its diff:
```python
import functools

import jax
import jax.numpy as jnp
import numpy as np
from jax import lax
from jax.experimental import pallas as pl
from jax.experimental.pallas import tpu as pltpu
from jax.sharding import PartitionSpec as P

PHASES = 72
HALF = PHASES // 2
RAD = 8
MAXS = 16
HALO = RAD + MAXS
ROWS = 64
WIDTH = 256
SNAPS = 128
EXT = ROWS + 2 * HALO
GROUP = 8
CHUNK = 64
GAP = 16
MIB = 1024 * 1024
FIRST = 32
FIRST_CUTS = (480,)
REST_CUTS = (608, 1016, 1184)
F32 = jnp.float32
BF16 = jnp.bfloat16
I32 = jnp.int32


def taps():
    steps = np.arange(2 * RAD + 1, dtype=np.float64) - RAD
    sigma = RAD / 2.0
    values = np.exp(-steps * steps / (2.0 * sigma * sigma))
    return values / values.sum()


def split_const(values):
    high = values.astype(BF16)
    low = (values - high.astype(np.float64)).astype(BF16)
    return high, low


def column_constant():
    weight = taps()
    source = np.arange(WIDTH)[:, None]
    target = np.arange(WIDTH)[None, :]
    distance = source - target
    band = np.where(np.abs(distance) <= RAD, weight[np.clip(distance + RAD, 0, 2 * RAD)], 0.0)
    return np.stack(split_const(band))


def row_constant():
    weight = taps()
    target = np.arange(EXT)[None, :, None] - HALO
    source = np.arange(ROWS)[None, None, :]
    shift = np.arange(-MAXS, MAXS + 1)[:, None, None]
    distance = source - shift - target
    band = np.where(np.abs(distance) <= RAD, weight[np.clip(distance + RAD, 0, 2 * RAD)], 0.0)
    seen = source - shift
    kinds = []
    for kind in range(3):
        keep = np.ones_like(seen, dtype=bool)
        if kind == 0:
            keep = seen >= 0
        if kind == 2:
            keep = seen < ROWS
        high, low = split_const(np.where(keep, band, 0.0))
        kinds.append(np.concatenate([high, low, high], axis=2))
    return np.stack(kinds)


def level_rows(need, level):
    return jnp.clip(need - 8 * level, 0, 8)


def needs(dy):
    return jnp.clip(RAD + dy, 0, HALO), jnp.clip(RAD - dy, 0, HALO)


def next_start(end):
    return (end & -8) + 16


def split(value):
    high = value.astype(BF16)
    return high, (value - high.astype(F32)).astype(BF16)


def smooth_kernel(first, count, cuts, earlier, meta, *refs):
    pieces = len(cuts)
    groups = count // GROUP
    vel, colop, rowop, refs = *refs[:3], refs[3:]
    if earlier is not None:
        early_strip, refs = refs[0], refs[1:]
    strips = 3 if earlier is not None else 4
    y_refs, refs = refs[:strips], refs[strips:]
    out_up, out_dn = refs[:pieces], refs[pieces:2 * pieces]
    pos_ref, refs = refs[2 * pieces], refs[2 * pieces + 1:]
    if earlier is not None:
        mine, theirs, early_buf, acc, refs = *refs[:4], refs[4:]
    vel_buf, oper_buf, col_buf, refs = *refs[:3], refs[3:]
    y_bufs, refs = refs[:strips], refs[strips:]
    xs_hi, xs_lo, stack, up, dn, cursor, load_sem, store_sem, sem = refs
    row = lax.broadcasted_iota(I32, (8, WIDTH), 0)
    lane = lax.broadcasted_iota(I32, (1, WIDTH), 1)
    dot = functools.partial(jnp.dot, preferred_element_type=F32)

    def load(g):
        return pltpu.make_async_copy(
            vel.at[pl.ds(first + GROUP * g, GROUP)], vel_buf.at[pl.ds(GROUP * g, GROUP)], load_sem.at[g])

    def store(g, level):
        part = pl.ds(GROUP * g, GROUP)
        return pltpu.make_async_copy(y_bufs[level].at[part], y_refs[level].at[part], store_sem.at[g, level])

    def add_fields(phase, place, u, v):
        for at_field, field in enumerate((u, v, u * u, v * v, u * v)):
            acc[phase, at_field, place] += field

    load(0).start()
    tables = [pltpu.make_async_copy(colop, col_buf, sem.at[0]),
              pltpu.make_async_copy(rowop.at[meta[3 * SNAPS]], oper_buf, sem.at[1])]
    for copy in tables:
        copy.start()
    for g in range(1, groups):
        load(g).start()
    if earlier is not None:
        early = pltpu.make_async_copy(early_strip, early_buf, sem.at[2])
        early.start()
        acc[...] = jnp.zeros_like(acc)

    def count_rows(n, sums):
        dy = meta[first + n]
        out = list(sums)
        for side, need in enumerate(needs(dy)):
            for level in range(3):
                out[3 * side + level] += level_rows(need, level)
        return tuple(out)

    sums = lax.fori_loop(0, count, count_rows, (I32(0),) * 6)
    for side in range(2):
        start = I32(0)
        for level in range(3):
            cursor[3 * side + level] = start
            start = next_start(start + sums[3 * side + level])
    if earlier is not None:
        early.wait()

        def one_early(n, carry):
            phase = meta[2 * SNAPS + earlier + n]
            for place in range(2):
                add_fields(phase, place, early_buf[n, place, 0], early_buf[n, place, 1])
            return carry

        lax.fori_loop(0, first - earlier, one_early, 0)
    for copy in tables:
        copy.wait()

    def group(g, carry):
        load(g).wait()
        for b in range(GROUP):
            n = first + GROUP * g + b
            dx = meta[SNAPS + n]
            rolled = pltpu.roll(vel_buf[GROUP * g + b].reshape(2 * ROWS, WIDTH), (WIDTH - dx) & (WIDTH - 1), 1)
            moved = lane + dx
            high, low = split(jnp.where((moved >= 0) & (moved < WIDTH), rolled, 0.0))
            xs_hi[2 * ROWS * b:2 * ROWS * (b + 1)] = high
            xs_lo[2 * ROWS * b:2 * ROWS * (b + 1)] = low
        horizontal = dot(xs_hi[...], col_buf[0]) + dot(xs_hi[...], col_buf[1]) + dot(xs_lo[...], col_buf[0])
        high, low = split(horizontal)
        for b in range(GROUP):
            for comp in range(2):
                rows = slice(ROWS * (2 * b + comp), ROWS * (2 * b + comp + 1))
                stack[b, comp, 0:ROWS] = high[rows]
                stack[b, comp, ROWS:2 * ROWS] = high[rows]
                stack[b, comp, 2 * ROWS:3 * ROWS] = low[rows]
        for b in range(GROUP):
            local = GROUP * g + b
            n = first + local
            oper = oper_buf[meta[n] + MAXS]
            ext = [dot(oper, stack[b, comp]) for comp in range(2)]
            for level in range(strips):
                for comp in range(2):
                    top = HALO + 8 * level
                    bottom = HALO + ROWS - 8 - 8 * level
                    y_bufs[level][local, 0, comp] = ext[comp][top:top + 8]
                    y_bufs[level][local, 1, comp] = ext[comp][bottom:bottom + 8]
            if earlier is not None:
                phase = meta[2 * SNAPS + n]
                for place in range(2):
                    rows = slice(2 * HALO + 8 * place, 2 * HALO + 8 * place + 8)
                    add_fields(phase, place, ext[0][rows], ext[1][rows])
            for side, need in enumerate(needs(meta[n])):
                buffer = (up, dn)[side]
                for level in range(3):
                    slot = 3 * side + level
                    have = level_rows(need, level)
                    pos = cursor[slot]
                    cursor[slot] = pos + have
                    pos_ref[6 * local + slot] = pos
                    skew = pos & 7
                    base = pl.multiple_of(pos - skew, 8)
                    source = 16 - 8 * level if side == 0 else HALO + ROWS + 8 * level
                    turn = (skew + have) & 7 if side == 0 else skew
                    for comp in range(2):
                        tile = pltpu.roll(ext[comp][source:source + 8], turn, 0)
                        old = buffer[comp, pl.ds(base, 8)]
                        buffer[comp, pl.ds(base, 8)] = jnp.where(row < skew, old, tile)
                        buffer[comp, pl.ds(base + 8, 8)] = tile
        for level in range(strips):
            store(g, level).start()
        return carry

    lax.fori_loop(0, groups, group, 0)
    copies = []
    low = 0
    for piece, high in enumerate(cuts):
        for side in range(2):
            copies.append(pltpu.make_async_copy(
                (up, dn)[side].at[:, low:high], (out_up, out_dn)[side][piece], sem.at[3 + len(copies)]))
        low = high
    if earlier is not None:
        copies.append(pltpu.make_async_copy(acc.at[0:HALF], mine, sem.at[3 + len(copies)]))
        copies.append(pltpu.make_async_copy(acc.at[HALF:PHASES], theirs, sem.at[3 + len(copies)]))
    for copy in copies:
        copy.start()
    for g in range(groups):
        for level in range(strips):
            store(g, level).wait()
    for copy in copies:
        copy.wait()


def smooth_part(meta, velocity, colop, rowop, first, count, cuts, earlier, early_strip):
    pieces = len(cuts)
    sizes = [high - low for low, high in zip((0,) + cuts[:-1], cuts)]
    any_space = pl.BlockSpec(memory_space=pl.ANY)
    smem = pl.BlockSpec(memory_space=pltpu.SMEM)
    piece_shapes = [jax.ShapeDtypeStruct((2, size, WIDTH), F32) for size in sizes]
    strip = jax.ShapeDtypeStruct((count, 2, 2, 8, WIDTH), F32)
    total = jax.ShapeDtypeStruct((HALF, 5, 2, 8, WIDTH), F32)
    room = cuts[-1] + GAP
    sums = earlier is not None
    strips = 3 if sums else 4
    sum_scratch = [pltpu.VMEM((max(first - earlier, 1), 2, 2, 8, WIDTH), F32),
                   pltpu.VMEM((PHASES, 5, 2, 8, WIDTH), F32)] if sums else []
    out = pl.pallas_call(
        functools.partial(smooth_kernel, first, count, cuts, earlier),
        in_specs=[smem] + [any_space] * (3 + sums),
        out_specs=[any_space] * (strips + 2 * pieces) + [smem] + [any_space] * (2 * sums),
        scratch_shapes=sum_scratch + [
            pltpu.VMEM((count, 2, ROWS, WIDTH), F32),
            pltpu.VMEM((2 * MAXS + 1, EXT, 3 * ROWS), BF16),
            pltpu.VMEM((2, WIDTH, WIDTH), BF16),
        ] + [pltpu.VMEM((count, 2, 2, 8, WIDTH), F32)] * strips + [
            pltpu.VMEM((GROUP * 2 * ROWS, WIDTH), BF16),
            pltpu.VMEM((GROUP * 2 * ROWS, WIDTH), BF16),
            pltpu.VMEM((GROUP, 2, 3 * ROWS, WIDTH), BF16),
            pltpu.VMEM((2, room, WIDTH), F32),
            pltpu.VMEM((2, room, WIDTH), F32),
            pltpu.SMEM((8,), I32),
            pltpu.SemaphoreType.DMA((count // GROUP,)),
            pltpu.SemaphoreType.DMA((count // GROUP, strips)),
            pltpu.SemaphoreType.DMA((5 + 2 * pieces,)),
        ],
        out_shape=[strip] * strips + piece_shapes * 2
        + [jax.ShapeDtypeStruct((count * 6,), I32)] + [total] * (2 * sums),
        compiler_params=pltpu.CompilerParams(vmem_limit_bytes=(10 + (count + 1) * 3 // 8) * 1024 * 1024),
        name="smooth_part",
    )(meta, velocity, colop, rowop, *([early_strip] if sums else []))
    up, dn = out[strips:strips + pieces], out[strips + pieces:strips + 2 * pieces]
    return out[:strips], up, dn, out[strips + 2 * pieces], out[strips + 2 * pieces + 1:]


def finish_kernel(level, parts, meta, *refs):
    count = len(parts)
    pos_refs, refs = refs[:count], refs[count:]
    y_refs, refs = refs[:count], refs[count:]
    piece_refs = []
    for _, _, cuts in parts:
        piece_refs.append((refs[:len(cuts)], refs[len(cuts):2 * len(cuts)]))
        refs = refs[2 * len(cuts):]
    mine, theirs, refs = refs[0], refs[1], refs[2:]
    acc, refs = refs[0], refs[1:]
    y_bufs, refs = refs[:count], refs[count:]
    buffers, refs = [refs[2 * k:2 * k + 2] for k in range(count)], refs[2 * count:]
    sem = refs[0]
    chunk = 32
    plans = []
    at_sem = 0
    for k, (_, size, cuts) in enumerate(parts):
        here = []
        low = 0
        for piece, high in enumerate(cuts):
            for side in range(2):
                begin = pos_refs[k][3 * side + level]
                end = pos_refs[k][6 * (size - 1) + 3 * side + level] + 16
                for row_at in range(low, high, CHUNK):
                    stop = min(row_at + CHUNK, high)
                    copy = pltpu.make_async_copy(
                        piece_refs[k][side][piece].at[:, row_at - low:stop - low],
                        buffers[k][side].at[:, row_at:stop], sem.at[at_sem])
                    here.append((copy, (begin < stop) & (end > row_at)))
                    at_sem += 1
            low = high
        for start in range(0, size, chunk):
            copy = pltpu.make_async_copy(
                y_refs[k].at[start:start + chunk], y_bufs[k].at[start:start + chunk], sem.at[at_sem])
            at_sem += 1
            plans.append((k, start, here + [(copy, None)]))
            here = []

    def each(group, action):
        for copy, needed in group:
            if needed is None:
                action(copy)
            else:
                pl.when(needed)(functools.partial(action, copy))

    for _, _, group in plans:
        each(group, lambda copy: copy.start())
    acc[...] = jnp.zeros_like(acc)
    row = lax.broadcasted_iota(I32, (8, WIDTH), 0)
    for k, start, group in plans:
        each(group, lambda copy: copy.wait())

        def one(local, k=k):
            n = parts[k][0] + local
            phase = meta[2 * SNAPS + n]
            for place in range(2):
                side = 1 - place
                have = level_rows(needs(meta[n])[side], level)
                pos = pos_refs[k][6 * local + 3 * side + level]
                skew = pos & 7
                base = pl.multiple_of(pos - skew, 8)
                fields = []
                turn = skew if place == 0 else (skew + have) & 7
                keep = row < have if place == 0 else row >= 8 - have
                for comp in range(2):
                    lower = buffers[k][side][comp, pl.ds(base, 8)]
                    upper = buffers[k][side][comp, pl.ds(base + 8, 8)]
                    tile = pltpu.roll(jnp.where(row >= skew, lower, upper), (8 - turn) & 7, 0)
                    fields.append(y_bufs[k][local, place, comp] + jnp.where(keep, tile, 0.0))
                u, v = fields
                for at_field, field in enumerate((u, v, u * u, v * v, u * v)):
                    acc[phase, at_field, place] += field

        def several(i, carry, one=one, start=start):
            for b in range(4):
                one(start + 4 * i + b)
            return carry

        lax.fori_loop(0, chunk // 4, several, 0)
    stores = [pltpu.make_async_copy(acc.at[HALF:PHASES], theirs, sem.at[0]),
              pltpu.make_async_copy(acc.at[0:HALF], mine, sem.at[1])]
    for copy in stores:
        copy.start()
    for copy in stores:
        copy.wait()


def finish_level(level, meta, parts):
    any_space = pl.BlockSpec(memory_space=pl.ANY)
    smem = pl.BlockSpec(memory_space=pltpu.SMEM)
    shape = jax.ShapeDtypeStruct((HALF, 5, 2, 8, WIDTH), F32)
    plan = [(first, count, level_cuts(cuts, level)) for first, count, cuts, *_ in parts]
    positions = [part[3] for part in parts]
    strips = [part[4][level] for part in parts]
    packs = [piece for part in parts for side in part[5:7] for piece in side[:len(level_cuts(part[2], level))]]
    scratch = [pltpu.VMEM((PHASES, 5, 2, 8, WIDTH), F32)]
    scratch += [pltpu.VMEM((count, 2, 2, 8, WIDTH), F32) for _, count, _ in plan]
    for _, _, cuts in plan:
        scratch += [pltpu.VMEM((2, cuts[-1] + GAP, WIDTH), F32)] * 2
    chunks = sum(2 * (-(-(high - low) // CHUNK)) for _, _, cuts in plan for low, high in zip((0,) + cuts[:-1], cuts))
    scratch.append(pltpu.SemaphoreType.DMA((SNAPS // 32 + chunks + 2,)))
    bytes_used = 4 * WIDTH * sum(2 * 2 * (cuts[-1] + GAP) for _, _, cuts in plan)
    return pl.pallas_call(
        functools.partial(finish_kernel, level, plan),
        in_specs=[smem] * (1 + len(positions)) + [any_space] * (len(strips) + len(packs)),
        out_specs=[any_space] * 2,
        out_shape=[shape] * 2,
        scratch_shapes=scratch,
        compiler_params=pltpu.CompilerParams(vmem_limit_bytes=12 * MIB + bytes_used),
        name="finish_level",
    )(meta, *positions, *strips, *packs)


def scale_kernel(level, block, scale, mine, other, *refs):
    mean, moment, a_buf, b_buf, mean_buf, moment_buf, sem = refs[-7:]
    count = HALF // block
    loads, stores = [], []
    for k in range(count):
        part = slice(block * k, block * (k + 1))
        loads.append([pltpu.make_async_copy(mine.at[part], a_buf.at[part], sem.at[2 * k]),
                      pltpu.make_async_copy(other.at[part], b_buf.at[part], sem.at[2 * k + 1])])
        group = []
        for place in range(2):
            rows = slice(8 * level, 8 * level + 8) if place == 0 else slice(ROWS - 8 - 8 * level, ROWS - 8 * level)
            for which, (buf, out) in enumerate(((mean_buf, mean), (moment_buf, moment))):
                group.append(pltpu.make_async_copy(
                    buf.at[place, part], out.at[part, :, rows], sem.at[2 * count + 4 * k + 2 * place + which]))
        stores.append(group)
    for copies in loads:
        for copy in copies:
            copy.start()
    for k in range(count):
        for copy in loads[k]:
            copy.wait()

        def one(p, carry):
            factor = scale[p]
            for place in range(2):
                total = (a_buf[p, :, place] + b_buf[p, :, place]) * factor
                mean_buf[place, p] = total[0:2]
                moment_buf[place, p] = total[2:5]
            return carry

        lax.fori_loop(block * k, block * (k + 1), one, 0)
        for copy in stores[k]:
            copy.start()
    for copies in stores:
        for copy in copies:
            copy.wait()


def scale_level(level, scale, mine, other, before):
    block = 18
    count = HALF // block
    any_space = pl.BlockSpec(memory_space=pl.ANY)
    return pl.pallas_call(
        functools.partial(scale_kernel, level, block),
        in_specs=[pl.BlockSpec(memory_space=pltpu.SMEM)] + [any_space] * (2 + len(before)),
        out_specs=[pl.BlockSpec(memory_space=pltpu.HBM)] * 2,
        out_shape=[jax.ShapeDtypeStruct((HALF, 2, ROWS, WIDTH), F32), jax.ShapeDtypeStruct((HALF, 3, ROWS, WIDTH), F32)],
        scratch_shapes=[
            pltpu.VMEM((HALF, 5, 2, 8, WIDTH), F32),
            pltpu.VMEM((HALF, 5, 2, 8, WIDTH), F32),
            pltpu.VMEM((2, HALF, 2, 8, WIDTH), F32),
            pltpu.VMEM((2, HALF, 3, 8, WIDTH), F32),
            pltpu.SemaphoreType.DMA((6 * count,)),
        ],
        input_output_aliases={3: 0, 4: 1} if before else {},
        compiler_params=pltpu.CompilerParams(vmem_limit_bytes=10 * MIB),
        name="scale_level",
    )(scale, mine, other, *before)


def to_partner(value):
    return lax.ppermute(value, "snap", [(0, 1), (1, 0)])


def to_above(value):
    size = lax.axis_size("tile")
    return lax.ppermute(value, "tile", [(i + 1, i) for i in range(size - 1)])


def to_below(value):
    size = lax.axis_size("tile")
    return lax.ppermute(value, "tile", [(i, i + 1) for i in range(size - 1)])


def level_cuts(cuts, level):
    return cuts[:level + 1] if len(cuts) == 3 else cuts


def excess(dy, first, cuts, count):
    need = jnp.stack(needs(dy[first:first + count]))
    over = []
    end = jnp.zeros((2,), I32)
    for level in range(3):
        end = next_start(end + jnp.sum(level_rows(need, level), axis=1))
        over.append(end - level_cuts(cuts, level)[-1])
    return jnp.concatenate(over)


def send(up_pieces, dn_pieces):
    from_below = [to_above(piece) for piece in up_pieces]
    from_above = [to_below(piece) for piece in dn_pieces]
    return from_below, from_above


def per_device(velocity, offsets, phase):
    snap = lax.axis_index("snap")
    tile = lax.axis_index("tile")
    dy, dx = offsets[:, 0].astype(I32), offsets[:, 1].astype(I32)
    turned = lax.rem(phase.astype(I32) + PHASES - HALF * snap, PHASES)
    kind = jnp.where(tile == 0, 0, jnp.where(tile == lax.axis_size("tile") - 1, 2, 1)).astype(I32)
    meta = jnp.concatenate([dy, dx, turned, kind[None]])
    colop = jnp.asarray(column_constant())
    rowop = jnp.asarray(row_constant())
    smooth = functools.partial(smooth_part, meta, velocity, colop, rowop)
    strips_a, up_a, dn_a, pos_a, _ = smooth(0, FIRST, FIRST_CUTS, None, None)
    below_a, above_a = send(up_a, dn_a)

    onehot = (turned[:, None] == jnp.arange(PHASES, dtype=I32)[None, :]).astype(I32)
    own = jnp.sum(onehot, axis=0)
    over = jnp.max(jnp.concatenate([excess(dy, 0, FIRST_CUTS, FIRST), excess(dy, FIRST, REST_CUTS, SNAPS - FIRST)]))
    message = jnp.concatenate([own, jnp.full((8,), over, I32)])
    reply = to_partner(message)
    scale = 1.0 / jnp.maximum((message[:HALF] + reply[HALF:PHASES]).astype(F32), 1.0)
    over = jnp.max(jnp.maximum(message[PHASES:], reply[PHASES:]))

    strips_b, up_b, dn_b, pos_b, sums_b = smooth(FIRST, SNAPS - FIRST, REST_CUTS, 0, strips_a[3])

    def tail(parts, sums, scale):
        before = scale_level(3, scale, sums[0], to_partner(sums[1]), ())
        here, before = lax.optimization_barrier((meta, before))
        waiting = []
        for level in range(3):
            mine, theirs = finish_level(level, here, parts)
            waiting.append((level, mine, to_partner(theirs)))
        for at, mine, other in waiting:
            before = scale_level(at, scale, mine, other, before)
        return tuple(before)

    def fast(scale, sums_b, strips_a, pos_a, below_a, above_a, strips_b, pos_b, up_b, dn_b):
        below_b, above_b = send(up_b, dn_b)
        parts = [(0, FIRST, FIRST_CUTS, pos_a, strips_a, below_a, above_a),
                 (FIRST, SNAPS - FIRST, REST_CUTS, pos_b, strips_b, below_b, above_b)]
        return tail(parts, sums_b, scale)

    def full(scale, *_):
        cuts = (HALO * SNAPS + 4 * GAP,)
        empty = jnp.zeros((1, 2, 2, 8, WIDTH), F32)
        strips, up, dn, pos, sums = smooth(0, SNAPS, cuts, 0, empty)
        below, above = send(up, dn)
        return tail([(0, SNAPS, cuts, pos, strips, below, above)], sums, scale)

    return lax.cond(over <= 0, fast, full, scale, sums_b, strips_a, pos_a, below_a, above_a, strips_b, pos_b, up_b, dn_b)


def solution(mesh):
    in_specs = (P("snap", None, "tile", None), P("snap", None), P("snap"))
    out_specs = (P("snap", None, "tile", None), P("snap", None, "tile", None))
    return jax.shard_map(
        per_device, mesh=mesh, in_specs=in_specs, out_specs=out_specs, check_vma=False
    )
```

time: 194 us -> 143 us (0.74)
  Pallas kernels: 103 us -> 69.5 us
  waiting for transfers between devices: 38.2 us -> 18.5 us
  starting transfers between devices: 35.9 us -> 44.4 us
  local copies, waits for them, and re-layouts: 6.89 us -> 0.8 us
    pallas_call x6, Pallas kernels: 77.7 us -> 50.7 us  [the longest x2 35.8 us: smooth_part(): pl.pallas_call(functools.partial(smooth_kernel, first, count, cuts, earli...]
    ppermute x4, waiting for transfers between devices: 13.5 us -> 3.14 us  [to_below(): return lax.ppermute(value, 'tile', [(i, i + 1) for i in range(size - 1)])]
    ppermute x4, waiting for transfers between devices: 24.7 us -> 15.3 us  [to_above(): return lax.ppermute(value, 'tile', [(i + 1, i) for i in range(size - 1)])]
    ppermute x4, starting transfers between devices: 22.6 us -> 30.6 us  [to_above(): return lax.ppermute(value, 'tile', [(i + 1, i) for i in range(size - 1)])]
    pallas_call x3, Pallas kernels: 24.9 us -> 18.8 us  [finish_level(): pl.pallas_call(functools.partial(finish_kernel, level, plan), in_specs=[s...]
    cond x20 -> x12, local copies, waits for them, and re-layouts: 6.11 us -> 0.02 us
    ppermute x5, starting transfers between devices: 4.04 us -> 6.11 us  [to_partner(): return lax.ppermute(value, 'snap', [(0, 1), (1, 0)])]
  transfers between devices with their start and end apart: 13 -> 13, of which waited for: 3 -> 2; matrix products, arithmetic and copies ran while one was open for 1% -> 2% of each run, Pallas kernels for 43% -> 39%
where the time goes in v3:
time: 143 us; the launch traced here: 142 us
  Pallas kernels  69.5 us (49%)
  starting transfers between devices  44.4 us (31%)
  waiting for transfers between devices  18.5 us (13%)
  between operations  5.41 us (4%)
  other arithmetic  3.45 us (2%)
    pallas_call x2, Pallas kernels, smooth_part(): pl.pallas_call(functools.partial(smooth_kernel, first, count, cuts, earli...  35.8 us
    ppermute x4, starting transfers between devices, to_above(): return lax.ppermute(value, 'tile', [(i + 1, i) for i in range(size - 1)])  30.6 us
    pallas_call x3, Pallas kernels, finish_level(): pl.pallas_call(functools.partial(finish_kernel, level, plan), in_specs=[s...  18.8 us
    ppermute x4, waiting for transfers between devices, to_above(): return lax.ppermute(value, 'tile', [(i + 1, i) for i in range(size - 1)])  15.3 us
    pallas_call x4, Pallas kernels, scale_level(): pl.pallas_call(functools.partial(scale_kernel, level, block), in_specs=[p...  14.9 us
    ppermute x4, starting transfers between devices, to_below(): return lax.ppermute(value, 'tile', [(i, i + 1) for i in range(size - 1)])  7.68 us
    ppermute x5, starting transfers between devices, to_partner(): return lax.ppermute(value, 'snap', [(0, 1), (1, 0)])  6.11 us
    ppermute x4, waiting for transfers between devices, to_below(): return lax.ppermute(value, 'tile', [(i, i + 1) for i in range(size - 1)])  3.14 us
  transfers between devices with their start and end apart: 13, of which 2 were waited for; matrix products, arithmetic and copies ran while one was open for 2% of the time, Pallas kernels for 39%

profile of v3, /device:TPU:97, one launch (start us, length us, event | category | flops | bytes accessed | tf_op | source)
XLA Modules:
  0.0 142.4 jit_solution(11282817201457901998)
XLA Ops:
  0.6 0.8 slice_bitcast_fusion.1
  1.4 0.7 subtract_remainder_fusion
  2.1 0.0 copy-start.8
  2.1 10.2 %smooth_part.4 = (f32[32,2,2,8,256]{4,3,2,1,0:T(8,128)}, f32[32,2,2,8,256]{4,3,2,1,0:T(8,128)}, f32[32,2,2,8,256]{4,3,2,1,0:T(8,128)}, f32[32,2,2,8,256]{4,3,2,1...) custom-call(s32[385]{0:T(512)S(1)} %pad_add_fusion.meta, ...), custom_call_target="tpu_custom_call" | custom-call | tf_op jit(solution)/shard_map/smooth_part/pallas_call | solution.py:249
  12.3 6.7 %collective-permute-start.17 = (f32[2,480,256]{2,1,0:T(8,128)S(1)}, f32[2,480,256]{2,1,0:T(8,128)}, u32[]{:S(2)}, u32[]{:S(2)}) collective-permute-start(f32[2,480,256]{2,1,0:T(8,128)S(1)} %get-tuple-element.147), channel_id=1, source_target_pairs={{1,0},{2,1},{3,2},{4,3},{5,4},{6,5},{7,6},{8,7},{9,8},{10,9},{11,1... | collective-permute-start | bytes 2949128 | tf_op jit(solution)/shard_map/ppermute | solution.py:456
  18.9 1.9 %collective-permute-start.18 = (f32[2,480,256]{2,1,0:T(8,128)S(1)}, f32[2,480,256]{2,1,0:T(8,128)}, u32[]{:S(2)}, u32[]{:S(2)}) collective-permute-start(f32[2,480,256]{2,1,0:T(8,128)S(1)} %get-tuple-element.148), channel_id=1, source_target_pairs={{0,1},{1,2},{2,3},{3,4},{4,5},{5,6},{6,7},{7,8},{8,9},{9,10},{10,1... | collective-permute-start | bytes 2949128 | tf_op jit(solution)/shard_map/ppermute | solution.py:461
  20.9 0.2 clamp_reduce_fusion.3
  21.1 0.7 add_reduce_fusion.3
  23.7 0.1 clamp_bitcast_fusion.1
  23.8 0.2 clamp_reduce_fusion
  24.0 0.7 add_reduce_fusion
  26.6 0.1 convert_reduce_fusion
  26.7 1.0 collective-permute-start.16
  27.8 25.7 %smooth_part.5 = (f32[96,2,2,8,256]{4,3,2,1,0:T(8,128)}, f32[96,2,2,8,256]{4,3,2,1,0:T(8,128)}, f32[96,2,2,8,256]{4,3,2,1,0:T(8,128)}, f32[2,608,256]{2,1,0:T(8,...) custom-call(s32[385]{0:T(512)S(1)} %pad_add_fusion.meta, ...), custom_call_target="tpu_custom_call" | custom-call | tf_op jit(solution)/shard_map/smooth_part/pallas_call | solution.py:249
  53.5 0.0 collective-permute-done.16
  53.5 0.7 maximum_reduce_fusion
  54.8 0.1 maximum_divide_fusion
  54.9 0.0 collective-permute-done.17
  54.9 0.0 collective-permute-done.18
  54.9 87.3 %conditional.1 = ((f32[36,2,64,256]{3,2,1,0:T(8,128)}, f32[36,3,64,256]{3,2,1,0:T(8,128)})) conditional(s32[]{:T(128)} %convert_element_type.10, (s32[385]{0:T(512)S(1)}, f32[128,2,64,256]{3,2,1,0:T(8,128)}, bf16[2,256,256]{2,1,0:T(8,128)(2,1)S(1)}, bf16[3,33,112,192]{3,2,1,0:T(8,128)(2,1)}, f32[36]{0:T(128)S(1)}) %tuple.36, ...), branch_computations={%region_14.15_spmd, %region_15.16_spmd} | conditional | bytes 160739712 | solution.py:531
  55.2 0.2 collective-permute-start.6
  55.4 8.1 %collective-permute-start.7 = (f32[2,608,256]{2,1,0:T(8,128)}, f32[2,608,256]{2,1,0:T(8,128)S(1)}, u32[]{:S(2)}, u32[]{:S(2)}) collective-permute-start(f32[2,608,256]{2,1,0:T(8,128)} %get-tuple-element.91), channel_id=1, source_target_pairs={{1,0},{2,1},{3,2},{4,3},{5,4},{6,5},{7,6},{8,7},{9,8},{10,9},{11,1... | collective-permute-start | bytes 3735560 | tf_op jit(solution)/shard_map/cond/branch_1_fun/ppermute | solution.py:456
  63.5 1.9 %collective-permute-start.10 = (f32[2,608,256]{2,1,0:T(8,128)}, f32[2,608,256]{2,1,0:T(8,128)S(1)}, u32[]{:S(2)}, u32[]{:S(2)}) collective-permute-start(f32[2,608,256]{2,1,0:T(8,128)} %get-tuple-element.94), channel_id=1, source_target_pairs={{0,1},{1,2},{2,3},{3,4},{4,5},{5,6},{6,7},{7,8},{8,9},{9,10},{10,1... | collective-permute-start | bytes 3735560 | tf_op jit(solution)/shard_map/cond/branch_1_fun/ppermute | solution.py:461
  65.4 7.6 %collective-permute-start.8 = (f32[2,408,256]{2,1,0:T(8,128)}, f32[2,408,256]{2,1,0:T(8,128)S(1)}, u32[]{:S(2)}, u32[]{:S(2)}) collective-permute-start(f32[2,408,256]{2,1,0:T(8,128)} %get-tuple-element.92), channel_id=1, source_target_pairs={{1,0},{2,1},{3,2},{4,3},{5,4},{6,5},{7,6},{8,7},{9,8},{10,9},{11,1... | collective-permute-start | bytes 2506760 | tf_op jit(solution)/shard_map/cond/branch_1_fun/ppermute | solution.py:456
  73.0 1.9 %collective-permute-start.11 = (f32[2,408,256]{2,1,0:T(8,128)}, f32[2,408,256]{2,1,0:T(8,128)S(1)}, u32[]{:S(2)}, u32[]{:S(2)}) collective-permute-start(f32[2,408,256]{2,1,0:T(8,128)} %get-tuple-element.95), channel_id=1, source_target_pairs={{0,1},{1,2},{2,3},{3,4},{4,5},{5,6},{6,7},{7,8},{8,9},{9,10},{10,1... | collective-permute-start | bytes 2506760 | tf_op jit(solution)/shard_map/cond/branch_1_fun/ppermute | solution.py:461
  74.9 15.3 %collective-permute-done.7.refs_6_ = f32[2,608,256]{2,1,0:T(8,128)S(1)} collective-permute-done((f32[2,608,256]{2,1,0:T(8,128)}, f32[2,608,256]{2,1,0:T(8,128)S(1)}, u32[]{:S(2)}, u32[]{:S(2)}) %collective-permute-start.7) | collective-permute-done | bytes 1245216 | tf_op jit(solution)/shard_map/cond/branch_1_fun/ppermute | solution.py:456
  90.2 8.2 %collective-permute-start.9 = (f32[2,168,256]{2,1,0:T(8,128)}, f32[2,168,256]{2,1,0:T(8,128)S(1)}, u32[]{:S(2)}, u32[]{:S(2)}) collective-permute-start(f32[2,168,256]{2,1,0:T(8,128)} %get-tuple-element.93), channel_id=1, source_target_pairs={{1,0},{2,1},{3,2},{4,3},{5,4},{6,5},{7,6},{8,7},{9,8},{10,9},{11,1... | collective-permute-start | bytes 1032200 | tf_op jit(solution)/shard_map/cond/branch_1_fun/ppermute | solution.py:456
  98.4 0.0 collective-permute-done.6.other
  98.5 1.9 %collective-permute-start.12 = (f32[2,168,256]{2,1,0:T(8,128)}, f32[2,168,256]{2,1,0:T(8,128)S(1)}, u32[]{:S(2)}, u32[]{:S(2)}) collective-permute-start(f32[2,168,256]{2,1,0:T(8,128)} %get-tuple-element.96), channel_id=1, source_target_pairs={{0,1},{1,2},{2,3},{3,4},{4,5},{5,6},{6,7},{7,8},{8,9},{9,10},{10,1... | collective-permute-start | bytes 1032200 | tf_op jit(solution)/shard_map/cond/branch_1_fun/ppermute | solution.py:461
  100.4 3.9 %scale_level.12 = (f32[36,2,64,256]{3,2,1,0:T(8,128)}, f32[36,3,64,256]{3,2,1,0:T(8,128)}) custom-call(f32[36]{0:T(128)S(1)} %get-tuple-element.78.scale, f32[36,5,2,8,256]{4,3,2,1,0:T(8,128)} %get-tuple-element.80.mine, f32[36,5,2,8,256]{4,3,2,1,0:T(8,128)S(1)} %collective-permute-done.6.other), custom_call_target="tpu_custom_call" | custom-call | tf_op jit(solution)/shard_map/cond/branch_1_fun/scale_level/pallas_call | solution.py:432
  104.3 0.0 collective-permute-done.10.refs_9_.refs_8_.refs_7_
  104.3 0.0 copy-done.5
  104.3 6.5 %finish_level.11 = (f32[36,5,2,8,256]{4,3,2,1,0:T(8,128)S(1)}, f32[36,5,2,8,256]{4,3,2,1,0:T(8,128)S(1)}) custom-call(s32[385]{0:T(512)S(1)} %get-tuple-element.84.meta, s32[192]{0:T(256)S(1)} %get-tuple-element.85.refs_0_, s32[576]{0:T(1024)S(1)} %get-tuple-element.86.refs_1_, f32[32,2,2,8,256]{4,3,2,1,0:T(8,128)S(1)} %copy-done.9, ...), custom_call_target="tpu_custom_call" | custom-call | tf_op jit(solution)/shard_map/cond/branch_1_fun/finish_level/pallas_call | solution.py:379
  110.9 2.0 %collective-permute-start.15 = (f32[36,5,2,8,256]{4,3,2,1,0:T(8,128)S(1)}, f32[36,5,2,8,256]{4,3,2,1,0:T(8,128)S(1)}, u32[]{:S(2)}, u32[]{:S(2)}) collective-permute-start(f32[36,5,2,8,256]{4,3,2,1,0:T(8,128)S(1)} %get-tuple-element.106), channel_id=1, source_target_pairs={{0,64},{64,0},{1,65},{65,1},{2,66},{66,2},{3,67},{67,3},{4,68},{68... | collective-permute-start | bytes 8847368 | tf_op jit(solution)/shard_map/cond/branch_1_fun/ppermute | solution.py:451
  112.9 0.0 collective-permute-done.8.refs_7_
  112.9 3.1 %collective-permute-done.11.refs_10_.refs_9_ = f32[2,408,256]{2,1,0:T(8,128)S(1)} collective-permute-done((f32[2,408,256]{2,1,0:T(8,128)}, f32[2,408,256]{2,1,0:T(8,128)S(1)}, u32[]{:S(2)}, u32[]{:S(2)}) %collective-permute-start.11) | collective-permute-done | bytes 835616 | tf_op jit(solution)/shard_map/cond/branch_1_fun/ppermute | solution.py:461
  116.1 6.3 %finish_level.10 = (f32[36,5,2,8,256]{4,3,2,1,0:T(8,128)S(1)}, f32[36,5,2,8,256]{4,3,2,1,0:T(8,128)S(1)}) custom-call(s32[385]{0:T(512)S(1)} %get-tuple-element.84.meta, s32[192]{0:T(256)S(1)} %get-tuple-element.85.refs_0_, s32[576]{0:T(1024)S(1)} %get-tuple-element.86.refs_1_, f32[32,2,2,8,256]{4,3,2,1,0:T(8,128)S(1)} %copy-done.11, ...), custom_call_target="tpu_custom_call" | custom-call | tf_op jit(solution)/shard_map/cond/branch_1_fun/finish_level/pallas_call | solution.py:379
  122.4 2.7 %collective-permute-start.14 = (f32[36,5,2,8,256]{4,3,2,1,0:T(8,128)S(1)}, f32[36,5,2,8,256]{4,3,2,1,0:T(8,128)S(1)}, u32[]{:S(2)}, u32[]{:S(2)}) collective-permute-start(f32[36,5,2,8,256]{4,3,2,1,0:T(8,128)S(1)} %get-tuple-element.102), channel_id=1, source_target_pairs={{0,64},{64,0},{1,65},{65,1},{2,66},{66,2},{3,67},{67,3},{4,68},{68... | collective-permute-start | bytes 8847368 | tf_op jit(solution)/shard_map/cond/branch_1_fun/ppermute | solution.py:451
  125.0 0.0 collective-permute-done.9.refs_8_
  125.0 0.0 collective-permute-done.12.refs_11_
  125.1 5.9 %finish_level.9 = (f32[36,5,2,8,256]{4,3,2,1,0:T(8,128)S(1)}, f32[36,5,2,8,256]{4,3,2,1,0:T(8,128)S(1)}) custom-call(s32[385]{0:T(512)S(1)} %get-tuple-element.84.meta, s32[192]{0:T(256)S(1)} %get-tuple-element.85.refs_0_, s32[576]{0:T(1024)S(1)} %get-tuple-element.86.refs_1_, f32[32,2,2,8,256]{4,3,2,1,0:T(8,128)S(1)} %copy-done.10, ...), custom_call_target="tpu_custom_call" | custom-call | tf_op jit(solution)/shard_map/cond/branch_1_fun/finish_level/pallas_call | solution.py:379
  131.0 0.2 collective-permute-start.13
  131.2 0.0 collective-permute-done.15.other
  131.2 3.7 %scale_level.13 = (f32[36,2,64,256]{3,2,1,0:T(8,128)}, f32[36,3,64,256]{3,2,1,0:T(8,128)}) custom-call(f32[36]{0:T(128)S(1)} %get-tuple-element.78.scale, f32[36,5,2,8,256]{4,3,2,1,0:T(8,128)S(1)} %get-tuple-element.105.mine, f32[36,5,2,8,256]{4,3,2,1,0:T(8,128)S(1)} %collective-permute-done.15.other, ...), custom_call_target="tpu_custom_call", output_to_operand_aliasing={{0}: (3, {}), {1}: (4, {})} | custom-call | tf_op jit(solution)/shard_map/cond/branch_1_fun/scale_level/pallas_call | solution.py:432
  134.9 0.0 collective-permute-done.14.other
  134.9 3.7 %scale_level.14 = (f32[36,2,64,256]{3,2,1,0:T(8,128)}, f32[36,3,64,256]{3,2,1,0:T(8,128)}) custom-call(f32[36]{0:T(128)S(1)} %get-tuple-element.78.scale, f32[36,5,2,8,256]{4,3,2,1,0:T(8,128)S(1)} %get-tuple-element.101.mine, f32[36,5,2,8,256]{4,3,2,1,0:T(8,128)S(1)} %collective-permute-done.14.other, ...), custom_call_target="tpu_custom_call", output_to_operand_aliasing={{0}: (3, {}), {1}: (4, {})} | custom-call | tf_op jit(solution)/shard_map/cond/branch_1_fun/scale_level/pallas_call | solution.py:432
  138.6 0.0 collective-permute-done.13.other
  138.6 3.7 %scale_level.15 = (f32[36,2,64,256]{3,2,1,0:T(8,128)}, f32[36,3,64,256]{3,2,1,0:T(8,128)}) custom-call(f32[36]{0:T(128)S(1)} %get-tuple-element.78.scale, f32[36,5,2,8,256]{4,3,2,1,0:T(8,128)S(1)} %get-tuple-element.97.mine, f32[36,5,2,8,256]{4,3,2,1,0:T(8,128)S(1)} %collective-permute-done.13.other, ...), custom_call_target="tpu_custom_call", output_to_operand_aliasing={{0}: (3, {}), {1}: (4, {})} | custom-call | tf_op jit(solution)/shard_map/cond/branch_1_fun/scale_level/pallas_call | solution.py:432
  (17 shorter events, 0.0 us)
Async XLA Ops:
  2.1 18.8 %copy-start.12 = (s32[128,2]{0,1:T(2,128)S(1)}, s32[128,2]{0,1:T(2,128)}, u32[]{:S(2)}) copy-start(s32[128,2]{0,1:T(2,128)} %param.8) | copy-start | bytes 3076
  2.1 25.7 %copy-start.8 = (bf16[2,256,256]{2,1,0:T(8,128)(2,1)S(1)}, bf16[2,256,256]{2,1,0:T(8,128)(2,1)}, u32[]{:S(2)}) copy-start(bf16[2,256,256]{2,1,0:T(8,128)(2,1)} %constant.70.clone.refs_1_) | copy-start | bytes 786436
  12.3 42.7 %collective-permute-start.17 = (f32[2,480,256]{2,1,0:T(8,128)S(1)}, f32[2,480,256]{2,1,0:T(8,128)}, u32[]{:S(2)}, u32[]{:S(2)}) collective-permute-start(f32[2,480,256]{2,1,0:T(8,128)S(1)} %get-tuple-element.147), channel_id=1, source_target_pairs={{1,0},{2,1},{3,2},{4,3},{5,4},{6,5},{7,6},{8,7},{9,8},{10,9},{11,1... | collective-permute-start | bytes 2949128 | tf_op jit(solution)/shard_map/ppermute | solution.py:456
  18.9 36.0 %collective-permute-start.18 = (f32[2,480,256]{2,1,0:T(8,128)S(1)}, f32[2,480,256]{2,1,0:T(8,128)}, u32[]{:S(2)}, u32[]{:S(2)}) collective-permute-start(f32[2,480,256]{2,1,0:T(8,128)S(1)} %get-tuple-element.148), channel_id=1, source_target_pairs={{0,1},{1,2},{2,3},{3,4},{4,5},{5,6},{6,7},{7,8},{8,9},{9,10},{10,1... | collective-permute-start | bytes 2949128 | tf_op jit(solution)/shard_map/ppermute | solution.py:461
  26.7 26.7 %collective-permute-start.16 = (s32[80]{0:T(128)S(1)}, s32[80]{0:T(128)S(1)}, u32[]{:S(2)}, u32[]{:S(2)}) collective-permute-start(s32[80]{0:T(128)S(1)} %concatenate.7), channel_id=1, source_target_pairs={{0,64},{64,0},{1,65},{65,1},{2,66},{66,2},{3,67},{67,3},{4,68},{68... | collective-permute-start | bytes 968 | tf_op jit(solution)/shard_map/ppermute | solution.py:451
  55.2 49.1 %copy-start.5 = (f32[96,2,2,8,256]{4,3,2,1,0:T(8,128)S(1)}, f32[96,2,2,8,256]{4,3,2,1,0:T(8,128)}, u32[]{:S(2)}) copy-start(f32[96,2,2,8,256]{4,3,2,1,0:T(8,128)} %get-tuple-element.104.refs_3_) | copy-start | bytes 9437188 | tf_op jit(solution)/shard_map/cond
  55.2 49.1 %copy-start.9 = (f32[32,2,2,8,256]{4,3,2,1,0:T(8,128)S(1)}, f32[32,2,2,8,256]{4,3,2,1,0:T(8,128)}, u32[]{:S(2)}) copy-start(f32[32,2,2,8,256]{4,3,2,1,0:T(8,128)} %get-tuple-element.103.refs_2_) | copy-start | bytes 3145732 | tf_op jit(solution)/shard_map/cond
  55.2 43.2 %collective-permute-start.6 = (f32[36,5,2,8,256]{4,3,2,1,0:T(8,128)}, f32[36,5,2,8,256]{4,3,2,1,0:T(8,128)S(1)}, u32[]{:S(2)}, u32[]{:S(2)}) collective-permute-start(f32[36,5,2,8,256]{4,3,2,1,0:T(8,128)} %get-tuple-element.81), channel_id=1, source_target_pairs={{0,64},{64,0},{1,65},{65,1},{2,66},{66,2},{3,67},{67,3},{4,68},{68... | collective-permute-start | bytes 8847368 | tf_op jit(solution)/shard_map/cond/branch_1_fun/ppermute | solution.py:451
  55.4 34.9 %collective-permute-start.7 = (f32[2,608,256]{2,1,0:T(8,128)}, f32[2,608,256]{2,1,0:T(8,128)S(1)}, u32[]{:S(2)}, u32[]{:S(2)}) collective-permute-start(f32[2,608,256]{2,1,0:T(8,128)} %get-tuple-element.91), channel_id=1, source_target_pairs={{1,0},{2,1},{3,2},{4,3},{5,4},{6,5},{7,6},{8,7},{9,8},{10,9},{11,1... | collective-permute-start | bytes 3735560 | tf_op jit(solution)/shard_map/cond/branch_1_fun/ppermute | solution.py:456
  63.5 40.8 %collective-permute-start.10 = (f32[2,608,256]{2,1,0:T(8,128)}, f32[2,608,256]{2,1,0:T(8,128)S(1)}, u32[]{:S(2)}, u32[]{:S(2)}) collective-permute-start(f32[2,608,256]{2,1,0:T(8,128)} %get-tuple-element.94), channel_id=1, source_target_pairs={{0,1},{1,2},{2,3},{3,4},{4,5},{5,6},{6,7},{7,8},{8,9},{9,10},{10,1... | collective-permute-start | bytes 3735560 | tf_op jit(solution)/shard_map/cond/branch_1_fun/ppermute | solution.py:461
  65.4 47.5 %collective-permute-start.8 = (f32[2,408,256]{2,1,0:T(8,128)}, f32[2,408,256]{2,1,0:T(8,128)S(1)}, u32[]{:S(2)}, u32[]{:S(2)}) collective-permute-start(f32[2,408,256]{2,1,0:T(8,128)} %get-tuple-element.92), channel_id=1, source_target_pairs={{1,0},{2,1},{3,2},{4,3},{5,4},{6,5},{7,6},{8,7},{9,8},{10,9},{11,1... | collective-permute-start | bytes 2506760 | tf_op jit(solution)/shard_map/cond/branch_1_fun/ppermute | solution.py:456
  73.0 43.1 %collective-permute-start.11 = (f32[2,408,256]{2,1,0:T(8,128)}, f32[2,408,256]{2,1,0:T(8,128)S(1)}, u32[]{:S(2)}, u32[]{:S(2)}) collective-permute-start(f32[2,408,256]{2,1,0:T(8,128)} %get-tuple-element.95), channel_id=1, source_target_pairs={{0,1},{1,2},{2,3},{3,4},{4,5},{5,6},{6,7},{7,8},{8,9},{9,10},{10,1... | collective-permute-start | bytes 2506760 | tf_op jit(solution)/shard_map/cond/branch_1_fun/ppermute | solution.py:461
  90.2 34.8 %collective-permute-start.9 = (f32[2,168,256]{2,1,0:T(8,128)}, f32[2,168,256]{2,1,0:T(8,128)S(1)}, u32[]{:S(2)}, u32[]{:S(2)}) collective-permute-start(f32[2,168,256]{2,1,0:T(8,128)} %get-tuple-element.93), channel_id=1, source_target_pairs={{1,0},{2,1},{3,2},{4,3},{5,4},{6,5},{7,6},{8,7},{9,8},{10,9},{11,1... | collective-permute-start | bytes 1032200 | tf_op jit(solution)/shard_map/cond/branch_1_fun/ppermute | solution.py:456
  98.5 26.6 %collective-permute-start.12 = (f32[2,168,256]{2,1,0:T(8,128)}, f32[2,168,256]{2,1,0:T(8,128)S(1)}, u32[]{:S(2)}, u32[]{:S(2)}) collective-permute-start(f32[2,168,256]{2,1,0:T(8,128)} %get-tuple-element.96), channel_id=1, source_target_pairs={{0,1},{1,2},{2,3},{3,4},{4,5},{5,6},{6,7},{7,8},{8,9},{9,10},{10,1... | collective-permute-start | bytes 1032200 | tf_op jit(solution)/shard_map/cond/branch_1_fun/ppermute | solution.py:461
  104.3 11.8 %copy-start.6 = (f32[96,2,2,8,256]{4,3,2,1,0:T(8,128)S(1)}, f32[96,2,2,8,256]{4,3,2,1,0:T(8,128)}, u32[]{:S(2)}) copy-start(f32[96,2,2,8,256]{4,3,2,1,0:T(8,128)} %get-tuple-element.100.refs_3_) | copy-start | bytes 9437188 | tf_op jit(solution)/shard_map/cond
  104.3 11.7 %copy-start.11 = (f32[32,2,2,8,256]{4,3,2,1,0:T(8,128)S(1)}, f32[32,2,2,8,256]{4,3,2,1,0:T(8,128)}, u32[]{:S(2)}) copy-start(f32[32,2,2,8,256]{4,3,2,1,0:T(8,128)} %get-tuple-element.99.refs_2_) | copy-start | bytes 3145732 | tf_op jit(solution)/shard_map/cond
  110.9 20.3 %collective-permute-start.15 = (f32[36,5,2,8,256]{4,3,2,1,0:T(8,128)S(1)}, f32[36,5,2,8,256]{4,3,2,1,0:T(8,128)S(1)}, u32[]{:S(2)}, u32[]{:S(2)}) collective-permute-start(f32[36,5,2,8,256]{4,3,2,1,0:T(8,128)S(1)} %get-tuple-element.106), channel_id=1, source_target_pairs={{0,64},{64,0},{1,65},{65,1},{2,66},{66,2},{3,67},{67,3},{4,68},{68... | collective-permute-start | bytes 8847368 | tf_op jit(solution)/shard_map/cond/branch_1_fun/ppermute | solution.py:451
  116.0 9.0 %copy-start.7 = (f32[96,2,2,8,256]{4,3,2,1,0:T(8,128)S(1)}, f32[96,2,2,8,256]{4,3,2,1,0:T(8,128)}, u32[]{:S(2)}) copy-start(f32[96,2,2,8,256]{4,3,2,1,0:T(8,128)} %get-tuple-element.88.refs_3_) | copy-start | bytes 9437188 | tf_op jit(solution)/shard_map/cond
  116.0 9.0 %copy-start.10 = (f32[32,2,2,8,256]{4,3,2,1,0:T(8,128)S(1)}, f32[32,2,2,8,256]{4,3,2,1,0:T(8,128)}, u32[]{:S(2)}) copy-start(f32[32,2,2,8,256]{4,3,2,1,0:T(8,128)} %get-tuple-element.87.refs_2_) | copy-start | bytes 3145732 | tf_op jit(solution)/shard_map/cond
  122.4 12.5 %collective-permute-start.14 = (f32[36,5,2,8,256]{4,3,2,1,0:T(8,128)S(1)}, f32[36,5,2,8,256]{4,3,2,1,0:T(8,128)S(1)}, u32[]{:S(2)}, u32[]{:S(2)}) collective-permute-start(f32[36,5,2,8,256]{4,3,2,1,0:T(8,128)S(1)} %get-tuple-element.102), channel_id=1, source_target_pairs={{0,64},{64,0},{1,65},{65,1},{2,66},{66,2},{3,67},{67,3},{4,68},{68... | collective-permute-start | bytes 8847368 | tf_op jit(solution)/shard_map/cond/branch_1_fun/ppermute | solution.py:451
  131.0 7.6 %collective-permute-start.13 = (f32[36,5,2,8,256]{4,3,2,1,0:T(8,128)S(1)}, f32[36,5,2,8,256]{4,3,2,1,0:T(8,128)S(1)}, u32[]{:S(2)}, u32[]{:S(2)}) collective-permute-start(f32[36,5,2,8,256]{4,3,2,1,0:T(8,128)S(1)} %get-tuple-element.98), channel_id=1, source_target_pairs={{0,64},{64,0},{1,65},{65,1},{2,66},{66,2},{3,67},{67,3},{4,68},{68... | collective-permute-start | bytes 8847368 | tf_op jit(solution)/shard_map/cond/branch_1_fun/ppermute | solution.py:451

commit v4 on v3

v4 whole, which is shorter than its diff:
```python
import functools

import jax
import jax.numpy as jnp
import numpy as np
from jax import lax
from jax.experimental import pallas as pl
from jax.experimental.pallas import tpu as pltpu
from jax.sharding import PartitionSpec as P

PHASES = 72
HALF = PHASES // 2
RAD = 8
MAXS = 16
HALO = RAD + MAXS
ROWS = 64
WIDTH = 256
SNAPS = 128
EXT = ROWS + 2 * HALO
GROUP = 8
CHUNK = 128
GAP = 16
MIB = 1024 * 1024
FIRST_CUTS = (640,)
REST_CUTS = (512, 984)
FULL_CUTS = (3072 + 64,)
GROUPS = SNAPS // 8
F32 = jnp.float32
BF16 = jnp.bfloat16
I32 = jnp.int32


def taps():
    steps = np.arange(2 * RAD + 1, dtype=np.float64) - RAD
    sigma = RAD / 2.0
    values = np.exp(-steps * steps / (2.0 * sigma * sigma))
    return values / values.sum()


def split_const(values):
    high = values.astype(BF16)
    low = (values - high.astype(np.float64)).astype(BF16)
    return high, low


def column_constant():
    weight = taps()
    source = np.arange(WIDTH)[:, None]
    target = np.arange(WIDTH)[None, :]
    distance = source - target
    band = np.where(np.abs(distance) <= RAD, weight[np.clip(distance + RAD, 0, 2 * RAD)], 0.0)
    high, low = split_const(band)
    return np.concatenate([high, low, high], axis=0)


def row_constant():
    weight = taps()
    target = np.arange(EXT)[None, :, None] - HALO
    source = np.arange(ROWS)[None, None, :]
    shift = np.arange(-MAXS, MAXS + 1)[:, None, None]
    distance = source - shift - target
    band = np.where(np.abs(distance) <= RAD, weight[np.clip(distance + RAD, 0, 2 * RAD)], 0.0)
    seen = source - shift
    kinds = []
    for kind in range(3):
        keep = np.ones_like(seen, dtype=bool)
        if kind == 0:
            keep = seen >= 0
        if kind == 2:
            keep = seen < ROWS
        high, low = split_const(np.where(keep, band, 0.0))
        kinds.append(np.concatenate([high, low, high], axis=2))
    return np.stack(kinds)


def level_rows(need, level):
    return jnp.clip(need - 8 * level, 0, 8)


def needs(dy):
    return jnp.clip(RAD + dy, 0, HALO), jnp.clip(RAD - dy, 0, HALO)


def next_start(end):
    return (end & -8) + 16


def split(value):
    high = value.astype(BF16)
    return high, (value - high.astype(F32)).astype(BF16)


def smooth_kernel(part, cuts, meta, plan, *refs):
    pieces = len(cuts)
    vel, colop, rowop, refs = *refs[:3], refs[3:]
    y_refs, refs = refs[:4], refs[4:]
    out_up, out_dn = refs[:pieces], refs[pieces:2 * pieces]
    pos_ref, plan_ref, refs = *refs[2 * pieces:2 * pieces + 2], refs[2 * pieces + 2:]
    vel_buf, oper_buf, col_buf, refs = *refs[:3], refs[3:]
    y_bufs, refs = refs[:4], refs[4:]
    xs, stack, up, dn, cursor, load_sem, store_sem, sem = refs
    row = lax.broadcasted_iota(I32, (8, WIDTH), 0)
    lane = lax.broadcasted_iota(I32, (1, WIDTH), 1)
    dot = functools.partial(jnp.dot, preferred_element_type=F32)

    def load(g):
        rows = pl.ds(GROUP * g, GROUP)
        return pltpu.make_async_copy(vel.at[rows], vel_buf.at[rows], load_sem.at[g])

    def store(g, level):
        rows = pl.ds(GROUP * g, GROUP)
        return pltpu.make_async_copy(y_bufs[level].at[rows], y_refs[level].at[rows], store_sem.at[g, level])

    def loop(low, high, body):
        lax.fori_loop(low, high, lambda g, carry: (body(g), carry)[1], 0)

    def ends(sums):
        starts, stops = [], []
        for side in range(2):
            start = I32(0)
            for level in range(3):
                starts.append(start)
                start = next_start(start + sums[3 * side + level])
                stops.append(start)
        return starts, stops

    def count_group(g, sums):
        for b in range(GROUP):
            sums = list(sums)
            for side, need in enumerate(needs(meta[GROUP * g + b])):
                for level in range(3):
                    sums[3 * side + level] += level_rows(need, level)
        return tuple(sums)

    tables = [pltpu.make_async_copy(colop, col_buf, sem.at[0]),
              pltpu.make_async_copy(rowop.at[meta[3 * SNAPS]], oper_buf, sem.at[1])]
    zero = (I32(0),) * 6
    if part == 0:
        load(0).start()
        for copy in tables:
            copy.start()
        for g in range(1, 4):
            load(g).start()

        def add_group(g, carry):
            sums, taken, count, going = carry
            sums = count_group(g, sums)
            stops = ends(sums)[1]
            going = going & (jnp.maximum(stops[2], stops[5]) <= cuts[-1]).astype(I32)
            taken = tuple(jnp.where(going > 0, new, old) for new, old in zip(sums, taken))
            return sums, taken, count + going, going

        sums, taken, count, _ = lax.fori_loop(0, GROUPS, add_group, (zero, zero, I32(0), I32(1)))
        begin, end = I32(0), count
        starts = ends(taken)[0]
        rest_starts, rest_stops = ends([whole - some for whole, some in zip(sums, taken)])
        over = I32(0)
        for side in range(2):
            for level in range(3):
                limit = level_cuts(REST_CUTS, level)[-1]
                over = jnp.maximum(over, rest_stops[3 * side + level] - limit)
        for k in range(8):
            plan_ref[k] = rest_starts[k] if k < 6 else count
            plan_ref[8 + k] = over
        loop(4, end, lambda g: load(g).start())
    elif part == 1:
        begin, end = plan[6], I32(GROUPS)
        loop(begin, end, lambda g: load(g).start())
        for copy in tables:
            copy.start()
        starts = [plan[k] for k in range(6)]
    else:
        begin, end = I32(0), I32(GROUPS)
        loop(begin, end, lambda g: load(g).start())
        for copy in tables:
            copy.start()
        starts = ends(lax.fori_loop(0, GROUPS, count_group, zero))[0]
    if part:
        for k in range(16):
            plan_ref[k] = I32(GROUPS)
    for k in range(6):
        cursor[k] = starts[k]
    for copy in tables:
        copy.wait()

    def group(g):
        load(g).wait()
        for b in range(GROUP):
            n = GROUP * g + b
            dx = meta[SNAPS + n]
            rolled = pltpu.roll(vel_buf[n].reshape(2 * ROWS, WIDTH), (WIDTH - dx) & (WIDTH - 1), 1)
            moved = lane + dx
            high, low = split(jnp.where((moved >= 0) & (moved < WIDTH), rolled, 0.0))
            rows = slice(2 * ROWS * b, 2 * ROWS * (b + 1))
            xs[rows, 0:WIDTH] = high
            xs[rows, WIDTH:2 * WIDTH] = high
            xs[rows, 2 * WIDTH:3 * WIDTH] = low
        high, low = split(dot(xs[...], col_buf[...]))
        for b in range(GROUP):
            for comp in range(2):
                rows = slice(ROWS * (2 * b + comp), ROWS * (2 * b + comp + 1))
                stack[b, comp, 0:ROWS] = high[rows]
                stack[b, comp, ROWS:2 * ROWS] = high[rows]
                stack[b, comp, 2 * ROWS:3 * ROWS] = low[rows]
        for b in range(GROUP):
            n = GROUP * g + b
            oper = oper_buf[meta[n] + MAXS]
            ext = [dot(oper, stack[b, comp]) for comp in range(2)]
            for level in range(4):
                for comp in range(2):
                    top = HALO + 8 * level
                    bottom = HALO + ROWS - 8 - 8 * level
                    y_bufs[level][n, 0, comp] = ext[comp][top:top + 8]
                    y_bufs[level][n, 1, comp] = ext[comp][bottom:bottom + 8]
            for side, need in enumerate(needs(meta[n])):
                buffer = (up, dn)[side]
                for level in range(3):
                    slot = 3 * side + level
                    have = level_rows(need, level)
                    here = cursor[slot]
                    cursor[slot] = here + have
                    pos = jnp.minimum(here, cuts[-1] - 16)
                    pos_ref[6 * n + slot] = pos
                    skew = pos & 7
                    base = pl.multiple_of(pos - skew, 8)
                    source = 16 - 8 * level if side == 0 else HALO + ROWS + 8 * level
                    turn = (skew + have) & 7 if side == 0 else skew
                    for comp in range(2):
                        tile = pltpu.roll(ext[comp][source:source + 8], turn, 0)
                        old = buffer[comp, pl.ds(base, 8)]
                        buffer[comp, pl.ds(base, 8)] = jnp.where(row < skew, old, tile)
                        buffer[comp, pl.ds(base + 8, 8)] = tile
        for level in range(4):
            store(g, level).start()

    loop(begin, end, group)
    copies = []
    low = 0
    for piece, high in enumerate(cuts):
        for side in range(2):
            copies.append(pltpu.make_async_copy(
                (up, dn)[side].at[:, low:high], (out_up, out_dn)[side][piece], sem.at[2 + len(copies)]))
        low = high
    for copy in copies:
        copy.start()
    if part == 0:
        for g in range(4):
            pl.when(g >= end)(load(g).wait)

    def stored(g):
        for level in range(4):
            store(g, level).wait()

    loop(begin, end, stored)
    for copy in copies:
        copy.wait()


def smooth_part(part, meta, plan, velocity, colop, rowop, cuts):
    pieces = len(cuts)
    sizes = [high - low for low, high in zip((0,) + cuts[:-1], cuts)]
    any_space = pl.BlockSpec(memory_space=pl.ANY)
    smem = pl.BlockSpec(memory_space=pltpu.SMEM)
    piece_shapes = [jax.ShapeDtypeStruct((2, size, WIDTH), F32) for size in sizes]
    strip = jax.ShapeDtypeStruct((SNAPS, 2, 2, 8, WIDTH), F32)
    room = cuts[-1] + GAP
    out = pl.pallas_call(
        functools.partial(smooth_kernel, part, cuts),
        in_specs=[smem] * 2 + [any_space] * 3,
        out_specs=[any_space] * (4 + 2 * pieces) + [smem, smem],
        scratch_shapes=[
            pltpu.VMEM((SNAPS, 2, ROWS, WIDTH), F32),
            pltpu.VMEM((2 * MAXS + 1, EXT, 3 * ROWS), BF16),
            pltpu.VMEM((3 * WIDTH, WIDTH), BF16),
        ] + [pltpu.VMEM((SNAPS, 2, 2, 8, WIDTH), F32)] * 4 + [
            pltpu.VMEM((GROUP * 2 * ROWS, 3 * WIDTH), BF16),
            pltpu.VMEM((GROUP, 2, 3 * ROWS, WIDTH), BF16),
            pltpu.VMEM((2, room, WIDTH), F32),
            pltpu.VMEM((2, room, WIDTH), F32),
            pltpu.SMEM((8,), I32),
            pltpu.SemaphoreType.DMA((GROUPS,)),
            pltpu.SemaphoreType.DMA((GROUPS, 4)),
            pltpu.SemaphoreType.DMA((2 + 2 * pieces,)),
        ],
        out_shape=[strip] * 4 + piece_shapes * 2
        + [jax.ShapeDtypeStruct((SNAPS * 6,), I32), jax.ShapeDtypeStruct((16,), I32)],
        compiler_params=pltpu.CompilerParams(vmem_limit_bytes=56 * MIB),
        name="smooth_part",
    )(meta, plan, velocity, colop, rowop)
    return out[:4], out[4:4 + pieces], out[4 + pieces:4 + 2 * pieces], out[-2], out[-1]


def finish_kernel(level, cuts, meta, plan, *refs):
    parts = len(cuts)
    pos_refs, strips, refs = refs[:parts], refs[parts:2 * parts], refs[2 * parts:]
    pieces = []
    for k in range(parts):
        many = len(cuts[k])
        pieces.append((refs[:many], refs[many:2 * many]))
        refs = refs[2 * many:]
    mine, theirs, acc, y_buf, *refs = refs
    buffers, (y_sem, sem) = refs[:-2], refs[-2:]
    middle = plan[6] if parts == 2 else I32(GROUPS)
    ranges = [(I32(0), middle), (middle, I32(GROUPS))][:parts]

    def loop(low, high, body):
        lax.fori_loop(low, high, lambda g, carry: (body(g), carry)[1], 0)

    def load(k, g):
        rows = pl.ds(GROUP * g, GROUP)
        return pltpu.make_async_copy(strips[k].at[rows], y_buf.at[rows], y_sem.at[g])

    packs = [[] for _ in range(parts)]
    total = 0
    for k in range(parts):
        low = 0
        first, last = ranges[k]
        for piece, high in enumerate(cuts[k]):
            for side in range(2):
                slot = 3 * side + level
                begin = pos_refs[k][6 * GROUP * jnp.minimum(first, GROUPS - 1) + slot]
                end = pos_refs[k][6 * (GROUP * jnp.maximum(last, 1) - 1) + slot] + 16
                for row_at in range(low, high, CHUNK):
                    stop = min(row_at + CHUNK, high)
                    copy = pltpu.make_async_copy(
                        pieces[k][side][piece].at[:, row_at - low:stop - low],
                        buffers[2 * k + side].at[:, row_at:stop], sem.at[total])
                    total += 1
                    packs[k].append((copy, (first < last) & (begin < stop) & (end > row_at)))
            low = high
    for k in range(parts):
        for copy, needed in packs[k]:
            pl.when(needed)(copy.start)
        loop(*ranges[k], lambda g, k=k: load(k, g).start())
    acc[...] = jnp.zeros_like(acc)
    row = lax.broadcasted_iota(I32, (8, WIDTH), 0)

    def one(n, k):
        phase = meta[2 * SNAPS + n]
        for place in range(2):
            fields = [y_buf[n, place, comp] for comp in range(2)]
            if cuts[k]:
                side = 1 - place
                have = level_rows(needs(meta[n])[side], level)
                pos = pos_refs[k][6 * n + 3 * side + level]
                skew = pos & 7
                base = pl.multiple_of(pos - skew, 8)
                turn = skew if place == 0 else (skew + have) & 7
                keep = row < have if place == 0 else row >= 8 - have
                for comp in range(2):
                    lower = buffers[2 * k + side][comp, pl.ds(base, 8)]
                    upper = buffers[2 * k + side][comp, pl.ds(base + 8, 8)]
                    tile = pltpu.roll(jnp.where(row >= skew, lower, upper), (8 - turn) & 7, 0)
                    fields[comp] += jnp.where(keep, tile, 0.0)
            u, v = fields
            for at_field, field in enumerate((u, v, u * u, v * v, u * v)):
                acc[phase, at_field, place] += field

    def group(g, k):
        load(k, g).wait()
        for b in range(GROUP):
            one(GROUP * g + b, k)

    for k in range(parts):
        for copy, needed in packs[k]:
            pl.when(needed)(copy.wait)
        loop(*ranges[k], lambda g, k=k: group(g, k))
    stores = [pltpu.make_async_copy(acc.at[HALF:PHASES], theirs, y_sem.at[0]),
              pltpu.make_async_copy(acc.at[0:HALF], mine, y_sem.at[1])]
    for copy in stores:
        copy.start()
    for copy in stores:
        copy.wait()


def finish_level(level, meta, plan, parts):
    any_space = pl.BlockSpec(memory_space=pl.ANY)
    smem = pl.BlockSpec(memory_space=pltpu.SMEM)
    shape = jax.ShapeDtypeStruct((HALF, 5, 2, 8, WIDTH), F32)
    cuts = [level_cuts(part[2], level) if level < 3 else () for part in parts]
    packs = [piece for part, some in zip(parts, cuts) for side in part[3:5] for piece in side[:len(some)]]
    chunks = sum(2 * (-(-(high - low) // CHUNK)) for some in cuts for low, high in zip((0,) + some[:-1], some))
    rooms = [some[-1] + GAP for some in cuts if some]
    return pl.pallas_call(
        functools.partial(finish_kernel, level, cuts),
        in_specs=[smem] * (2 + len(parts)) + [any_space] * (len(parts) + len(packs)),
        out_specs=[any_space] * 2,
        out_shape=[shape] * 2,
        scratch_shapes=[
            pltpu.VMEM((PHASES, 5, 2, 8, WIDTH), F32),
            pltpu.VMEM((SNAPS, 2, 2, 8, WIDTH), F32),
        ] + [pltpu.VMEM((2, room, WIDTH), F32) for room in rooms for _ in range(2)] + [
            pltpu.SemaphoreType.DMA((GROUPS,)),
            pltpu.SemaphoreType.DMA((max(chunks, 1),)),
        ],
        compiler_params=pltpu.CompilerParams(vmem_limit_bytes=12 * MIB + 16 * WIDTH * sum(rooms)),
        name="finish_level",
    )(meta, plan, *[part[0] for part in parts], *[part[1][level] for part in parts], *packs)


def scale_kernel(level, block, scale, mine, other, *refs):
    mean, moment, a_buf, b_buf, mean_buf, moment_buf, sem = refs[-7:]
    count = HALF // block
    loads, stores = [], []
    for k in range(count):
        part = slice(block * k, block * (k + 1))
        loads.append([pltpu.make_async_copy(mine.at[part], a_buf.at[part], sem.at[2 * k]),
                      pltpu.make_async_copy(other.at[part], b_buf.at[part], sem.at[2 * k + 1])])
        group = []
        for place in range(2):
            rows = slice(8 * level, 8 * level + 8) if place == 0 else slice(ROWS - 8 - 8 * level, ROWS - 8 * level)
            for which, (buf, out) in enumerate(((mean_buf, mean), (moment_buf, moment))):
                group.append(pltpu.make_async_copy(
                    buf.at[place, part], out.at[part, :, rows], sem.at[2 * count + 4 * k + 2 * place + which]))
        stores.append(group)
    for copies in loads:
        for copy in copies:
            copy.start()
    for k in range(count):
        for copy in loads[k]:
            copy.wait()

        def one(p, carry):
            factor = scale[p]
            for place in range(2):
                total = (a_buf[p, :, place] + b_buf[p, :, place]) * factor
                mean_buf[place, p] = total[0:2]
                moment_buf[place, p] = total[2:5]
            return carry

        lax.fori_loop(block * k, block * (k + 1), one, 0)
        for copy in stores[k]:
            copy.start()
    for copies in stores:
        for copy in copies:
            copy.wait()


def scale_level(level, scale, mine, other, before):
    block = 18
    count = HALF // block
    any_space = pl.BlockSpec(memory_space=pl.ANY)
    return pl.pallas_call(
        functools.partial(scale_kernel, level, block),
        in_specs=[pl.BlockSpec(memory_space=pltpu.SMEM)] + [any_space] * (2 + len(before)),
        out_specs=[pl.BlockSpec(memory_space=pltpu.HBM)] * 2,
        out_shape=[jax.ShapeDtypeStruct((HALF, 2, ROWS, WIDTH), F32), jax.ShapeDtypeStruct((HALF, 3, ROWS, WIDTH), F32)],
        scratch_shapes=[
            pltpu.VMEM((HALF, 5, 2, 8, WIDTH), F32),
            pltpu.VMEM((HALF, 5, 2, 8, WIDTH), F32),
            pltpu.VMEM((2, HALF, 2, 8, WIDTH), F32),
            pltpu.VMEM((2, HALF, 3, 8, WIDTH), F32),
            pltpu.SemaphoreType.DMA((6 * count,)),
        ],
        input_output_aliases={3: 0, 4: 1} if before else {},
        compiler_params=pltpu.CompilerParams(vmem_limit_bytes=10 * MIB),
        name="scale_level",
    )(scale, mine, other, *before)


def to_partner(value):
    return lax.ppermute(value, "snap", [(0, 1), (1, 0)])


def to_above(value):
    size = lax.axis_size("tile")
    return lax.ppermute(value, "tile", [(i + 1, i) for i in range(size - 1)])


def to_below(value):
    size = lax.axis_size("tile")
    return lax.ppermute(value, "tile", [(i, i + 1) for i in range(size - 1)])


def level_cuts(cuts, level):
    return cuts[:level + 1]


def send(up_pieces, dn_pieces):
    from_below = [to_above(piece) for piece in up_pieces]
    from_above = [to_below(piece) for piece in dn_pieces]
    return from_below, from_above


def per_device(velocity, offsets, phase):
    snap = lax.axis_index("snap")
    tile = lax.axis_index("tile")
    dy, dx = offsets[:, 0].astype(I32), offsets[:, 1].astype(I32)
    turned = lax.rem(phase.astype(I32) + PHASES - HALF * snap, PHASES)
    kind = jnp.where(tile == 0, 0, jnp.where(tile == lax.axis_size("tile") - 1, 2, 1)).astype(I32)
    meta = jnp.concatenate([dy, dx, turned, kind[None]])
    colop = jnp.asarray(column_constant())
    rowop = jnp.asarray(row_constant())
    onehot = (turned[:, None] == jnp.arange(PHASES, dtype=I32)[None, :]).astype(I32)
    own = jnp.sum(onehot, axis=0)

    smooth = functools.partial(smooth_part, velocity=velocity, colop=colop, rowop=rowop)

    def full(scale, *_):
        strips, up, dn, positions, plan = smooth(2, meta, jnp.zeros((16,), I32), cuts=FULL_CUTS)
        below, above = send(up, dn)
        before = ()
        for level in (3, 0, 1, 2):
            mine, theirs = finish_level(level, meta, plan, [(positions, strips, FULL_CUTS, below, above)])
            before = scale_level(level, scale, mine, to_partner(theirs), before)
        return tuple(before)

    def fast(scale, mine, theirs, plan, strips_a, pos_a, below_a, above_a, strips_b, pos_b, up_b, dn_b):
        rest = (up_b[1], dn_b[1])
        below_b, above_b = send(up_b[:1], dn_b[:1])
        other = to_partner(theirs)
        more = send(rest[0:1], rest[1:2])
        before = scale_level(3, scale, mine, other, ())
        here, before = lax.optimization_barrier((meta, tuple(before)))
        parts = [(pos_a, strips_a, FIRST_CUTS, below_a, above_a),
                 (pos_b, strips_b, REST_CUTS, below_b + more[0], above_b + more[1])]
        totals = [finish_level(level, here, plan, parts) for level in range(3)]
        for level, (mine, theirs) in enumerate(totals):
            before = scale_level(level, scale, mine, to_partner(theirs), before)
        return tuple(before)

    strips_a, up_a, dn_a, pos_a, plan = smooth(0, meta, jnp.zeros((16,), I32), cuts=FIRST_CUTS)
    below_a, above_a = send(up_a, dn_a)
    message = jnp.concatenate([own, plan[8:]])
    reply = to_partner(message)
    strips_b, up_b, dn_b, pos_b, _ = smooth(1, meta, plan, cuts=REST_CUTS)
    mine, theirs = finish_level(3, meta, plan, [(pos_a, strips_a, (), (), ()), (pos_b, strips_b, (), (), ())])
    scale = 1.0 / jnp.maximum((message[:HALF] + reply[HALF:PHASES]).astype(F32), 1.0)
    over = jnp.maximum(message[PHASES], reply[PHASES])
    return lax.cond(over <= 0, fast, full, scale, mine, theirs,
                    plan, strips_a, pos_a, below_a, above_a, strips_b, pos_b, up_b, dn_b)


def solution(mesh):
    in_specs = (P("snap", None, "tile", None), P("snap", None), P("snap"))
    out_specs = (P("snap", None, "tile", None), P("snap", None, "tile", None))
    return jax.shard_map(
        per_device, mesh=mesh, in_specs=in_specs, out_specs=out_specs, check_vma=False
    )
```

time: 143 us -> 143 us (level)
  starting transfers between devices: 44.4 us -> 34.3 us
  waiting for transfers between devices: 18.5 us -> 28.6 us
  local copies, waits for them, and re-layouts: 0.8 us -> 4.71 us
  between operations: 5.41 us -> 2.12 us
  other arithmetic: 3.45 us -> 1.48 us
    ppermute x4 -> x3, waiting for transfers between devices: 3.14 us -> 15.8 us  [to_below(): return lax.ppermute(value, 'tile', [(i, i + 1) for i in range(size - 1)])]
    ppermute x4 -> x3, starting transfers between devices: 30.6 us -> 19.7 us  [to_above(): return lax.ppermute(value, 'tile', [(i + 1, i) for i in range(size - 1)])]
    ppermute x5, starting transfers between devices: 6.11 us -> 8.91 us  [to_partner(): return lax.ppermute(value, 'snap', [(0, 1), (1, 0)])]
    ppermute x4 -> x3, waiting for transfers between devices: 15.3 us -> 12.8 us  [to_above(): return lax.ppermute(value, 'tile', [(i + 1, i) for i in range(size - 1)])]
    reduce_max x3 -> x0, other arithmetic: 2.19 us -> none  [the longest x2 1.49 us: per_device(): jnp.max(jnp.concatenate([excess(dy, 0, FIRST_CUTS, FIRST), excess(dy, FIR...]
    unnamed x4 -> x6, local copies, waits for them, and re-layouts: 0.01 us -> 2.19 us
    ppermute x4 -> x3, starting transfers between devices: 7.68 us -> 5.76 us  [to_below(): return lax.ppermute(value, 'tile', [(i, i + 1) for i in range(size - 1)])]
    pallas_call x5 -> x6, Pallas kernels: 54.6 us -> 55.8 us  [the longest x2 35.5 us: smooth_part(): pl.pallas_call(functools.partial(smooth_kernel, part, cuts), in_specs=[sm...]
  transfers between devices with their start and end apart: 13 -> 11, of which waited for: 2 -> 4; matrix products, arithmetic and copies ran while one was open for 2% -> 1% of each run, Pallas kernels for 39% -> 36%
where the time goes in v4:
time: 143 us; the launch traced here: 142 us
  Pallas kernels  70.8 us (50%)
  starting transfers between devices  34.3 us (24%)
  waiting for transfers between devices  28.6 us (20%)
  local copies, waits for them, and re-layouts  4.71 us (3%)
  between operations  2.12 us (1%)
  other arithmetic  1.48 us (1%)
    pallas_call x2, Pallas kernels, smooth_part(): pl.pallas_call(functools.partial(smooth_kernel, part, cuts), in_specs=[sm...  35.5 us
    pallas_call x4, Pallas kernels, finish_level(): pl.pallas_call(functools.partial(finish_kernel, level, cuts), in_specs=[s...  20.2 us
    ppermute x3, starting transfers between devices, to_above(): return lax.ppermute(value, 'tile', [(i + 1, i) for i in range(size - 1)])  19.7 us
    ppermute x3, waiting for transfers between devices, to_below(): return lax.ppermute(value, 'tile', [(i, i + 1) for i in range(size - 1)])  15.8 us
    pallas_call x4, Pallas kernels, scale_level(): pl.pallas_call(functools.partial(scale_kernel, level, block), in_specs=[p...  15 us
    ppermute x3, waiting for transfers between devices, to_above(): return lax.ppermute(value, 'tile', [(i + 1, i) for i in range(size - 1)])  12.8 us
    ppermute x5, starting transfers between devices, to_partner(): return lax.ppermute(value, 'snap', [(0, 1), (1, 0)])  8.91 us
    ppermute x3, starting transfers between devices, to_below(): return lax.ppermute(value, 'tile', [(i, i + 1) for i in range(size - 1)])  5.76 us
  transfers between devices with their start and end apart: 11, of which 4 were waited for; matrix products, arithmetic and copies ran while one was open for 1% of the time, Pallas kernels for 36%

profile of v4, /device:TPU:97, one launch (start us, length us, event | category | flops | bytes accessed | tf_op | source)
XLA Modules:
  0.0 142.2 jit_solution(7017876276309879781)
XLA Ops:
  0.6 0.8 slice_bitcast_fusion.1
  1.4 0.7 subtract_remainder_fusion
  2.1 0.5 broadcast_6_plan.2.plan
  2.6 15.6 %smooth_part.4 = (f32[128,2,2,8,256]{4,3,2,1,0:T(8,128)}, f32[128,2,2,8,256]{4,3,2,1,0:T(8,128)}, f32[128,2,2,8,256]{4,3,2,1,0:T(8,128)}, f32[128,2,2,8,256]{4,3...) custom-call(s32[385]{0:T(512)S(1)} %pad_add_fusion.meta, ...), custom_call_target="tpu_custom_call" | custom-call | tf_op jit(solution)/shard_map/smooth_part/pallas_call | solution.py:267
  18.2 6.7 %collective-permute-start.15 = (f32[2,640,256]{2,1,0:T(8,128)}, f32[2,640,256]{2,1,0:T(8,128)S(1)}, u32[]{:S(2)}, u32[]{:S(2)}) collective-permute-start(f32[2,640,256]{2,1,0:T(8,128)} %get-tuple-element.143), channel_id=1, source_target_pairs={{1,0},{2,1},{3,2},{4,3},{5,4},{6,5},{7,6},{8,7},{9,8},{10,9},{11,1... | collective-permute-start | bytes 3932168 | tf_op jit(solution)/shard_map/ppermute | solution.py:467
  24.9 1.9 %collective-permute-start.16 = (f32[2,640,256]{2,1,0:T(8,128)}, f32[2,640,256]{2,1,0:T(8,128)S(1)}, u32[]{:S(2)}, u32[]{:S(2)}) collective-permute-start(f32[2,640,256]{2,1,0:T(8,128)} %get-tuple-element.144), channel_id=1, source_target_pairs={{0,1},{1,2},{2,3},{3,4},{4,5},{5,6},{6,7},{7,8},{8,9},{9,10},{10,1... | collective-permute-start | bytes 3932168 | tf_op jit(solution)/shard_map/ppermute | solution.py:472
  26.8 0.1 slice.25
  26.9 0.1 convert_reduce_fusion
  27.0 0.1 pad_add_fusion.1
  27.0 2.2 %collective-permute-start.14 = (s32[80]{0:T(128)S(1)}, s32[80]{0:T(128)S(1)}, u32[]{:S(2)}, u32[]{:S(2)}) collective-permute-start(s32[80]{0:T(128)S(1)} %pad_add_fusion.1), channel_id=1, source_target_pairs={{0,64},{64,0},{1,65},{65,1},{2,66},{66,2},{3,67},{67,3},{4,68},{68... | collective-permute-start | bytes 968 | tf_op jit(solution)/shard_map/ppermute | solution.py:462
  29.2 0.6 slice.24
  29.8 20.0 %smooth_part.5 = (f32[128,2,2,8,256]{4,3,2,1,0:T(8,128)}, f32[128,2,2,8,256]{4,3,2,1,0:T(8,128)}, f32[128,2,2,8,256]{4,3,2,1,0:T(8,128)}, f32[128,2,2,8,256]{4,3...) custom-call(s32[385]{0:T(512)S(1)} %pad_add_fusion.meta, ...), custom_call_target="tpu_custom_call" | custom-call | tf_op jit(solution)/shard_map/smooth_part/pallas_call | solution.py:267
  49.8 0.0 copy-done.1
  49.8 0.0 copy-start.2
  49.8 2.2 %copy-done.2 = f32[128,2,2,8,256]{4,3,2,1,0:T(8,128)S(1)} copy-done((f32[128,2,2,8,256]{4,3,2,1,0:T(8,128)S(1)}, f32[128,2,2,8,256]{4,3,2,1,0:T(8,128)}, u32[]{:S(2)}) %copy-start.2) | copy-done | bytes 4194328
  52.0 5.1 %finish_level.15 = (f32[36,5,2,8,256]{4,3,2,1,0:T(8,128)}, f32[36,5,2,8,256]{4,3,2,1,0:T(8,128)}) custom-call(s32[385]{0:T(512)S(1)} %pad_add_fusion.meta, s32[16]{0:T(128)S(1)} %get-tuple-element.130.plan, s32[768]{0:T(1024)S(1)} %get-tuple-element.131.refs_0_, s32[768]{0:T(1024)S(1)} %get-tuple-element.132.refs_1_, f32[128,2,2,8,256]{4,3,2,1,0:T(8,128)S(1)} %copy-done.1, ...), custom_call_target="tpu_custom_call" | custom-call | tf_op jit(solution)/shard_map/finish_level/pallas_call | solution.py:384
  57.1 0.0 collective-permute-done.14
  57.1 0.6 slice.26
  58.9 0.6 maximum_divide_fusion
  59.5 0.0 collective-permute-done.15
  59.5 0.0 collective-permute-done.16
  59.5 82.4 %conditional.1 = ((f32[36,2,64,256]{3,2,1,0:T(8,128)}, f32[36,3,64,256]{3,2,1,0:T(8,128)})) conditional(s32[]{:T(128)} %bitcast.3, (s32[385]{0:T(512)S(1)}, f32[128,2,64,256]{3,2,1,0:T(8,128)}, bf16[768,256]{1,0:T(8,128)(2,1)S(1)}, bf16[3,33,112,192]{3,2,1,0:T(8,128)(2,1)}, f32[36]{0:T(128)}) %tuple.25, (f32[36,5,2,8,256]{4,3,2,1,0:T(8,128)}, ...), branch_computations={%region_1.2_spmd, %region_2.3_spmd} | conditional | bytes 189306624 | solution.py:530
  59.5 2.8 %collective-permute-start.6 = (f32[36,5,2,8,256]{4,3,2,1,0:T(8,128)}, f32[36,5,2,8,256]{4,3,2,1,0:T(8,128)S(1)}, u32[]{:S(2)}, u32[]{:S(2)}) collective-permute-start(f32[36,5,2,8,256]{4,3,2,1,0:T(8,128)} %get-tuple-element.78), channel_id=1, source_target_pairs={{0,64},{64,0},{1,65},{65,1},{2,66},{66,2},{3,67},{67,3},{4,68},{68... | collective-permute-start | bytes 8847368 | tf_op jit(solution)/shard_map/cond/branch_1_fun/ppermute | solution.py:462
  62.4 5.4 %collective-permute-start.7 = (f32[2,512,256]{2,1,0:T(8,128)}, f32[2,512,256]{2,1,0:T(8,128)S(1)}, u32[]{:S(2)}, u32[]{:S(2)}) collective-permute-start(f32[2,512,256]{2,1,0:T(8,128)} %get-tuple-element.89), channel_id=1, source_target_pairs={{1,0},{2,1},{3,2},{4,3},{5,4},{6,5},{7,6},{8,7},{9,8},{10,9},{11,1... | collective-permute-start | bytes 3145736 | tf_op jit(solution)/shard_map/cond/branch_1_fun/ppermute | solution.py:467
  67.8 1.9 %collective-permute-start.9 = (f32[2,512,256]{2,1,0:T(8,128)}, f32[2,512,256]{2,1,0:T(8,128)S(1)}, u32[]{:S(2)}, u32[]{:S(2)}) collective-permute-start(f32[2,512,256]{2,1,0:T(8,128)} %get-tuple-element.91), channel_id=1, source_target_pairs={{0,1},{1,2},{2,3},{3,4},{4,5},{5,6},{6,7},{7,8},{8,9},{9,10},{10,1... | collective-permute-start | bytes 3145736 | tf_op jit(solution)/shard_map/cond/branch_1_fun/ppermute | solution.py:472
  69.7 7.6 %collective-permute-start.8 = (f32[2,472,256]{2,1,0:T(8,128)}, f32[2,472,256]{2,1,0:T(8,128)S(1)}, u32[]{:S(2)}, u32[]{:S(2)}) collective-permute-start(f32[2,472,256]{2,1,0:T(8,128)} %get-tuple-element.90), channel_id=1, source_target_pairs={{1,0},{2,1},{3,2},{4,3},{5,4},{6,5},{7,6},{8,7},{9,8},{10,9},{11,1... | collective-permute-start | bytes 2899976 | tf_op jit(solution)/shard_map/cond/branch_1_fun/ppermute | solution.py:467
  77.3 1.9 %collective-permute-start.10 = (f32[2,472,256]{2,1,0:T(8,128)}, f32[2,472,256]{2,1,0:T(8,128)S(1)}, u32[]{:S(2)}, u32[]{:S(2)}) collective-permute-start(f32[2,472,256]{2,1,0:T(8,128)} %get-tuple-element.92), channel_id=1, source_target_pairs={{0,1},{1,2},{2,3},{3,4},{4,5},{5,6},{6,7},{7,8},{8,9},{9,10},{10,1... | collective-permute-start | bytes 2899976 | tf_op jit(solution)/shard_map/cond/branch_1_fun/ppermute | solution.py:472
  79.2 0.0 collective-permute-done.6.other
  79.2 4.0 %scale_level.12 = (f32[36,2,64,256]{3,2,1,0:T(8,128)}, f32[36,3,64,256]{3,2,1,0:T(8,128)}) custom-call(f32[36]{0:T(128)} %get-tuple-element.75.scale, f32[36,5,2,8,256]{4,3,2,1,0:T(8,128)} %get-tuple-element.77.mine, f32[36,5,2,8,256]{4,3,2,1,0:T(8,128)S(1)} %collective-permute-done.6.other), custom_call_target="tpu_custom_call" | custom-call | tf_op jit(solution)/shard_map/cond/branch_1_fun/scale_level/pallas_call | solution.py:443
  83.2 7.2 %collective-permute-done.7.refs_6_ = f32[2,512,256]{2,1,0:T(8,128)S(1)} collective-permute-done((f32[2,512,256]{2,1,0:T(8,128)}, f32[2,512,256]{2,1,0:T(8,128)S(1)}, u32[]{:S(2)}, u32[]{:S(2)}) %collective-permute-start.7) | collective-permute-done | bytes 1048608 | tf_op jit(solution)/shard_map/cond/branch_1_fun/ppermute | solution.py:467
  90.4 7.9 %collective-permute-done.9.refs_8_.refs_7_ = f32[2,512,256]{2,1,0:T(8,128)S(1)} collective-permute-done((f32[2,512,256]{2,1,0:T(8,128)}, f32[2,512,256]{2,1,0:T(8,128)S(1)}, u32[]{:S(2)}, u32[]{:S(2)}) %collective-permute-start.9) | collective-permute-done | bytes 1048608 | tf_op jit(solution)/shard_map/cond/branch_1_fun/ppermute | solution.py:472
  98.3 4.8 %finish_level.14 = (f32[36,5,2,8,256]{4,3,2,1,0:T(8,128)S(1)}, f32[36,5,2,8,256]{4,3,2,1,0:T(8,128)S(1)}) custom-call(s32[385]{0:T(512)S(1)} %get-tuple-element.81.meta, s32[16]{0:T(128)S(1)} %get-tuple-element.82.plan, s32[768]{0:T(1024)S(1)} %get-tuple-element.83.refs_0_, s32[768]{0:T(1024)S(1)} %get-tuple-element.84.refs_1_, ...), custom_call_target="tpu_custom_call" | custom-call | tf_op jit(solution)/shard_map/cond/branch_1_fun/finish_level/pallas_call | solution.py:384
  103.1 2.4 %collective-permute-start.13 = (f32[36,5,2,8,256]{4,3,2,1,0:T(8,128)S(1)}, f32[36,5,2,8,256]{4,3,2,1,0:T(8,128)S(1)}, u32[]{:S(2)}, u32[]{:S(2)}) collective-permute-start(f32[36,5,2,8,256]{4,3,2,1,0:T(8,128)S(1)} %get-tuple-element.102), channel_id=1, source_target_pairs={{0,64},{64,0},{1,65},{65,1},{2,66},{66,2},{3,67},{67,3},{4,68},{68... | collective-permute-start | bytes 8847368 | tf_op jit(solution)/shard_map/cond/branch_1_fun/ppermute | solution.py:462
  105.5 5.6 %collective-permute-done.8.refs_7_ = f32[2,472,256]{2,1,0:T(8,128)S(1)} collective-permute-done((f32[2,472,256]{2,1,0:T(8,128)}, f32[2,472,256]{2,1,0:T(8,128)S(1)}, u32[]{:S(2)}, u32[]{:S(2)}) %collective-permute-start.8) | collective-permute-done | bytes 966688 | tf_op jit(solution)/shard_map/cond/branch_1_fun/ppermute | solution.py:467
  111.1 7.9 %collective-permute-done.10.refs_9_ = f32[2,472,256]{2,1,0:T(8,128)S(1)} collective-permute-done((f32[2,472,256]{2,1,0:T(8,128)}, f32[2,472,256]{2,1,0:T(8,128)S(1)}, u32[]{:S(2)}, u32[]{:S(2)}) %collective-permute-start.10) | collective-permute-done | bytes 966688 | tf_op jit(solution)/shard_map/cond/branch_1_fun/ppermute | solution.py:472
  119.0 0.0 copy-done.14
  119.0 5.2 %finish_level.13 = (f32[36,5,2,8,256]{4,3,2,1,0:T(8,128)S(1)}, f32[36,5,2,8,256]{4,3,2,1,0:T(8,128)S(1)}) custom-call(s32[385]{0:T(512)S(1)} %get-tuple-element.81.meta, s32[16]{0:T(128)S(1)} %get-tuple-element.82.plan, s32[768]{0:T(1024)S(1)} %get-tuple-element.83.refs_0_, s32[768]{0:T(1024)S(1)} %get-tuple-element.84.refs_1_, ...), custom_call_target="tpu_custom_call" | custom-call | tf_op jit(solution)/shard_map/cond/branch_1_fun/finish_level/pallas_call | solution.py:384
  124.3 1.4 collective-permute-start.12
  125.7 0.0 copy-done.15
  125.7 5.1 %finish_level.12 = (f32[36,5,2,8,256]{4,3,2,1,0:T(8,128)S(1)}, f32[36,5,2,8,256]{4,3,2,1,0:T(8,128)S(1)}) custom-call(s32[385]{0:T(512)S(1)} %get-tuple-element.81.meta, s32[16]{0:T(128)S(1)} %get-tuple-element.82.plan, s32[768]{0:T(1024)S(1)} %get-tuple-element.83.refs_0_, s32[768]{0:T(1024)S(1)} %get-tuple-element.84.refs_1_, ...), custom_call_target="tpu_custom_call" | custom-call | tf_op jit(solution)/shard_map/cond/branch_1_fun/finish_level/pallas_call | solution.py:384
  130.8 0.1 collective-permute-start.11
  130.9 0.0 collective-permute-done.13.other
  130.9 0.0 copy-done.21
  130.9 3.7 %scale_level.13 = (f32[36,2,64,256]{3,2,1,0:T(8,128)}, f32[36,3,64,256]{3,2,1,0:T(8,128)}) custom-call(f32[36]{0:T(128)S(1)} %copy-done.21, f32[36,5,2,8,256]{4,3,2,1,0:T(8,128)S(1)} %get-tuple-element.101.mine, f32[36,5,2,8,256]{4,3,2,1,0:T(8,128)S(1)} %collective-permute-done.13.other, ...), custom_call_target="tpu_custom_call", output_to_operand_aliasing={{0}: (3, {}), {1}: (4, {})} | custom-call | tf_op jit(solution)/shard_map/cond/branch_1_fun/scale_level/pallas_call | solution.py:443
  134.6 0.0 collective-permute-done.12.other
  134.6 3.7 %scale_level.14 = (f32[36,2,64,256]{3,2,1,0:T(8,128)}, f32[36,3,64,256]{3,2,1,0:T(8,128)}) custom-call(f32[36]{0:T(128)S(1)} %copy-done.21, f32[36,5,2,8,256]{4,3,2,1,0:T(8,128)S(1)} %get-tuple-element.97.mine, f32[36,5,2,8,256]{4,3,2,1,0:T(8,128)S(1)} %collective-permute-done.12.other, ...), custom_call_target="tpu_custom_call", output_to_operand_aliasing={{0}: (3, {}), {1}: (4, {})} | custom-call | tf_op jit(solution)/shard_map/cond/branch_1_fun/scale_level/pallas_call | solution.py:443
  138.3 0.0 collective-permute-done.11.other
  138.3 3.7 %scale_level.15 = (f32[36,2,64,256]{3,2,1,0:T(8,128)}, f32[36,3,64,256]{3,2,1,0:T(8,128)}) custom-call(f32[36]{0:T(128)S(1)} %copy-done.21, f32[36,5,2,8,256]{4,3,2,1,0:T(8,128)S(1)} %get-tuple-element.93.mine, f32[36,5,2,8,256]{4,3,2,1,0:T(8,128)S(1)} %collective-permute-done.11.other, ...), custom_call_target="tpu_custom_call", output_to_operand_aliasing={{0}: (3, {}), {1}: (4, {})} | custom-call | tf_op jit(solution)/shard_map/cond/branch_1_fun/scale_level/pallas_call | solution.py:443
  (13 shorter events, 0.0 us)
Async XLA Ops:
  2.6 27.2 %copy-start.17 = (bf16[768,256]{1,0:T(8,128)(2,1)S(1)}, bf16[768,256]{1,0:T(8,128)(2,1)}, u32[]{:S(2)}) copy-start(bf16[768,256]{1,0:T(8,128)(2,1)} %constant.32.clone.refs_1_) | copy-start | bytes 1179652
  18.2 41.4 %collective-permute-start.15 = (f32[2,640,256]{2,1,0:T(8,128)}, f32[2,640,256]{2,1,0:T(8,128)S(1)}, u32[]{:S(2)}, u32[]{:S(2)}) collective-permute-start(f32[2,640,256]{2,1,0:T(8,128)} %get-tuple-element.143), channel_id=1, source_target_pairs={{1,0},{2,1},{3,2},{4,3},{5,4},{6,5},{7,6},{8,7},{9,8},{10,9},{11,1... | collective-permute-start | bytes 3932168 | tf_op jit(solution)/shard_map/ppermute | solution.py:467
  24.9 34.7 %collective-permute-start.16 = (f32[2,640,256]{2,1,0:T(8,128)}, f32[2,640,256]{2,1,0:T(8,128)S(1)}, u32[]{:S(2)}, u32[]{:S(2)}) collective-permute-start(f32[2,640,256]{2,1,0:T(8,128)} %get-tuple-element.144), channel_id=1, source_target_pairs={{0,1},{1,2},{2,3},{3,4},{4,5},{5,6},{6,7},{7,8},{8,9},{9,10},{10,1... | collective-permute-start | bytes 3932168 | tf_op jit(solution)/shard_map/ppermute | solution.py:472
  27.0 30.1 %collective-permute-start.14 = (s32[80]{0:T(128)S(1)}, s32[80]{0:T(128)S(1)}, u32[]{:S(2)}, u32[]{:S(2)}) collective-permute-start(s32[80]{0:T(128)S(1)} %pad_add_fusion.1), channel_id=1, source_target_pairs={{0,64},{64,0},{1,65},{65,1},{2,66},{66,2},{3,67},{67,3},{4,68},{68... | collective-permute-start | bytes 968 | tf_op jit(solution)/shard_map/ppermute | solution.py:462
  29.8 20.0 %copy-start.1 = (f32[128,2,2,8,256]{4,3,2,1,0:T(8,128)S(1)}, f32[128,2,2,8,256]{4,3,2,1,0:T(8,128)}, u32[]{:S(2)}) copy-start(f32[128,2,2,8,256]{4,3,2,1,0:T(8,128)} %get-tuple-element.133.refs_2_) | copy-start | bytes 12582916
  49.8 2.2 %copy-start.2 = (f32[128,2,2,8,256]{4,3,2,1,0:T(8,128)S(1)}, f32[128,2,2,8,256]{4,3,2,1,0:T(8,128)}, u32[]{:S(2)}) copy-start(f32[128,2,2,8,256]{4,3,2,1,0:T(8,128)} %get-tuple-element.134.refs_3_) | copy-start | bytes 12582916
  59.5 38.8 %copy-start.16 = (f32[128,2,2,8,256]{4,3,2,1,0:T(8,128)S(1)}, f32[128,2,2,8,256]{4,3,2,1,0:T(8,128)}, u32[]{:S(2)}) copy-start(f32[128,2,2,8,256]{4,3,2,1,0:T(8,128)} %get-tuple-element.99.refs_2_) | copy-start | bytes 12582916 | tf_op jit(solution)/shard_map/cond
  59.5 19.7 %collective-permute-start.6 = (f32[36,5,2,8,256]{4,3,2,1,0:T(8,128)}, f32[36,5,2,8,256]{4,3,2,1,0:T(8,128)S(1)}, u32[]{:S(2)}, u32[]{:S(2)}) collective-permute-start(f32[36,5,2,8,256]{4,3,2,1,0:T(8,128)} %get-tuple-element.78), channel_id=1, source_target_pairs={{0,64},{64,0},{1,65},{65,1},{2,66},{66,2},{3,67},{67,3},{4,68},{68... | collective-permute-start | bytes 8847368 | tf_op jit(solution)/shard_map/cond/branch_1_fun/ppermute | solution.py:462
  62.4 28.0 %collective-permute-start.7 = (f32[2,512,256]{2,1,0:T(8,128)}, f32[2,512,256]{2,1,0:T(8,128)S(1)}, u32[]{:S(2)}, u32[]{:S(2)}) collective-permute-start(f32[2,512,256]{2,1,0:T(8,128)} %get-tuple-element.89), channel_id=1, source_target_pairs={{1,0},{2,1},{3,2},{4,3},{5,4},{6,5},{7,6},{8,7},{9,8},{10,9},{11,1... | collective-permute-start | bytes 3145736 | tf_op jit(solution)/shard_map/cond/branch_1_fun/ppermute | solution.py:467
  67.8 30.5 %collective-permute-start.9 = (f32[2,512,256]{2,1,0:T(8,128)}, f32[2,512,256]{2,1,0:T(8,128)S(1)}, u32[]{:S(2)}, u32[]{:S(2)}) collective-permute-start(f32[2,512,256]{2,1,0:T(8,128)} %get-tuple-element.91), channel_id=1, source_target_pairs={{0,1},{1,2},{2,3},{3,4},{4,5},{5,6},{6,7},{7,8},{8,9},{9,10},{10,1... | collective-permute-start | bytes 3145736 | tf_op jit(solution)/shard_map/cond/branch_1_fun/ppermute | solution.py:472
  69.7 41.4 %collective-permute-start.8 = (f32[2,472,256]{2,1,0:T(8,128)}, f32[2,472,256]{2,1,0:T(8,128)S(1)}, u32[]{:S(2)}, u32[]{:S(2)}) collective-permute-start(f32[2,472,256]{2,1,0:T(8,128)} %get-tuple-element.90), channel_id=1, source_target_pairs={{1,0},{2,1},{3,2},{4,3},{5,4},{6,5},{7,6},{8,7},{9,8},{10,9},{11,1... | collective-permute-start | bytes 2899976 | tf_op jit(solution)/shard_map/cond/branch_1_fun/ppermute | solution.py:467
  77.3 41.7 %collective-permute-start.10 = (f32[2,472,256]{2,1,0:T(8,128)}, f32[2,472,256]{2,1,0:T(8,128)S(1)}, u32[]{:S(2)}, u32[]{:S(2)}) collective-permute-start(f32[2,472,256]{2,1,0:T(8,128)} %get-tuple-element.92), channel_id=1, source_target_pairs={{0,1},{1,2},{2,3},{3,4},{4,5},{5,6},{6,7},{7,8},{8,9},{9,10},{10,1... | collective-permute-start | bytes 2899976 | tf_op jit(solution)/shard_map/cond/branch_1_fun/ppermute | solution.py:472
  98.3 20.7 %copy-start.12 = (f32[128,2,2,8,256]{4,3,2,1,0:T(8,128)S(1)}, f32[128,2,2,8,256]{4,3,2,1,0:T(8,128)}, u32[]{:S(2)}) copy-start(f32[128,2,2,8,256]{4,3,2,1,0:T(8,128)} %get-tuple-element.95.refs_2_) | copy-start | bytes 12582916 | tf_op jit(solution)/shard_map/cond
  98.3 20.7 %copy-start.14 = (f32[128,2,2,8,256]{4,3,2,1,0:T(8,128)S(1)}, f32[128,2,2,8,256]{4,3,2,1,0:T(8,128)}, u32[]{:S(2)}) copy-start(f32[128,2,2,8,256]{4,3,2,1,0:T(8,128)} %get-tuple-element.96.refs_3_) | copy-start | bytes 12582916 | tf_op jit(solution)/shard_map/cond
  103.1 27.8 %collective-permute-start.13 = (f32[36,5,2,8,256]{4,3,2,1,0:T(8,128)S(1)}, f32[36,5,2,8,256]{4,3,2,1,0:T(8,128)S(1)}, u32[]{:S(2)}, u32[]{:S(2)}) collective-permute-start(f32[36,5,2,8,256]{4,3,2,1,0:T(8,128)S(1)} %get-tuple-element.102), channel_id=1, source_target_pairs={{0,64},{64,0},{1,65},{65,1},{2,66},{66,2},{3,67},{67,3},{4,68},{68... | collective-permute-start | bytes 8847368 | tf_op jit(solution)/shard_map/cond/branch_1_fun/ppermute | solution.py:462
  119.0 6.6 %copy-start.13 = (f32[128,2,2,8,256]{4,3,2,1,0:T(8,128)S(1)}, f32[128,2,2,8,256]{4,3,2,1,0:T(8,128)}, u32[]{:S(2)}) copy-start(f32[128,2,2,8,256]{4,3,2,1,0:T(8,128)} %get-tuple-element.85.refs_2_) | copy-start | bytes 12582916 | tf_op jit(solution)/shard_map/cond
  119.0 6.6 %copy-start.15 = (f32[128,2,2,8,256]{4,3,2,1,0:T(8,128)S(1)}, f32[128,2,2,8,256]{4,3,2,1,0:T(8,128)}, u32[]{:S(2)}) copy-start(f32[128,2,2,8,256]{4,3,2,1,0:T(8,128)} %get-tuple-element.86.refs_3_) | copy-start | bytes 12582916 | tf_op jit(solution)/shard_map/cond
  124.3 10.4 %collective-permute-start.12 = (f32[36,5,2,8,256]{4,3,2,1,0:T(8,128)S(1)}, f32[36,5,2,8,256]{4,3,2,1,0:T(8,128)S(1)}, u32[]{:S(2)}, u32[]{:S(2)}) collective-permute-start(f32[36,5,2,8,256]{4,3,2,1,0:T(8,128)S(1)} %get-tuple-element.98), channel_id=1, source_target_pairs={{0,64},{64,0},{1,65},{65,1},{2,66},{66,2},{3,67},{67,3},{4,68},{68... | collective-permute-start | bytes 8847368 | tf_op jit(solution)/shard_map/cond/branch_1_fun/ppermute | solution.py:462
  125.7 5.3 %copy-start.21 = (f32[36]{0:T(128)S(1)}, f32[36]{0:T(128)}, u32[]{:S(2)}) copy-start(f32[36]{0:T(128)} %get-tuple-element.75.scale) | copy-start | bytes 436 | tf_op jit(solution)/shard_map/cond
  130.8 7.5 %collective-permute-start.11 = (f32[36,5,2,8,256]{4,3,2,1,0:T(8,128)S(1)}, f32[36,5,2,8,256]{4,3,2,1,0:T(8,128)S(1)}, u32[]{:S(2)}, u32[]{:S(2)}) collective-permute-start(f32[36,5,2,8,256]{4,3,2,1,0:T(8,128)S(1)} %get-tuple-element.94), channel_id=1, source_target_pairs={{0,64},{64,0},{1,65},{65,1},{2,66},{66,2},{3,67},{67,3},{4,68},{68... | collective-permute-start | bytes 8847368 | tf_op jit(solution)/shard_map/cond/branch_1_fun/ppermute | solution.py:462

commit v5 on v4

--- a/solution.py
+++ b/solution.py
@@ -22,7 +22,7 @@
 GAP = 16
 MIB = 1024 * 1024
 FIRST_CUTS = (640,)
-REST_CUTS = (512, 984)
+REST_CUTS = (984,)
 FULL_CUTS = (3072 + 64,)
 GROUPS = SNAPS // 8
 F32 = jnp.float32
@@ -93,11 +93,18 @@
 def smooth_kernel(part, cuts, meta, plan, *refs):
     pieces = len(cuts)
     vel, colop, rowop, refs = *refs[:3], refs[3:]
-    y_refs, refs = refs[:4], refs[4:]
+    if part == 1:
+        early, refs = refs[0], refs[1:]
+    strips = 3 if part else 4
+    y_refs, refs = refs[:strips], refs[strips:]
+    if part:
+        mine, theirs, refs = refs[0], refs[1], refs[2:]
     out_up, out_dn = refs[:pieces], refs[pieces:2 * pieces]
     pos_ref, plan_ref, refs = *refs[2 * pieces:2 * pieces + 2], refs[2 * pieces + 2:]
     vel_buf, oper_buf, col_buf, refs = *refs[:3], refs[3:]
     y_bufs, refs = refs[:4], refs[4:]
+    if part:
+        acc, refs = refs[0], refs[1:]
     xs, stack, up, dn, cursor, load_sem, store_sem, sem = refs
     row = lax.broadcasted_iota(I32, (8, WIDTH), 0)
     lane = lax.broadcasted_iota(I32, (1, WIDTH), 1)
@@ -110,6 +117,15 @@
     def store(g, level):
         rows = pl.ds(GROUP * g, GROUP)
         return pltpu.make_async_copy(y_bufs[level].at[rows], y_refs[level].at[rows], store_sem.at[g, level])
+
+    def load_early(g):
+        rows = pl.ds(GROUP * g, GROUP)
+        return pltpu.make_async_copy(early.at[rows], y_bufs[3].at[rows], store_sem.at[g, 3])
+
+    def add_fields(n, place, u, v):
+        phase = meta[2 * SNAPS + n]
+        for at_field, field in enumerate((u, v, u * u, v * v, u * v)):
+            acc[phase, at_field, place] += field
 
     def loop(low, high, body):
         lax.fori_loop(low, high, lambda g, carry: (body(g), carry)[1], 0)
@@ -168,6 +184,7 @@
         loop(begin, end, lambda g: load(g).start())
         for copy in tables:
             copy.start()
+        loop(0, begin, lambda g: load_early(g).start())
         starts = [plan[k] for k in range(6)]
     else:
         begin, end = I32(0), I32(GROUPS)
@@ -176,6 +193,7 @@
             copy.start()
         starts = ends(lax.fori_loop(0, GROUPS, count_group, zero))[0]
     if part:
+        acc[...] = jnp.zeros_like(acc)
         for k in range(16):
             plan_ref[k] = I32(GROUPS)
     for k in range(6):
@@ -206,12 +224,16 @@
             n = GROUP * g + b
             oper = oper_buf[meta[n] + MAXS]
             ext = [dot(oper, stack[b, comp]) for comp in range(2)]
-            for level in range(4):
+            for level in range(strips):
                 for comp in range(2):
                     top = HALO + 8 * level
                     bottom = HALO + ROWS - 8 - 8 * level
                     y_bufs[level][n, 0, comp] = ext[comp][top:top + 8]
                     y_bufs[level][n, 1, comp] = ext[comp][bottom:bottom + 8]
+            if part:
+                for place in range(2):
+                    rows = slice(2 * HALO + 8 * place, 2 * HALO + 8 * place + 8)
+                    add_fields(n, place, ext[0][rows], ext[1][rows])
             for side, need in enumerate(needs(meta[n])):
                 buffer = (up, dn)[side]
                 for level in range(3):
@@ -230,7 +252,7 @@
                         old = buffer[comp, pl.ds(base, 8)]
                         buffer[comp, pl.ds(base, 8)] = jnp.where(row < skew, old, tile)
                         buffer[comp, pl.ds(base + 8, 8)] = tile
-        for level in range(4):
+        for level in range(strips):
             store(g, level).start()
 
     loop(begin, end, group)
@@ -243,12 +265,26 @@
         low = high
     for copy in copies:
         copy.start()
-    if part == 0:
+    if part:
+        def add_early(g):
+            load_early(g).wait()
+            for n in range(GROUP):
+                for place in range(2):
+                    add_fields(GROUP * g + n, place, y_bufs[3][GROUP * g + n, place, 0], y_bufs[3][GROUP * g + n, place, 1])
+
+        if part == 1:
+            loop(0, begin, add_early)
+        sums_out = [pltpu.make_async_copy(acc.at[HALF:PHASES], theirs, sem.at[2 + len(copies)]),
+                    pltpu.make_async_copy(acc.at[0:HALF], mine, sem.at[3 + len(copies)])]
+        for copy in sums_out:
+            copy.start()
+        copies += sums_out
+    else:
         for g in range(4):
             pl.when(g >= end)(load(g).wait)
 
     def stored(g):
-        for level in range(4):
+        for level in range(strips):
             store(g, level).wait()
 
     loop(begin, end, stored)
@@ -256,23 +292,26 @@
         copy.wait()
 
 
-def smooth_part(part, meta, plan, velocity, colop, rowop, cuts):
+def smooth_part(part, meta, plan, velocity, colop, rowop, cuts, early=()):
     pieces = len(cuts)
     sizes = [high - low for low, high in zip((0,) + cuts[:-1], cuts)]
-    any_space = pl.BlockSpec(memory_space=pl.ANY)
+    any_space = pl.BlockSpec(memory_space=pltpu.HBM)
     smem = pl.BlockSpec(memory_space=pltpu.SMEM)
     piece_shapes = [jax.ShapeDtypeStruct((2, size, WIDTH), F32) for size in sizes]
     strip = jax.ShapeDtypeStruct((SNAPS, 2, 2, 8, WIDTH), F32)
     room = cuts[-1] + GAP
+    total = jax.ShapeDtypeStruct((HALF, 5, 2, 8, WIDTH), F32)
+    strips, sums = (3, 2) if part else (4, 0)
     out = pl.pallas_call(
         functools.partial(smooth_kernel, part, cuts),
-        in_specs=[smem] * 2 + [any_space] * 3,
-        out_specs=[any_space] * (4 + 2 * pieces) + [smem, smem],
+        in_specs=[smem] * 2 + [any_space] * (3 + len(early)),
+        out_specs=[any_space] * (strips + sums + 2 * pieces) + [smem, smem],
         scratch_shapes=[
             pltpu.VMEM((SNAPS, 2, ROWS, WIDTH), F32),
             pltpu.VMEM((2 * MAXS + 1, EXT, 3 * ROWS), BF16),
             pltpu.VMEM((3 * WIDTH, WIDTH), BF16),
-        ] + [pltpu.VMEM((SNAPS, 2, 2, 8, WIDTH), F32)] * 4 + [
+        ] + [pltpu.VMEM((SNAPS, 2, 2, 8, WIDTH), F32)] * 4
+        + ([pltpu.VMEM((PHASES, 5, 2, 8, WIDTH), F32)] if part else []) + [
             pltpu.VMEM((GROUP * 2 * ROWS, 3 * WIDTH), BF16),
             pltpu.VMEM((GROUP, 2, 3 * ROWS, WIDTH), BF16),
             pltpu.VMEM((2, room, WIDTH), F32),
@@ -280,14 +319,15 @@
             pltpu.SMEM((8,), I32),
             pltpu.SemaphoreType.DMA((GROUPS,)),
             pltpu.SemaphoreType.DMA((GROUPS, 4)),
-            pltpu.SemaphoreType.DMA((2 + 2 * pieces,)),
+            pltpu.SemaphoreType.DMA((4 + 2 * pieces,)),
         ],
-        out_shape=[strip] * 4 + piece_shapes * 2
+        out_shape=[strip] * strips + [total] * sums + piece_shapes * 2
         + [jax.ShapeDtypeStruct((SNAPS * 6,), I32), jax.ShapeDtypeStruct((16,), I32)],
-        compiler_params=pltpu.CompilerParams(vmem_limit_bytes=56 * MIB),
+        compiler_params=pltpu.CompilerParams(vmem_limit_bytes=62 * MIB),
         name="smooth_part",
-    )(meta, plan, velocity, colop, rowop)
-    return out[:4], out[4:4 + pieces], out[4 + pieces:4 + 2 * pieces], out[-2], out[-1]
+    )(meta, plan, velocity, colop, rowop, *early)
+    packs = out[strips + sums:]
+    return out[:strips], out[strips:strips + sums], packs[:pieces], packs[pieces:2 * pieces], out[-2], out[-1]
 
 
 def finish_kernel(level, cuts, meta, plan, *refs):
@@ -346,7 +386,8 @@
                 skew = pos & 7
                 base = pl.multiple_of(pos - skew, 8)
                 turn = skew if place == 0 else (skew + have) & 7
-                keep = row < have if place == 0 else row >= 8 - have
+                known = jnp.where(meta[3 * SNAPS] == 2 * place, 0, have)
+                keep = row < known if place == 0 else row >= 8 - known
                 for comp in range(2):
                     lower = buffers[2 * k + side][comp, pl.ds(base, 8)]
                     upper = buffers[2 * k + side][comp, pl.ds(base + 8, 8)]
@@ -374,7 +415,7 @@
 
 
 def finish_level(level, meta, plan, parts):
-    any_space = pl.BlockSpec(memory_space=pl.ANY)
+    any_space = pl.BlockSpec(memory_space=pltpu.HBM)
     smem = pl.BlockSpec(memory_space=pltpu.SMEM)
     shape = jax.ShapeDtypeStruct((HALF, 5, 2, 8, WIDTH), F32)
     cuts = [level_cuts(part[2], level) if level < 3 else () for part in parts]
@@ -393,69 +434,99 @@
             pltpu.SemaphoreType.DMA((GROUPS,)),
             pltpu.SemaphoreType.DMA((max(chunks, 1),)),
         ],
-        compiler_params=pltpu.CompilerParams(vmem_limit_bytes=12 * MIB + 16 * WIDTH * sum(rooms)),
+        compiler_params=pltpu.CompilerParams(vmem_limit_bytes=62 * MIB),
         name="finish_level",
     )(meta, plan, *[part[0] for part in parts], *[part[1][level] for part in parts], *packs)
 
 
-def scale_kernel(level, block, scale, mine, other, *refs):
-    mean, moment, a_buf, b_buf, mean_buf, moment_buf, sem = refs[-7:]
-    count = HALF // block
+def scale_kernel(levels, block, message, reply, *refs):
+    many = len(levels)
+    mines, others = refs[:many], refs[many:2 * many]
+    mean, moment, a_buf, b_buf, load_sem, store_sem = refs[-6:]
+    parts = [(k, slice(start, start + block)) for k in range(many) for start in range(0, HALF, block)]
     loads, stores = [], []
-    for k in range(count):
-        part = slice(block * k, block * (k + 1))
-        loads.append([pltpu.make_async_copy(mine.at[part], a_buf.at[part], sem.at[2 * k]),
-                      pltpu.make_async_copy(other.at[part], b_buf.at[part], sem.at[2 * k + 1])])
+    for at, (k, part) in enumerate(parts):
+        loads.append([pltpu.make_async_copy(mines[k].at[part], a_buf.at[k, part], load_sem.at[2 * at]),
+                      pltpu.make_async_copy(others[k].at[part], b_buf.at[k, part], load_sem.at[2 * at + 1])])
         group = []
         for place in range(2):
-            rows = slice(8 * level, 8 * level + 8) if place == 0 else slice(ROWS - 8 - 8 * level, ROWS - 8 * level)
-            for which, (buf, out) in enumerate(((mean_buf, mean), (moment_buf, moment))):
+            first = 8 * levels[k] if place == 0 else ROWS - 8 - 8 * levels[k]
+            rows = slice(first, first + 8)
+            for which, (fields, out) in enumerate(((slice(0, 2), mean), (slice(2, 5), moment))):
                 group.append(pltpu.make_async_copy(
-                    buf.at[place, part], out.at[part, :, rows], sem.at[2 * count + 4 * k + 2 * place + which]))
+                    a_buf.at[k, part, fields, place], out.at[part, :, rows], store_sem.at[4 * at + 2 * place + which]))
         stores.append(group)
     for copies in loads:
         for copy in copies:
             copy.start()
-    for k in range(count):
-        for copy in loads[k]:
+    for at, (k, part) in enumerate(parts):
+        for copy in loads[at]:
             copy.wait()
 
-        def one(p, carry):
-            factor = scale[p]
-            for place in range(2):
-                total = (a_buf[p, :, place] + b_buf[p, :, place]) * factor
-                mean_buf[place, p] = total[0:2]
-                moment_buf[place, p] = total[2:5]
+        def one(p, carry, k=k):
+            count = jnp.full((8, WIDTH), message[0, p] + reply[0, HALF + p], I32).astype(F32)
+            a_buf[k, p] = (a_buf[k, p] + b_buf[k, p]) * (1.0 / jnp.maximum(count, 1.0))
             return carry
 
-        lax.fori_loop(block * k, block * (k + 1), one, 0)
-        for copy in stores[k]:
+        lax.fori_loop(part.start, part.stop, one, 0, unroll=2)
+        for copy in stores[at]:
             copy.start()
     for copies in stores:
         for copy in copies:
             copy.wait()
 
 
-def scale_level(level, scale, mine, other, before):
+def scale_levels(levels, counts, pairs, before):
     block = 18
-    count = HALF // block
-    any_space = pl.BlockSpec(memory_space=pl.ANY)
+    many = len(levels)
+    parts = many * HALF // block
+    smem = pl.BlockSpec(memory_space=pltpu.SMEM)
+    hbm = pl.BlockSpec(memory_space=pltpu.HBM)
+    buffer = pltpu.VMEM((many, HALF, 5, 2, 8, WIDTH), F32)
     return pl.pallas_call(
-        functools.partial(scale_kernel, level, block),
-        in_specs=[pl.BlockSpec(memory_space=pltpu.SMEM)] + [any_space] * (2 + len(before)),
-        out_specs=[pl.BlockSpec(memory_space=pltpu.HBM)] * 2,
+        functools.partial(scale_kernel, levels, block),
+        in_specs=[smem] * 2 + [hbm] * (2 * many + len(before)),
+        out_specs=[hbm] * 2,
         out_shape=[jax.ShapeDtypeStruct((HALF, 2, ROWS, WIDTH), F32), jax.ShapeDtypeStruct((HALF, 3, ROWS, WIDTH), F32)],
-        scratch_shapes=[
-            pltpu.VMEM((HALF, 5, 2, 8, WIDTH), F32),
-            pltpu.VMEM((HALF, 5, 2, 8, WIDTH), F32),
-            pltpu.VMEM((2, HALF, 2, 8, WIDTH), F32),
-            pltpu.VMEM((2, HALF, 3, 8, WIDTH), F32),
-            pltpu.SemaphoreType.DMA((6 * count,)),
-        ],
-        input_output_aliases={3: 0, 4: 1} if before else {},
-        compiler_params=pltpu.CompilerParams(vmem_limit_bytes=10 * MIB),
-        name="scale_level",
-    )(scale, mine, other, *before)
+        scratch_shapes=[buffer, buffer, pltpu.SemaphoreType.DMA((2 * parts,)), pltpu.SemaphoreType.DMA((4 * parts,))],
+        input_output_aliases={2 + 2 * many: 0, 3 + 2 * many: 1} if before else {},
+        compiler_params=pltpu.CompilerParams(vmem_limit_bytes=62 * MIB),
+        name="scale_levels",
+    )(*counts, *[pair[0] for pair in pairs], *[pair[1] for pair in pairs], *before)
+
+
+def exchange_kernel(up, dn, theirs, message, below, above, other, reply, send_sem, recv_sem):
+    snap, tile = lax.axis_index("snap"), lax.axis_index("tile")
+    size = lax.axis_size("tile")
+    to_up = (snap, lax.rem(tile + size - 1, size))
+    to_dn = (snap, lax.rem(tile + 1, size))
+    to_core = (1 - snap, tile)
+    barrier = pltpu.get_barrier_semaphore()
+    for target in (to_up, to_dn, to_core):
+        pl.semaphore_signal(barrier, inc=1, device_id=target, device_id_type=pl.DeviceIdType.MESH)
+    pl.semaphore_wait(barrier, 3)
+    copies = []
+    for source, landing, target in ((up, below, to_up), (dn, above, to_dn), (theirs, other, to_core), (message, reply, to_core)):
+        copies.append(pltpu.make_async_remote_copy(
+            src_ref=source, dst_ref=landing, send_sem=send_sem.at[len(copies)], recv_sem=recv_sem.at[len(copies)],
+            device_id=target, device_id_type=pl.DeviceIdType.MESH))
+    for copy in copies:
+        copy.start()
+    for copy in copies:
+        copy.wait()
+
+
+def exchange(up, dn, theirs, message):
+    any_space = pl.BlockSpec(memory_space=pltpu.HBM)
+    return pl.pallas_call(
+        exchange_kernel,
+        in_specs=[any_space] * 4,
+        out_specs=[any_space] * 4,
+        out_shape=[jax.ShapeDtypeStruct(value.shape, value.dtype) for value in (up, dn, theirs, message)],
+        scratch_shapes=[pltpu.SemaphoreType.DMA((4,)), pltpu.SemaphoreType.DMA((4,))],
+        compiler_params=pltpu.CompilerParams(collective_id=0, has_side_effects=True, vmem_limit_bytes=62 * MIB),
+        name="exchange",
+    )(up, dn, theirs, message)
 
 
 def to_partner(value):
@@ -496,39 +567,29 @@
 
     smooth = functools.partial(smooth_part, velocity=velocity, colop=colop, rowop=rowop)
 
-    def full(scale, *_):
-        strips, up, dn, positions, plan = smooth(2, meta, jnp.zeros((16,), I32), cuts=FULL_CUTS)
+    def full(counts, *_):
+        strips, sums, up, dn, positions, plan = smooth(2, meta, jnp.zeros((16,), I32), cuts=FULL_CUTS)
         below, above = send(up, dn)
-        before = ()
-        for level in (3, 0, 1, 2):
-            mine, theirs = finish_level(level, meta, plan, [(positions, strips, FULL_CUTS, below, above)])
-            before = scale_level(level, scale, mine, to_partner(theirs), before)
-        return tuple(before)
-
-    def fast(scale, mine, theirs, plan, strips_a, pos_a, below_a, above_a, strips_b, pos_b, up_b, dn_b):
-        rest = (up_b[1], dn_b[1])
-        below_b, above_b = send(up_b[:1], dn_b[:1])
-        other = to_partner(theirs)
-        more = send(rest[0:1], rest[1:2])
-        before = scale_level(3, scale, mine, other, ())
-        here, before = lax.optimization_barrier((meta, tuple(before)))
-        parts = [(pos_a, strips_a, FIRST_CUTS, below_a, above_a),
-                 (pos_b, strips_b, REST_CUTS, below_b + more[0], above_b + more[1])]
-        totals = [finish_level(level, here, plan, parts) for level in range(3)]
-        for level, (mine, theirs) in enumerate(totals):
-            before = scale_level(level, scale, mine, to_partner(theirs), before)
-        return tuple(before)
-
-    strips_a, up_a, dn_a, pos_a, plan = smooth(0, meta, jnp.zeros((16,), I32), cuts=FIRST_CUTS)
+        totals = [finish_level(level, meta, plan, [(positions, strips, FULL_CUTS, below, above)]) for level in range(3)]
+        totals = [(mine, to_partner(theirs)) for mine, theirs in (sums, *totals)]
+        before = scale_levels((3, 0), counts, totals[:2], ())
+        return tuple(scale_levels((1, 2), counts, totals[2:], before))
+
+    def last(counts, mine, other, mean, moment):
+        return tuple(scale_levels((2,), counts, [(mine, other)], (mean, moment)))
+
+    strips_a, _, up_a, dn_a, pos_a, plan = smooth(0, meta, jnp.zeros((16,), I32), cuts=FIRST_CUTS)
     below_a, above_a = send(up_a, dn_a)
-    message = jnp.concatenate([own, plan[8:]])
-    reply = to_partner(message)
-    strips_b, up_b, dn_b, pos_b, _ = smooth(1, meta, plan, cuts=REST_CUTS)
-    mine, theirs = finish_level(3, meta, plan, [(pos_a, strips_a, (), (), ()), (pos_b, strips_b, (), (), ())])
-    scale = 1.0 / jnp.maximum((message[:HALF] + reply[HALF:PHASES]).astype(F32), 1.0)
-    over = jnp.maximum(message[PHASES], reply[PHASES])
-    return lax.cond(over <= 0, fast, full, scale, mine, theirs,
-                    plan, strips_a, pos_a, below_a, above_a, strips_b, pos_b, up_b, dn_b)
+    message = jnp.broadcast_to(jnp.concatenate([own, plan[8:], jnp.zeros((48,), I32)])[None], (8, 128))
+    strips_b, sums, up_b, dn_b, pos_b, _ = smooth(1, meta, plan, cuts=REST_CUTS, early=(strips_a[3],))
+    below_b, above_b, other, reply = exchange(up_b[0], dn_b[0], sums[1], message)
+    counts = (message, reply)
+    over = jnp.max(jnp.maximum(message, reply)[0:1, PHASES:PHASES + 8])
+    parts = [(pos_a, strips_a, FIRST_CUTS, below_a, above_a), (pos_b, strips_b, REST_CUTS, [below_b], [above_b])]
+    totals = [finish_level(level, meta, plan, parts) for level in range(3)]
+    totals = [(sums[0], other)] + [(mine, to_partner(theirs)) for mine, theirs in totals]
+    before = scale_levels((3, 0, 1), counts, totals[:3], ())
+    return lax.cond(over <= 0, last, full, counts, *totals[3], *before)
 
 
 def solution(mesh):

time: 143 us -> 146 us (1.021)
  Pallas kernels: 70.8 us -> 128 us
  waiting for transfers between devices: 28.6 us -> 0.01 us
  starting transfers between devices: 34.3 us -> 11.1 us
  local copies, waits for them, and re-layouts: 4.71 us -> 3.07 us
    pallas_call x4 -> x3, Pallas kernels: 15 us -> 68.3 us  [the longest x1 53 us: exchange(): pl.pallas_call(exchange_kernel, in_specs=[any_space] * 4, out_specs=[any_...]
    ppermute x3 -> x1, waiting for transfers between devices: 15.8 us -> 0.01 us  [to_below(): return lax.ppermute(value, 'tile', [(i, i + 1) for i in range(size - 1)])]
    ppermute x3 -> x1, starting transfers between devices: 19.7 us -> 6.67 us  [to_above(): return lax.ppermute(value, 'tile', [(i + 1, i) for i in range(size - 1)])]
    ppermute x3 -> x1, waiting for transfers between devices: 12.8 us -> 0.01 us  [to_above(): return lax.ppermute(value, 'tile', [(i + 1, i) for i in range(size - 1)])]
    ppermute x5 -> x3, starting transfers between devices: 8.91 us -> 2.55 us  [to_partner(): return lax.ppermute(value, 'snap', [(0, 1), (1, 0)])]
    ppermute x3 -> x1, starting transfers between devices: 5.76 us -> 1.92 us  [to_below(): return lax.ppermute(value, 'tile', [(i, i + 1) for i in range(size - 1)])]
    pallas_call x4 -> x3, Pallas kernels: 20.2 us -> 22.6 us  [finish_level(): pl.pallas_call(functools.partial(finish_kernel, level, cuts), in_specs=[s...]
    pallas_call x2, Pallas kernels: 35.5 us -> 37.4 us  [smooth_part(): pl.pallas_call(functools.partial(smooth_kernel, part, cuts), in_specs=[sm...]
  transfers between devices with their start and end apart: 11 -> 5, of which waited for: 4 -> 0; matrix products, arithmetic and copies ran while one was open for 1% -> 1% of each run, Pallas kernels for 36% -> 70%
where the time goes in v5:
time: 146 us
  Pallas kernels  128 us (88%)
  starting transfers between devices  11.1 us (8%)
  local copies, waits for them, and re-layouts  3.07 us (2%)
  between operations  1.61 us (1%)
  other arithmetic  1.57 us (1%)
    pallas_call x1, Pallas kernels, exchange(): pl.pallas_call(exchange_kernel, in_specs=[any_space] * 4, out_specs=[any_...  53 us
    pallas_call x2, Pallas kernels, smooth_part(): pl.pallas_call(functools.partial(smooth_kernel, part, cuts), in_specs=[sm...  37.4 us
    pallas_call x3, Pallas kernels, finish_level(): pl.pallas_call(functools.partial(finish_kernel, level, cuts), in_specs=[s...  22.6 us
    pallas_call x2, Pallas kernels, scale_levels(): pl.pallas_call(functools.partial(scale_kernel, levels, block), in_specs=[...  15.3 us
    ppermute x1, starting transfers between devices, to_above(): return lax.ppermute(value, 'tile', [(i + 1, i) for i in range(size - 1)])  6.67 us
  transfers between devices with their start and end apart: 5, of which 0 were waited for; matrix products, arithmetic and copies ran while one was open for 1% of the time, Pallas kernels for 70%

profile of v5, /device:TPU:97, one launch (start us, length us, event | category | flops | bytes accessed | tf_op | source)
XLA Modules:
  0.0 146.0 jit_solution(12644710073941451035)
XLA Ops:
  0.6 0.8 slice_bitcast_fusion.1
  1.4 0.7 subtract_remainder_fusion
  2.1 0.5 broadcast_4_plan.2.plan
  2.6 0.0 copy-start.1
  2.6 14.3 %smooth_part.4 = (f32[128,2,2,8,256]{4,3,2,1,0:T(8,128)}, f32[128,2,2,8,256]{4,3,2,1,0:T(8,128)}, f32[128,2,2,8,256]{4,3,2,1,0:T(8,128)}, f32[128,2,2,8,256]{4,3...) custom-call(s32[385]{0:T(512)S(1)} %pad_add_fusion.meta, ...), custom_call_target="tpu_custom_call" | custom-call | tf_op jit(solution)/shard_map/smooth_part/pallas_call | solution.py:305
  16.9 6.7 %collective-permute-start.6 = (f32[2,640,256]{2,1,0:T(8,128)}, f32[2,640,256]{2,1,0:T(8,128)S(1)}, u32[]{:S(2)}, u32[]{:S(2)}) collective-permute-start(f32[2,640,256]{2,1,0:T(8,128)} %get-tuple-element.93), channel_id=1, source_target_pairs={{1,0},{2,1},{3,2},{4,3},{5,4},{6,5},{7,6},{8,7},{9,8},{10,9},{11,1... | collective-permute-start | bytes 3932168 | tf_op jit(solution)/shard_map/ppermute | solution.py:538
  23.6 1.9 %collective-permute-start.7 = (f32[2,640,256]{2,1,0:T(8,128)}, f32[2,640,256]{2,1,0:T(8,128)}, u32[]{:S(2)}, u32[]{:S(2)}) collective-permute-start(f32[2,640,256]{2,1,0:T(8,128)} %get-tuple-element.94), channel_id=1, source_target_pairs={{0,1},{1,2},{2,3},{3,4},{4,5},{5,6},{6,7},{7,8},{8,9},{9,10},{10,1... | collective-permute-start | bytes 3932168 | tf_op jit(solution)/shard_map/ppermute | solution.py:543
  25.5 0.7 slice.14
  26.2 0.0 copy-done.1
  26.2 23.2 %smooth_part.5 = (f32[128,2,2,8,256]{4,3,2,1,0:T(8,128)}, f32[128,2,2,8,256]{4,3,2,1,0:T(8,128)}, f32[128,2,2,8,256]{4,3,2,1,0:T(8,128)}, f32[36,5,2,8,256]{4,3,...) custom-call(s32[385]{0:T(512)S(1)} %pad_add_fusion.meta, ...), custom_call_target="tpu_custom_call" | custom-call | tf_op jit(solution)/shard_map/smooth_part/pallas_call | solution.py:305
  49.4 0.1 convert_reduce_fusion
  49.5 0.1 pad_add_fusion.1
  49.6 53.0 %exchange.1 = (f32[2,984,256]{2,1,0:T(8,128)}, f32[2,984,256]{2,1,0:T(8,128)}, f32[36,5,2,8,256]{4,3,2,1,0:T(8,128)}, s32[8,128]{1,0:T(8,128)S(1)}) custom-call(f32[2,984,256]{2,1,0:T(8,128)} %get-tuple-element.85.up, f32[2,984,256]{2,1,0:T(8,128)} %get-tuple-element.86.dn, f32[36,5,2,8,256]{4,3,2,1,0:T(8,128)} %get-tuple-element.87.theirs, ...), custom_call_target="tpu_custom_call" | custom-call | tf_op jit(solution)/shard_map/exchange/pallas_call | solution.py:521
  102.6 0.0 collective-permute-done.6.refs_4_
  102.6 0.0 copy-start
  102.6 0.0 collective-permute-done.7.refs_5_
  102.6 1.1 copy-done
  103.7 7.5 %finish_level.11 = (f32[36,5,2,8,256]{4,3,2,1,0:T(8,128)}, f32[36,5,2,8,256]{4,3,2,1,0:T(8,128)}) custom-call(s32[385]{0:T(512)S(1)} %pad_add_fusion.meta, s32[16]{0:T(128)} %get-tuple-element.83.plan, s32[768]{0:T(1024)} %get-tuple-element.89.refs_0_, s32[768]{0:T(1024)} %get-tuple-element.90.refs_1_, f32[128,2,2,8,256]{4,3,2,1,0:T(8,128)} %get-tuple-element.103.refs_2_, ...), custom_call_target="tpu_custom_call" | custom-call | tf_op jit(solution)/shard_map/finish_level/pallas_call | solution.py:425
  111.2 2.0 %collective-permute-start.10 = (f32[36,5,2,8,256]{4,3,2,1,0:T(8,128)}, f32[36,5,2,8,256]{4,3,2,1,0:T(8,128)}, u32[]{:S(2)}, u32[]{:S(2)}) collective-permute-start(f32[36,5,2,8,256]{4,3,2,1,0:T(8,128)} %get-tuple-element.108), channel_id=1, source_target_pairs={{0,64},{64,0},{1,65},{65,1},{2,66},{66,2},{3,67},{67,3},{4,68},{68... | collective-permute-start | bytes 8847368 | tf_op jit(solution)/shard_map/ppermute | solution.py:533
  113.2 7.7 %finish_level.10 = (f32[36,5,2,8,256]{4,3,2,1,0:T(8,128)}, f32[36,5,2,8,256]{4,3,2,1,0:T(8,128)}) custom-call(s32[385]{0:T(512)S(1)} %pad_add_fusion.meta, s32[16]{0:T(128)} %get-tuple-element.83.plan, s32[768]{0:T(1024)} %get-tuple-element.89.refs_0_, s32[768]{0:T(1024)} %get-tuple-element.90.refs_1_, f32[128,2,2,8,256]{4,3,2,1,0:T(8,128)} %get-tuple-element.100.refs_2_, ...), custom_call_target="tpu_custom_call" | custom-call | tf_op jit(solution)/shard_map/finish_level/pallas_call | solution.py:425
  120.9 0.1 collective-permute-start.9
  121.0 7.5 %finish_level.9 = (f32[36,5,2,8,256]{4,3,2,1,0:T(8,128)}, f32[36,5,2,8,256]{4,3,2,1,0:T(8,128)}) custom-call(s32[385]{0:T(512)S(1)} %pad_add_fusion.meta, s32[16]{0:T(128)} %get-tuple-element.83.plan, s32[768]{0:T(1024)} %get-tuple-element.89.refs_0_, s32[768]{0:T(1024)} %get-tuple-element.90.refs_1_, f32[128,2,2,8,256]{4,3,2,1,0:T(8,128)} %get-tuple-element.91.refs_2_, ...), custom_call_target="tpu_custom_call" | custom-call | tf_op jit(solution)/shard_map/finish_level/pallas_call | solution.py:425
  128.4 0.4 collective-permute-start.8
  128.9 0.7 slice_reduce_fusion
  130.2 0.0 collective-permute-done.10.refs_5_
  130.2 0.0 collective-permute-done.9.refs_4_
  130.2 10.5 %scale_levels.7 = (f32[36,2,64,256]{3,2,1,0:T(8,128)}, f32[36,3,64,256]{3,2,1,0:T(8,128)}) custom-call(s32[8,128]{1,0:T(8,128)S(1)} %broadcast_in_dim.16.message, s32[8,128]{1,0:T(8,128)S(1)} %get-tuple-element.88.reply, f32[36,5,2,8,256]{4,3,2,1,0:T(8,128)} %get-tuple-element.99.refs_0_, f32[36,5,2,8,256]{4,3,2,1,0:T(8,128)} %get-tuple-element.102.refs_1_, ...), custom_call_target="tpu_custom_call" | custom-call | tf_op jit(solution)/shard_map/scale_levels/pallas_call | solution.py:486
  140.8 0.0 collective-permute-done.8
  140.8 5.0 %conditional.1 = ((f32[36,2,64,256]{3,2,1,0:T(8,128)}, f32[36,3,64,256]{3,2,1,0:T(8,128)})) conditional(s32[]{:T(128)} %convert_element_type.7, (s32[385]{0:T(512)S(1)}, f32[128,2,64,256]{3,2,1,0:T(8,128)}, bf16[768,256]{1,0:T(8,128)(2,1)S(1)}, bf16[3,33,112,192]{3,2,1,0:T(8,128)(2,1)}, s32[8,128]{1,0:T(8,128)S(1)}, ...), branch_computations={%region_2.3_spmd, %region_3.4_spmd} | conditional | bytes 98566456 | solution.py:592
  141.0 4.8 %scale_levels.6 = (f32[36,2,64,256]{3,2,1,0:T(8,128)}, f32[36,3,64,256]{3,2,1,0:T(8,128)}) custom-call(s32[8,128]{1,0:T(8,128)S(1)} %get-tuple-element.47.message, s32[8,128]{1,0:T(8,128)S(1)} %get-tuple-element.48.reply, f32[36,5,2,8,256]{4,3,2,1,0:T(8,128)} %get-tuple-element.49.refs_0_, ...), custom_call_target="tpu_custom_call", output_to_operand_aliasing={{0}: (4, {}), {1}: (5, {})} | custom-call | tf_op jit(solution)/shard_map/cond/branch_1_fun/scale_levels/pallas_call | solution.py:486
  (4 shorter events, 0.0 us)
Async XLA Ops:
  2.6 23.6 %copy-start.1 = (bf16[768,256]{1,0:T(8,128)(2,1)S(1)}, bf16[768,256]{1,0:T(8,128)(2,1)}, u32[]{:S(2)}) copy-start(bf16[768,256]{1,0:T(8,128)(2,1)} %constant.31.clone.refs_1_) | copy-start | bytes 1179652
  16.9 85.7 %collective-permute-start.6 = (f32[2,640,256]{2,1,0:T(8,128)}, f32[2,640,256]{2,1,0:T(8,128)S(1)}, u32[]{:S(2)}, u32[]{:S(2)}) collective-permute-start(f32[2,640,256]{2,1,0:T(8,128)} %get-tuple-element.93), channel_id=1, source_target_pairs={{1,0},{2,1},{3,2},{4,3},{5,4},{6,5},{7,6},{8,7},{9,8},{10,9},{11,1... | collective-permute-start | bytes 3932168 | tf_op jit(solution)/shard_map/ppermute | solution.py:538
  23.6 79.0 %collective-permute-start.7 = (f32[2,640,256]{2,1,0:T(8,128)}, f32[2,640,256]{2,1,0:T(8,128)}, u32[]{:S(2)}, u32[]{:S(2)}) collective-permute-start(f32[2,640,256]{2,1,0:T(8,128)} %get-tuple-element.94), channel_id=1, source_target_pairs={{0,1},{1,2},{2,3},{3,4},{4,5},{5,6},{6,7},{7,8},{8,9},{9,10},{10,1... | collective-permute-start | bytes 3932168 | tf_op jit(solution)/shard_map/ppermute | solution.py:543
  102.6 1.1 copy-start
  111.2 19.0 %collective-permute-start.10 = (f32[36,5,2,8,256]{4,3,2,1,0:T(8,128)}, f32[36,5,2,8,256]{4,3,2,1,0:T(8,128)}, u32[]{:S(2)}, u32[]{:S(2)}) collective-permute-start(f32[36,5,2,8,256]{4,3,2,1,0:T(8,128)} %get-tuple-element.108), channel_id=1, source_target_pairs={{0,64},{64,0},{1,65},{65,1},{2,66},{66,2},{3,67},{67,3},{4,68},{68... | collective-permute-start | bytes 8847368 | tf_op jit(solution)/shard_map/ppermute | solution.py:533
  120.9 9.3 %collective-permute-start.9 = (f32[36,5,2,8,256]{4,3,2,1,0:T(8,128)}, f32[36,5,2,8,256]{4,3,2,1,0:T(8,128)}, u32[]{:S(2)}, u32[]{:S(2)}) collective-permute-start(f32[36,5,2,8,256]{4,3,2,1,0:T(8,128)} %get-tuple-element.107), channel_id=1, source_target_pairs={{0,64},{64,0},{1,65},{65,1},{2,66},{66,2},{3,67},{67,3},{4,68},{68... | collective-permute-start | bytes 8847368 | tf_op jit(solution)/shard_map/ppermute | solution.py:533
  128.4 12.3 %collective-permute-start.8 = (f32[36,5,2,8,256]{4,3,2,1,0:T(8,128)}, f32[36,5,2,8,256]{4,3,2,1,0:T(8,128)}, u32[]{:S(2)}, u32[]{:S(2)}) collective-permute-start(f32[36,5,2,8,256]{4,3,2,1,0:T(8,128)} %get-tuple-element.98), channel_id=1, source_target_pairs={{0,64},{64,0},{1,65},{65,1},{2,66},{66,2},{3,67},{67,3},{4,68},{68... | collective-permute-start | bytes 8847368 | tf_op jit(solution)/shard_map/ppermute | solution.py:533

commit v6 on v5

--- a/solution.py
+++ b/solution.py
@@ -22,7 +22,7 @@
 GAP = 16
 MIB = 1024 * 1024
 FIRST_CUTS = (640,)
-REST_CUTS = (984,)
+REST_CUTS = (512, 984)
 FULL_CUTS = (3072 + 64,)
 GROUPS = SNAPS // 8
 F32 = jnp.float32
@@ -434,7 +434,7 @@
             pltpu.SemaphoreType.DMA((GROUPS,)),
             pltpu.SemaphoreType.DMA((max(chunks, 1),)),
         ],
-        compiler_params=pltpu.CompilerParams(vmem_limit_bytes=62 * MIB),
+        compiler_params=pltpu.CompilerParams(vmem_limit_bytes=62 * MIB if level == 0 else 12 * MIB + 16 * WIDTH * sum(rooms)),
         name="finish_level",
     )(meta, plan, *[part[0] for part in parts], *[part[1][level] for part in parts], *packs)
 
@@ -490,7 +490,7 @@
         out_shape=[jax.ShapeDtypeStruct((HALF, 2, ROWS, WIDTH), F32), jax.ShapeDtypeStruct((HALF, 3, ROWS, WIDTH), F32)],
         scratch_shapes=[buffer, buffer, pltpu.SemaphoreType.DMA((2 * parts,)), pltpu.SemaphoreType.DMA((4 * parts,))],
         input_output_aliases={2 + 2 * many: 0, 3 + 2 * many: 1} if before else {},
-        compiler_params=pltpu.CompilerParams(vmem_limit_bytes=62 * MIB),
+        compiler_params=pltpu.CompilerParams(vmem_limit_bytes=(2 + 6 * many) * MIB),
         name="scale_levels",
     )(*counts, *[pair[0] for pair in pairs], *[pair[1] for pair in pairs], *before)
 
@@ -583,13 +583,22 @@
     message = jnp.broadcast_to(jnp.concatenate([own, plan[8:], jnp.zeros((48,), I32)])[None], (8, 128))
     strips_b, sums, up_b, dn_b, pos_b, _ = smooth(1, meta, plan, cuts=REST_CUTS, early=(strips_a[3],))
     below_b, above_b, other, reply = exchange(up_b[0], dn_b[0], sums[1], message)
+    (up_b, dn_b), here, below_b, above_b, other = lax.optimization_barrier(((up_b[1], dn_b[1]), meta, below_b, above_b, other))
+    more = send([up_b], [dn_b])
     counts = (message, reply)
     over = jnp.max(jnp.maximum(message, reply)[0:1, PHASES:PHASES + 8])
-    parts = [(pos_a, strips_a, FIRST_CUTS, below_a, above_a), (pos_b, strips_b, REST_CUTS, [below_b], [above_b])]
-    totals = [finish_level(level, meta, plan, parts) for level in range(3)]
-    totals = [(sums[0], other)] + [(mine, to_partner(theirs)) for mine, theirs in totals]
-    before = scale_levels((3, 0, 1), counts, totals[:3], ())
-    return lax.cond(over <= 0, last, full, counts, *totals[3], *before)
+    parts = [(pos_a, strips_a, FIRST_CUTS, below_a, above_a),
+             (pos_b, strips_b, REST_CUTS, [below_b, *more[0]], [above_b, *more[1]])]
+    totals = [finish_level(0, here, plan, parts)]
+    totals[0], other = lax.optimization_barrier((tuple(totals[0]), other))
+    before = scale_levels((3,), counts, [(sums[0], other)], ())
+    totals[0] = (totals[0][0], to_partner(totals[0][1]))
+    before = scale_levels((0,), counts, totals[:1], before)
+    here, before = lax.optimization_barrier((here, tuple(before)))
+    totals = [finish_level(level, here, plan, parts) for level in (1, 2)]
+    totals = [(mine, to_partner(theirs)) for mine, theirs in totals]
+    before = scale_levels((1,), counts, totals[:1], before)
+    return lax.cond(over <= 0, last, full, counts, *totals[1], *before)
 
 
 def solution(mesh):

time: 146 us -> 151 us (1.034)
  Pallas kernels: 128 us -> 108 us
  waiting for transfers between devices: 0.01 us -> 14.5 us
  starting transfers between devices: 11.1 us -> 18.4 us
  local copies, waits for them, and re-layouts: 3.07 us -> 6.72 us
    pallas_call x1, Pallas kernels: 53 us -> 32.7 us  [exchange(): pl.pallas_call(exchange_kernel, in_specs=[any_space] * 4, out_specs=[any_...]
    ppermute x1 -> x2, waiting for transfers between devices: 0.01 us -> 8.48 us  [to_above(): return lax.ppermute(value, 'tile', [(i + 1, i) for i in range(size - 1)])]
    ppermute x1 -> x2, waiting for transfers between devices: 0.01 us -> 5.93 us  [to_below(): return lax.ppermute(value, 'tile', [(i, i + 1) for i in range(size - 1)])]
    unnamed x4 -> x30, local copies, waits for them, and re-layouts: 1.06 us -> 4.74 us
    ppermute x1 -> x2, starting transfers between devices: 1.92 us -> 5.18 us  [to_below(): return lax.ppermute(value, 'tile', [(i, i + 1) for i in range(size - 1)])]
    ppermute x1 -> x2, starting transfers between devices: 6.67 us -> 8.69 us  [to_above(): return lax.ppermute(value, 'tile', [(i + 1, i) for i in range(size - 1)])]
    ppermute x3, starting transfers between devices: 2.55 us -> 4.51 us  [to_partner(): return lax.ppermute(value, 'snap', [(0, 1), (1, 0)])]
    pallas_call x2 -> x4, Pallas kernels: 15.3 us -> 16.6 us  [scale_levels(): pl.pallas_call(functools.partial(scale_kernel, levels, block), in_specs=[...]
  transfers between devices with their start and end apart: 5 -> 7, of which waited for: 0 -> 3; matrix products, arithmetic and copies ran while one was open for 1% -> 1% of each run, Pallas kernels for 70% -> 48%
where the time goes in v6:
time: 151 us
  Pallas kernels  108 us (72%)
  starting transfers between devices  18.4 us (12%)
  waiting for transfers between devices  14.5 us (10%)
  local copies, waits for them, and re-layouts  6.72 us (4%)
  between operations  1.75 us (1%)
  other arithmetic  1.57 us (1%)
    pallas_call x2, Pallas kernels, smooth_part(): pl.pallas_call(functools.partial(smooth_kernel, part, cuts), in_specs=[sm...  37.1 us
    pallas_call x1, Pallas kernels, exchange(): pl.pallas_call(exchange_kernel, in_specs=[any_space] * 4, out_specs=[any_...  32.7 us
    pallas_call x3, Pallas kernels, finish_level(): pl.pallas_call(functools.partial(finish_kernel, level, cuts), in_specs=[s...  21.3 us
    pallas_call x4, Pallas kernels, scale_levels(): pl.pallas_call(functools.partial(scale_kernel, levels, block), in_specs=[...  16.6 us
    ppermute x2, starting transfers between devices, to_above(): return lax.ppermute(value, 'tile', [(i + 1, i) for i in range(size - 1)])  8.69 us
    ppermute x2, waiting for transfers between devices, to_above(): return lax.ppermute(value, 'tile', [(i + 1, i) for i in range(size - 1)])  8.48 us
    ppermute x2, waiting for transfers between devices, to_below(): return lax.ppermute(value, 'tile', [(i, i + 1) for i in range(size - 1)])  5.93 us
    ppermute x2, starting transfers between devices, to_below(): return lax.ppermute(value, 'tile', [(i, i + 1) for i in range(size - 1)])  5.18 us
  transfers between devices with their start and end apart: 7, of which 3 were waited for; matrix products, arithmetic and copies ran while one was open for 1% of the time, Pallas kernels for 48%

profile of v6, /device:TPU:97, one launch (start us, length us, event | category | flops | bytes accessed | tf_op | source)
XLA Modules:
  0.0 150.8 jit_solution(8219454582747285894)
XLA Ops:
  0.6 0.8 slice_bitcast_fusion.1
  1.4 0.7 subtract_remainder_fusion
  2.1 0.5 broadcast_4_plan.2.plan
  2.6 15.6 %smooth_part.4 = (f32[128,2,2,8,256]{4,3,2,1,0:T(8,128)}, f32[128,2,2,8,256]{4,3,2,1,0:T(8,128)}, f32[128,2,2,8,256]{4,3,2,1,0:T(8,128)}, f32[128,2,2,8,256]{4,3...) custom-call(s32[385]{0:T(512)S(1)} %pad_add_fusion.meta, ...), custom_call_target="tpu_custom_call" | custom-call | tf_op jit(solution)/shard_map/smooth_part/pallas_call | solution.py:305
  18.2 6.7 %collective-permute-start.6 = (f32[2,640,256]{2,1,0:T(8,128)}, f32[2,640,256]{2,1,0:T(8,128)S(1)}, u32[]{:S(2)}, u32[]{:S(2)}) collective-permute-start(f32[2,640,256]{2,1,0:T(8,128)} %get-tuple-element.117), channel_id=1, source_target_pairs={{1,0},{2,1},{3,2},{4,3},{5,4},{6,5},{7,6},{8,7},{9,8},{10,9},{11,1... | collective-permute-start | bytes 3932168 | tf_op jit(solution)/shard_map/ppermute | solution.py:538
  24.8 1.9 %collective-permute-start.7 = (f32[2,640,256]{2,1,0:T(8,128)}, f32[2,640,256]{2,1,0:T(8,128)}, u32[]{:S(2)}, u32[]{:S(2)}) collective-permute-start(f32[2,640,256]{2,1,0:T(8,128)} %get-tuple-element.118), channel_id=1, source_target_pairs={{0,1},{1,2},{2,3},{3,4},{4,5},{5,6},{6,7},{7,8},{8,9},{9,10},{10,1... | collective-permute-start | bytes 3932168 | tf_op jit(solution)/shard_map/ppermute | solution.py:543
  26.8 0.7 slice.14
  27.5 0.0 copy-done.20
  27.5 21.5 %smooth_part.5 = (f32[128,2,2,8,256]{4,3,2,1,0:T(8,128)}, f32[128,2,2,8,256]{4,3,2,1,0:T(8,128)}, f32[128,2,2,8,256]{4,3,2,1,0:T(8,128)}, f32[36,5,2,8,256]{4,3,...) custom-call(s32[385]{0:T(512)S(1)} %pad_add_fusion.meta, ...), custom_call_target="tpu_custom_call" | custom-call | tf_op jit(solution)/shard_map/smooth_part/pallas_call | solution.py:305
  49.0 0.1 convert_reduce_fusion
  49.1 0.1 pad_add_fusion.1
  49.2 32.7 %exchange.1 = (f32[2,512,256]{2,1,0:T(8,128)}, f32[2,512,256]{2,1,0:T(8,128)}, f32[36,5,2,8,256]{4,3,2,1,0:T(8,128)}, s32[8,128]{1,0:T(8,128)S(1)}) custom-call(f32[2,512,256]{2,1,0:T(8,128)} %get-tuple-element.103.up, f32[2,512,256]{2,1,0:T(8,128)} %get-tuple-element.104.dn, f32[36,5,2,8,256]{4,3,2,1,0:T(8,128)} %get-tuple-element.105.theirs, ...), custom_call_target="tpu_custom_call" | custom-call | tf_op jit(solution)/shard_map/exchange/pallas_call | solution.py:521
  81.9 0.0 collective-permute-done.6.refs_4_
  81.9 0.0 copy-start
  81.9 0.0 collective-permute-done.7.refs_5_
  81.9 1.0 copy-done
  83.0 7.6 %finish_level.9 = (f32[36,5,2,8,256]{4,3,2,1,0:T(8,128)}, f32[36,5,2,8,256]{4,3,2,1,0:T(8,128)}) custom-call(s32[385]{0:T(512)S(1)} %pad_add_fusion.meta, s32[16]{0:T(128)} %get-tuple-element.101.plan, s32[768]{0:T(1024)} %get-tuple-element.113.refs_0_, s32[768]{0:T(1024)} %get-tuple-element.114.refs_1_, f32[128,2,2,8,256]{4,3,2,1,0:T(8,128)} %get-tuple-element.115.refs_2_, ...), custom_call_target="tpu_custom_call" | custom-call | tf_op jit(solution)/shard_map/finish_level/pallas_call | solution.py:425
  90.5 3.1 %collective-permute-start.8 = (f32[36,5,2,8,256]{4,3,2,1,0:T(8,128)}, f32[36,5,2,8,256]{4,3,2,1,0:T(8,128)S(1)}, u32[]{:S(2)}, u32[]{:S(2)}) collective-permute-start(f32[36,5,2,8,256]{4,3,2,1,0:T(8,128)} %get-tuple-element.125), channel_id=1, source_target_pairs={{0,64},{64,0},{1,65},{65,1},{2,66},{66,2},{3,67},{67,3},{4,68},{68... | collective-permute-start | bytes 8847368 | tf_op jit(solution)/shard_map/ppermute | solution.py:533
  93.6 2.0 %collective-permute-start.9 = (f32[2,472,256]{2,1,0:T(8,128)}, f32[2,472,256]{2,1,0:T(8,128)S(1)}, u32[]{:S(2)}, u32[]{:S(2)}) collective-permute-start(f32[2,472,256]{2,1,0:T(8,128)} %get-tuple-element.135), channel_id=1, source_target_pairs={{1,0},{2,1},{3,2},{4,3},{5,4},{6,5},{7,6},{8,7},{9,8},{10,9},{11,1... | collective-permute-start | bytes 2899976 | tf_op jit(solution)/shard_map/ppermute | solution.py:538
  95.7 3.3 %collective-permute-start.10 = (f32[2,472,256]{2,1,0:T(8,128)}, f32[2,472,256]{2,1,0:T(8,128)S(1)}, u32[]{:S(2)}, u32[]{:S(2)}) collective-permute-start(f32[2,472,256]{2,1,0:T(8,128)} %get-tuple-element.136), channel_id=1, source_target_pairs={{0,1},{1,2},{2,3},{3,4},{4,5},{5,6},{6,7},{7,8},{8,9},{9,10},{10,1... | collective-permute-start | bytes 2899976 | tf_op jit(solution)/shard_map/ppermute | solution.py:543
  98.9 0.0 copy-start.11
  98.9 1.8 %copy-done.11 = f32[36,5,2,8,256]{4,3,2,1,0:T(8,128)S(1)} copy-done((f32[36,5,2,8,256]{4,3,2,1,0:T(8,128)S(1)}, f32[36,5,2,8,256]{4,3,2,1,0:T(8,128)}, u32[]{:S(2)}) %copy-start.11) | copy-done | bytes 2949144
  100.8 1.8 %copy-done.13 = f32[36,5,2,8,256]{4,3,2,1,0:T(8,128)S(1)} copy-done((f32[36,5,2,8,256]{4,3,2,1,0:T(8,128)S(1)}, f32[36,5,2,8,256]{4,3,2,1,0:T(8,128)}, u32[]{:S(2)}) %copy-start.13) | copy-done | bytes 2949144
  102.6 3.8 %scale_levels.9 = (f32[36,2,64,256]{3,2,1,0:T(8,128)}, f32[36,3,64,256]{3,2,1,0:T(8,128)}) custom-call(s32[8,128]{1,0:T(8,128)S(1)} %broadcast_in_dim.16.message, s32[8,128]{1,0:T(8,128)S(1)} %get-tuple-element.106.reply, f32[36,5,2,8,256]{4,3,2,1,0:T(8,128)S(1)} %copy-done.11, f32[36,5,2,8,256]{4,3,2,1,0:T(8,128)S(1)} %copy-done.13), custom_call_target="tpu_custom_call" | custom-call | tf_op jit(solution)/shard_map/scale_levels/pallas_call | solution.py:486
  106.4 0.0 collective-permute-done.8.refs_1_
  106.4 0.0 copy-done.14
  106.4 0.0 copy-start.1
  106.4 0.0 copy-start.2
  106.4 0.0 copy-start.3
  106.4 0.0 copy-start.5
  106.4 0.0 copy-start.7
  106.4 0.0 copy-start.15
  106.5 0.0 copy-start.16
  106.5 0.0 copy-start.18
  106.5 3.8 %scale_levels.10 = (f32[36,2,64,256]{3,2,1,0:T(8,128)}, f32[36,3,64,256]{3,2,1,0:T(8,128)}) custom-call(s32[8,128]{1,0:T(8,128)S(1)} %broadcast_in_dim.16.message, s32[8,128]{1,0:T(8,128)S(1)} %get-tuple-element.106.reply, f32[36,5,2,8,256]{4,3,2,1,0:T(8,128)S(1)} %copy-done.14, ...), custom_call_target="tpu_custom_call", output_to_operand_aliasing={{0}: (4, {}), {1}: (5, {})} | custom-call | tf_op jit(solution)/shard_map/scale_levels/pallas_call | solution.py:486
  110.3 8.5 %collective-permute-done.9.refs_7_ = f32[2,472,256]{2,1,0:T(8,128)S(1)} collective-permute-done((f32[2,472,256]{2,1,0:T(8,128)}, f32[2,472,256]{2,1,0:T(8,128)S(1)}, u32[]{:S(2)}, u32[]{:S(2)}) %collective-permute-start.9) | collective-permute-done | bytes 966688 | tf_op jit(solution)/shard_map/ppermute | solution.py:538
  118.7 5.9 %collective-permute-done.10.refs_9_ = f32[2,472,256]{2,1,0:T(8,128)S(1)} collective-permute-done((f32[2,472,256]{2,1,0:T(8,128)}, f32[2,472,256]{2,1,0:T(8,128)S(1)}, u32[]{:S(2)}, u32[]{:S(2)}) %collective-permute-start.10) | collective-permute-done | bytes 966688 | tf_op jit(solution)/shard_map/ppermute | solution.py:543
  124.7 0.0 copy-done.1
  124.8 6.7 %finish_level.11 = (f32[36,5,2,8,256]{4,3,2,1,0:T(8,128)S(1)}, f32[36,5,2,8,256]{4,3,2,1,0:T(8,128)}) custom-call(s32[385]{0:T(512)S(1)} %pad_add_fusion.meta, s32[16]{0:T(128)S(1)} %copy-done.18, s32[768]{0:T(1024)S(1)} %copy-done.15, s32[768]{0:T(1024)S(1)} %copy-done.16, f32[128,2,2,8,256]{4,3,2,1,0:T(8,128)S(1)} %copy-done.5, ...), custom_call_target="tpu_custom_call" | custom-call | tf_op jit(solution)/shard_map/finish_level/pallas_call | solution.py:425
  131.4 1.3 collective-permute-start.12
  132.7 7.1 %finish_level.10 = (f32[36,5,2,8,256]{4,3,2,1,0:T(8,128)}, f32[36,5,2,8,256]{4,3,2,1,0:T(8,128)}) custom-call(s32[385]{0:T(512)S(1)} %pad_add_fusion.meta, s32[16]{0:T(128)S(1)} %copy-done.18, s32[768]{0:T(1024)S(1)} %copy-done.15, s32[768]{0:T(1024)S(1)} %copy-done.16, f32[128,2,2,8,256]{4,3,2,1,0:T(8,128)S(1)} %copy-done.4, ...), custom_call_target="tpu_custom_call" | custom-call | tf_op jit(solution)/shard_map/finish_level/pallas_call | solution.py:425
  139.8 0.1 collective-permute-start.11
  139.9 0.7 slice_reduce_fusion
  141.3 0.0 collective-permute-done.12.refs_1_
  141.3 4.3 %scale_levels.11 = (f32[36,2,64,256]{3,2,1,0:T(8,128)}, f32[36,3,64,256]{3,2,1,0:T(8,128)}) custom-call(s32[8,128]{1,0:T(8,128)S(1)} %broadcast_in_dim.16.message, s32[8,128]{1,0:T(8,128)S(1)} %get-tuple-element.106.reply, f32[36,5,2,8,256]{4,3,2,1,0:T(8,128)S(1)} %get-tuple-element.141.refs_0_, ...), custom_call_target="tpu_custom_call", output_to_operand_aliasing={{0}: (4, {}), {1}: (5, {})} | custom-call | tf_op jit(solution)/shard_map/scale_levels/pallas_call | solution.py:486
  145.6 0.1 collective-permute-done.11
  145.6 5.0 %conditional.1 = ((f32[36,2,64,256]{3,2,1,0:T(8,128)}, f32[36,3,64,256]{3,2,1,0:T(8,128)})) conditional(s32[]{:T(128)} %convert_element_type.7, (s32[385]{0:T(512)S(1)}, f32[128,2,64,256]{3,2,1,0:T(8,128)}, bf16[768,256]{1,0:T(8,128)(2,1)S(1)}, bf16[3,33,112,192]{3,2,1,0:T(8,128)(2,1)}, s32[8,128]{1,0:T(8,128)S(1)}, ...), branch_computations={%region_2.3_spmd, %region_3.4_spmd} | conditional | bytes 155726560 | solution.py:601
  145.8 4.8 %scale_levels.8 = (f32[36,2,64,256]{3,2,1,0:T(8,128)}, f32[36,3,64,256]{3,2,1,0:T(8,128)}) custom-call(s32[8,128]{1,0:T(8,128)S(1)} %get-tuple-element.47.message, s32[8,128]{1,0:T(8,128)S(1)} %get-tuple-element.48.reply, f32[36,5,2,8,256]{4,3,2,1,0:T(8,128)} %get-tuple-element.49.refs_0_, ...), custom_call_target="tpu_custom_call", output_to_operand_aliasing={{0}: (4, {}), {1}: (5, {})} | custom-call | tf_op jit(solution)/shard_map/cond/branch_1_fun/scale_levels/pallas_call | solution.py:486
  (18 shorter events, 0.0 us)
Async XLA Ops:
  2.6 24.9 %copy-start.20 = (bf16[768,256]{1,0:T(8,128)(2,1)S(1)}, bf16[768,256]{1,0:T(8,128)(2,1)}, u32[]{:S(2)}) copy-start(bf16[768,256]{1,0:T(8,128)(2,1)} %constant.31.clone.refs_1_) | copy-start | bytes 1179652
  18.2 63.8 %collective-permute-start.6 = (f32[2,640,256]{2,1,0:T(8,128)}, f32[2,640,256]{2,1,0:T(8,128)S(1)}, u32[]{:S(2)}, u32[]{:S(2)}) collective-permute-start(f32[2,640,256]{2,1,0:T(8,128)} %get-tuple-element.117), channel_id=1, source_target_pairs={{1,0},{2,1},{3,2},{4,3},{5,4},{6,5},{7,6},{8,7},{9,8},{10,9},{11,1... | collective-permute-start | bytes 3932168 | tf_op jit(solution)/shard_map/ppermute | solution.py:538
  24.8 57.1 %collective-permute-start.7 = (f32[2,640,256]{2,1,0:T(8,128)}, f32[2,640,256]{2,1,0:T(8,128)}, u32[]{:S(2)}, u32[]{:S(2)}) collective-permute-start(f32[2,640,256]{2,1,0:T(8,128)} %get-tuple-element.118), channel_id=1, source_target_pairs={{0,1},{1,2},{2,3},{3,4},{4,5},{5,6},{6,7},{7,8},{8,9},{9,10},{10,1... | collective-permute-start | bytes 3932168 | tf_op jit(solution)/shard_map/ppermute | solution.py:543
  81.9 1.1 copy-start
  90.5 15.8 %collective-permute-start.8 = (f32[36,5,2,8,256]{4,3,2,1,0:T(8,128)}, f32[36,5,2,8,256]{4,3,2,1,0:T(8,128)S(1)}, u32[]{:S(2)}, u32[]{:S(2)}) collective-permute-start(f32[36,5,2,8,256]{4,3,2,1,0:T(8,128)} %get-tuple-element.125), channel_id=1, source_target_pairs={{0,64},{64,0},{1,65},{65,1},{2,66},{66,2},{3,67},{67,3},{4,68},{68... | collective-permute-start | bytes 8847368 | tf_op jit(solution)/shard_map/ppermute | solution.py:533
  93.6 25.1 %collective-permute-start.9 = (f32[2,472,256]{2,1,0:T(8,128)}, f32[2,472,256]{2,1,0:T(8,128)S(1)}, u32[]{:S(2)}, u32[]{:S(2)}) collective-permute-start(f32[2,472,256]{2,1,0:T(8,128)} %get-tuple-element.135), channel_id=1, source_target_pairs={{1,0},{2,1},{3,2},{4,3},{5,4},{6,5},{7,6},{8,7},{9,8},{10,9},{11,1... | collective-permute-start | bytes 2899976 | tf_op jit(solution)/shard_map/ppermute | solution.py:538
  95.7 29.0 %collective-permute-start.10 = (f32[2,472,256]{2,1,0:T(8,128)}, f32[2,472,256]{2,1,0:T(8,128)S(1)}, u32[]{:S(2)}, u32[]{:S(2)}) collective-permute-start(f32[2,472,256]{2,1,0:T(8,128)} %get-tuple-element.136), channel_id=1, source_target_pairs={{0,1},{1,2},{2,3},{3,4},{4,5},{5,6},{6,7},{7,8},{8,9},{9,10},{10,1... | collective-permute-start | bytes 2899976 | tf_op jit(solution)/shard_map/ppermute | solution.py:543
  98.9 1.8 %copy-start.11 = (f32[36,5,2,8,256]{4,3,2,1,0:T(8,128)S(1)}, f32[36,5,2,8,256]{4,3,2,1,0:T(8,128)}, u32[]{:S(2)}) copy-start(f32[36,5,2,8,256]{4,3,2,1,0:T(8,128)} %get-tuple-element.126.refs_0_) | copy-start | bytes 8847364
  100.8 1.8 %copy-start.13 = (f32[36,5,2,8,256]{4,3,2,1,0:T(8,128)S(1)}, f32[36,5,2,8,256]{4,3,2,1,0:T(8,128)}, u32[]{:S(2)}) copy-start(f32[36,5,2,8,256]{4,3,2,1,0:T(8,128)} %get-tuple-element.127.refs_1_) | copy-start | bytes 8847364
  102.6 3.8 %copy-start.14 = (f32[36,5,2,8,256]{4,3,2,1,0:T(8,128)S(1)}, f32[36,5,2,8,256]{4,3,2,1,0:T(8,128)}, u32[]{:S(2)}) copy-start(f32[36,5,2,8,256]{4,3,2,1,0:T(8,128)} %get-tuple-element.124.refs_0_) | copy-start | bytes 8847364
  106.4 18.3 %copy-start.1 = (f32[2,640,256]{2,1,0:T(8,128)S(1)}, f32[2,640,256]{2,1,0:T(8,128)}, u32[]{:S(2)}) copy-start(f32[2,640,256]{2,1,0:T(8,128)} %copy-done) | copy-start | bytes 3932164
  106.4 18.3 %copy-start.2 = (f32[2,512,256]{2,1,0:T(8,128)S(1)}, f32[2,512,256]{2,1,0:T(8,128)}, u32[]{:S(2)}) copy-start(f32[2,512,256]{2,1,0:T(8,128)} %get-tuple-element.119.refs_6_) | copy-start | bytes 3145732
  106.4 18.3 %copy-start.3 = (f32[2,512,256]{2,1,0:T(8,128)S(1)}, f32[2,512,256]{2,1,0:T(8,128)}, u32[]{:S(2)}) copy-start(f32[2,512,256]{2,1,0:T(8,128)} %get-tuple-element.120.refs_7_.refs_8_) | copy-start | bytes 3145732
  106.4 18.3 %copy-start.5 = (f32[128,2,2,8,256]{4,3,2,1,0:T(8,128)S(1)}, f32[128,2,2,8,256]{4,3,2,1,0:T(8,128)}, u32[]{:S(2)}) copy-start(f32[128,2,2,8,256]{4,3,2,1,0:T(8,128)} %get-tuple-element.139.refs_2_) | copy-start | bytes 12582916
  106.4 18.3 %copy-start.7 = (f32[128,2,2,8,256]{4,3,2,1,0:T(8,128)S(1)}, f32[128,2,2,8,256]{4,3,2,1,0:T(8,128)}, u32[]{:S(2)}) copy-start(f32[128,2,2,8,256]{4,3,2,1,0:T(8,128)} %get-tuple-element.140.refs_3_) | copy-start | bytes 12582916
  106.4 18.3 %copy-start.15 = (s32[768]{0:T(1024)S(1)}, s32[768]{0:T(1024)}, u32[]{:S(2)}) copy-start(s32[768]{0:T(1024)} %get-tuple-element.113.refs_0_) | copy-start | bytes 9220
  106.5 18.3 %copy-start.16 = (s32[768]{0:T(1024)S(1)}, s32[768]{0:T(1024)}, u32[]{:S(2)}) copy-start(s32[768]{0:T(1024)} %get-tuple-element.114.refs_1_) | copy-start | bytes 9220
  106.5 18.3 %copy-start.18 = (s32[16]{0:T(128)S(1)}, s32[16]{0:T(128)}, u32[]{:S(2)}) copy-start(s32[16]{0:T(128)} %get-tuple-element.101.plan) | copy-start | bytes 196
  124.7 8.0 %copy-start.4 = (f32[128,2,2,8,256]{4,3,2,1,0:T(8,128)S(1)}, f32[128,2,2,8,256]{4,3,2,1,0:T(8,128)}, u32[]{:S(2)}) copy-start(f32[128,2,2,8,256]{4,3,2,1,0:T(8,128)} %get-tuple-element.133.refs_2_) | copy-start | bytes 12582916
  124.7 8.0 %copy-start.6 = (f32[128,2,2,8,256]{4,3,2,1,0:T(8,128)S(1)}, f32[128,2,2,8,256]{4,3,2,1,0:T(8,128)}, u32[]{:S(2)}) copy-start(f32[128,2,2,8,256]{4,3,2,1,0:T(8,128)} %get-tuple-element.134.refs_3_) | copy-start | bytes 12582916
  131.4 9.8 %collective-permute-start.12 = (f32[36,5,2,8,256]{4,3,2,1,0:T(8,128)}, f32[36,5,2,8,256]{4,3,2,1,0:T(8,128)}, u32[]{:S(2)}, u32[]{:S(2)}) collective-permute-start(f32[36,5,2,8,256]{4,3,2,1,0:T(8,128)} %get-tuple-element.142), channel_id=1, source_target_pairs={{0,64},{64,0},{1,65},{65,1},{2,66},{66,2},{3,67},{67,3},{4,68},{68... | collective-permute-start | bytes 8847368 | tf_op jit(solution)/shard_map/ppermute | solution.py:533
  139.8 5.8 %collective-permute-start.11 = (f32[36,5,2,8,256]{4,3,2,1,0:T(8,128)}, f32[36,5,2,8,256]{4,3,2,1,0:T(8,128)}, u32[]{:S(2)}, u32[]{:S(2)}) collective-permute-start(f32[36,5,2,8,256]{4,3,2,1,0:T(8,128)} %get-tuple-element.138), channel_id=1, source_target_pairs={{0,64},{64,0},{1,65},{65,1},{2,66},{66,2},{3,67},{67,3},{4,68},{68... | collective-permute-start | bytes 8847368 | tf_op jit(solution)/shard_map/ppermute | solution.py:533

commit v7 on v5

--- a/solution.py
+++ b/solution.py
@@ -19,10 +19,12 @@
 EXT = ROWS + 2 * HALO
 GROUP = 8
 CHUNK = 128
+BLOCK = 18
+SPLIT = 6
 GAP = 16
 MIB = 1024 * 1024
 FIRST_CUTS = (640,)
-REST_CUTS = (984,)
+REST_CUTS = (1008,)
 FULL_CUTS = (3072 + 64,)
 GROUPS = SNAPS // 8
 F32 = jnp.float32
@@ -330,25 +332,26 @@
     return out[:strips], out[strips:strips + sums], packs[:pieces], packs[pieces:2 * pieces], out[-2], out[-1]
 
 
-def finish_kernel(level, cuts, meta, plan, *refs):
-    parts = len(cuts)
-    pos_refs, strips, refs = refs[:parts], refs[parts:2 * parts], refs[2 * parts:]
+def finish_kernel(levels, cuts, meta, plan, *refs):
+    parts, many = len(cuts), len(levels)
+    pos_refs, refs = refs[:parts], refs[parts:]
+    strips, refs = [refs[many * k:many * (k + 1)] for k in range(parts)], refs[many * parts:]
     pieces = []
     for k in range(parts):
-        many = len(cuts[k])
-        pieces.append((refs[:many], refs[many:2 * many]))
-        refs = refs[2 * many:]
-    mine, theirs, acc, y_buf, *refs = refs
-    buffers, (y_sem, sem) = refs[:-2], refs[-2:]
+        count = len(cuts[k])
+        pieces.append((refs[:count], refs[count:2 * count]))
+        refs = refs[2 * count:]
+    outs, refs = refs[:2 * many], refs[2 * many:]
+    acc, y_buf, *buffers, y_sem, out_sem, sem = refs
     middle = plan[6] if parts == 2 else I32(GROUPS)
     ranges = [(I32(0), middle), (middle, I32(GROUPS))][:parts]
 
     def loop(low, high, body):
         lax.fori_loop(low, high, lambda g, carry: (body(g), carry)[1], 0)
 
-    def load(k, g):
+    def load(k, g, at):
         rows = pl.ds(GROUP * g, GROUP)
-        return pltpu.make_async_copy(strips[k].at[rows], y_buf.at[rows], y_sem.at[g])
+        return pltpu.make_async_copy(strips[k][at].at[rows], y_buf.at[at, rows], y_sem.at[at, g])
 
     packs = [[] for _ in range(parts)]
     total = 0
@@ -357,9 +360,8 @@
         first, last = ranges[k]
         for piece, high in enumerate(cuts[k]):
             for side in range(2):
-                slot = 3 * side + level
-                begin = pos_refs[k][6 * GROUP * jnp.minimum(first, GROUPS - 1) + slot]
-                end = pos_refs[k][6 * (GROUP * jnp.maximum(last, 1) - 1) + slot] + 16
+                begin = pos_refs[k][6 * GROUP * jnp.minimum(first, GROUPS - 1) + 3 * side + levels[0]]
+                end = pos_refs[k][6 * (GROUP * jnp.maximum(last, 1) - 1) + 3 * side + levels[-1]] + 16
                 for row_at in range(low, high, CHUNK):
                     stop = min(row_at + CHUNK, high)
                     copy = pltpu.make_async_copy(
@@ -368,82 +370,86 @@
                     total += 1
                     packs[k].append((copy, (first < last) & (begin < stop) & (end > row_at)))
             low = high
-    for k in range(parts):
-        for copy, needed in packs[k]:
-            pl.when(needed)(copy.start)
-        loop(*ranges[k], lambda g, k=k: load(k, g).start())
-    acc[...] = jnp.zeros_like(acc)
+    for at in range(many):
+        for k in range(parts):
+            if at == 0:
+                for copy, needed in packs[k]:
+                    pl.when(needed)(copy.start)
+            loop(*ranges[k], lambda g, k=k, at=at: load(k, g, at).start())
     row = lax.broadcasted_iota(I32, (8, WIDTH), 0)
 
-    def one(n, k):
+    def one(n, k, at):
         phase = meta[2 * SNAPS + n]
         for place in range(2):
-            fields = [y_buf[n, place, comp] for comp in range(2)]
-            if cuts[k]:
-                side = 1 - place
-                have = level_rows(needs(meta[n])[side], level)
-                pos = pos_refs[k][6 * n + 3 * side + level]
-                skew = pos & 7
-                base = pl.multiple_of(pos - skew, 8)
-                turn = skew if place == 0 else (skew + have) & 7
-                known = jnp.where(meta[3 * SNAPS] == 2 * place, 0, have)
-                keep = row < known if place == 0 else row >= 8 - known
-                for comp in range(2):
-                    lower = buffers[2 * k + side][comp, pl.ds(base, 8)]
-                    upper = buffers[2 * k + side][comp, pl.ds(base + 8, 8)]
-                    tile = pltpu.roll(jnp.where(row >= skew, lower, upper), (8 - turn) & 7, 0)
-                    fields[comp] += jnp.where(keep, tile, 0.0)
+            side = 1 - place
+            have = level_rows(needs(meta[n])[side], levels[at])
+            pos = pos_refs[k][6 * n + 3 * side + levels[at]]
+            skew = pos & 7
+            base = pl.multiple_of(pos - skew, 8)
+            turn = skew if place == 0 else (skew + have) & 7
+            known = jnp.where(meta[3 * SNAPS] == 2 * place, 0, have)
+            keep = row < known if place == 0 else row >= 8 - known
+            fields = []
+            for comp in range(2):
+                lower = buffers[2 * k + side][comp, pl.ds(base, 8)]
+                upper = buffers[2 * k + side][comp, pl.ds(base + 8, 8)]
+                tile = pltpu.roll(jnp.where(row >= skew, lower, upper), (8 - turn) & 7, 0)
+                fields.append(y_buf[at, n, place, comp] + jnp.where(keep, tile, 0.0))
             u, v = fields
             for at_field, field in enumerate((u, v, u * u, v * v, u * v)):
-                acc[phase, at_field, place] += field
-
-    def group(g, k):
-        load(k, g).wait()
+                acc[at, phase, at_field, place] += field
+
+    def group(g, k, at):
+        load(k, g, at).wait()
         for b in range(GROUP):
-            one(GROUP * g + b, k)
-
-    for k in range(parts):
-        for copy, needed in packs[k]:
-            pl.when(needed)(copy.wait)
-        loop(*ranges[k], lambda g, k=k: group(g, k))
-    stores = [pltpu.make_async_copy(acc.at[HALF:PHASES], theirs, y_sem.at[0]),
-              pltpu.make_async_copy(acc.at[0:HALF], mine, y_sem.at[1])]
-    for copy in stores:
-        copy.start()
+            one(GROUP * g + b, k, at)
+
+    stores = []
+    for at in range(many):
+        acc[at] = jnp.zeros(acc.shape[1:], F32)
+        for k in range(parts):
+            if at == 0:
+                for copy, needed in packs[k]:
+                    pl.when(needed)(copy.wait)
+            loop(*ranges[k], lambda g, k=k, at=at: group(g, k, at))
+        for which, part in enumerate((slice(0, HALF), slice(HALF, PHASES))):
+            stores.append(pltpu.make_async_copy(acc.at[at, part], outs[2 * at + which], out_sem.at[len(stores)]))
+            stores[-1].start()
     for copy in stores:
         copy.wait()
 
 
-def finish_level(level, meta, plan, parts):
+def finish_levels(levels, meta, plan, parts):
     any_space = pl.BlockSpec(memory_space=pltpu.HBM)
     smem = pl.BlockSpec(memory_space=pltpu.SMEM)
     shape = jax.ShapeDtypeStruct((HALF, 5, 2, 8, WIDTH), F32)
-    cuts = [level_cuts(part[2], level) if level < 3 else () for part in parts]
-    packs = [piece for part, some in zip(parts, cuts) for side in part[3:5] for piece in side[:len(some)]]
+    many = len(levels)
+    cuts = [part[2] for part in parts]
+    strips = [part[1][level] for part in parts for level in levels]
+    packs = [piece for part in parts for side in part[3:5] for piece in side]
     chunks = sum(2 * (-(-(high - low) // CHUNK)) for some in cuts for low, high in zip((0,) + some[:-1], some))
-    rooms = [some[-1] + GAP for some in cuts if some]
-    return pl.pallas_call(
-        functools.partial(finish_kernel, level, cuts),
-        in_specs=[smem] * (2 + len(parts)) + [any_space] * (len(parts) + len(packs)),
-        out_specs=[any_space] * 2,
-        out_shape=[shape] * 2,
+    out = pl.pallas_call(
+        functools.partial(finish_kernel, levels, cuts),
+        in_specs=[smem] * (2 + len(parts)) + [any_space] * (len(strips) + len(packs)),
+        out_specs=[any_space] * (2 * many),
+        out_shape=[shape] * (2 * many),
         scratch_shapes=[
-            pltpu.VMEM((PHASES, 5, 2, 8, WIDTH), F32),
-            pltpu.VMEM((SNAPS, 2, 2, 8, WIDTH), F32),
-        ] + [pltpu.VMEM((2, room, WIDTH), F32) for room in rooms for _ in range(2)] + [
-            pltpu.SemaphoreType.DMA((GROUPS,)),
-            pltpu.SemaphoreType.DMA((max(chunks, 1),)),
+            pltpu.VMEM((many, PHASES, 5, 2, 8, WIDTH), F32),
+            pltpu.VMEM((many, SNAPS, 2, 2, 8, WIDTH), F32),
+        ] + [pltpu.VMEM((2, some[-1] + GAP, WIDTH), F32) for some in cuts for _ in range(2)] + [
+            pltpu.SemaphoreType.DMA((many, GROUPS)),
+            pltpu.SemaphoreType.DMA((2 * many,)),
+            pltpu.SemaphoreType.DMA((chunks,)),
         ],
         compiler_params=pltpu.CompilerParams(vmem_limit_bytes=62 * MIB),
-        name="finish_level",
-    )(meta, plan, *[part[0] for part in parts], *[part[1][level] for part in parts], *packs)
-
-
-def scale_kernel(levels, block, message, reply, *refs):
+        name="finish_levels",
+    )(meta, plan, *[part[0] for part in parts], *strips, *packs)
+    return [(out[2 * at], out[2 * at + 1]) for at in range(many)]
+
+
+def scale_work(levels, message, reply, mines, others, mean, moment, a_buf, b_buf, load_sem, store_sem):
     many = len(levels)
-    mines, others = refs[:many], refs[many:2 * many]
-    mean, moment, a_buf, b_buf, load_sem, store_sem = refs[-6:]
-    parts = [(k, slice(start, start + block)) for k in range(many) for start in range(0, HALF, block)]
+    parts = [(k, slice(start, start + BLOCK)) for k in range(many) for start in range(0, HALF, BLOCK)]
     loads, stores = [], []
     for at, (k, part) in enumerate(parts):
         loads.append([pltpu.make_async_copy(mines[k].at[part], a_buf.at[k, part], load_sem.at[2 * at]),
@@ -456,39 +462,59 @@
                 group.append(pltpu.make_async_copy(
                     a_buf.at[k, part, fields, place], out.at[part, :, rows], store_sem.at[4 * at + 2 * place + which]))
         stores.append(group)
-    for copies in loads:
-        for copy in copies:
-            copy.start()
-    for at, (k, part) in enumerate(parts):
-        for copy in loads[at]:
-            copy.wait()
-
-        def one(p, carry, k=k):
-            count = jnp.full((8, WIDTH), message[0, p] + reply[0, HALF + p], I32).astype(F32)
-            a_buf[k, p] = (a_buf[k, p] + b_buf[k, p]) * (1.0 / jnp.maximum(count, 1.0))
-            return carry
-
-        lax.fori_loop(part.start, part.stop, one, 0, unroll=2)
-        for copy in stores[at]:
-            copy.start()
-    for copies in stores:
-        for copy in copies:
-            copy.wait()
+
+    def begin():
+        for copies in loads:
+            for copy in copies:
+                copy.start()
+
+    def work():
+        for at, (k, part) in enumerate(parts):
+            for copy in loads[at]:
+                copy.wait()
+
+            def one(p, carry, k=k):
+                count = jnp.full((8, WIDTH), message[0, p] + reply[0, HALF + p], I32).astype(F32)
+                a_buf[k, p] = (a_buf[k, p] + b_buf[k, p]) * (1.0 / jnp.maximum(count, 1.0))
+                return carry
+
+            lax.fori_loop(part.start, part.stop, one, 0, unroll=2)
+            for copy in stores[at]:
+                copy.start()
+
+    def end():
+        for copies in stores:
+            for copy in copies:
+                copy.wait()
+
+    return begin, work, end
+
+
+def scale_scratch(many):
+    parts = many * HALF // BLOCK
+    buffer = pltpu.VMEM((many, HALF, 5, 2, 8, WIDTH), F32)
+    return [buffer, buffer, pltpu.SemaphoreType.DMA((2 * parts,)), pltpu.SemaphoreType.DMA((4 * parts,))]
+
+
+OUTPUTS = [jax.ShapeDtypeStruct((HALF, 2, ROWS, WIDTH), F32), jax.ShapeDtypeStruct((HALF, 3, ROWS, WIDTH), F32)]
+
+
+def scale_kernel(levels, message, reply, *refs):
+    many = len(levels)
+    for step in scale_work(levels, message, reply, refs[:many], refs[many:2 * many], *refs[-6:]):
+        step()
 
 
 def scale_levels(levels, counts, pairs, before):
-    block = 18
     many = len(levels)
-    parts = many * HALF // block
     smem = pl.BlockSpec(memory_space=pltpu.SMEM)
     hbm = pl.BlockSpec(memory_space=pltpu.HBM)
-    buffer = pltpu.VMEM((many, HALF, 5, 2, 8, WIDTH), F32)
     return pl.pallas_call(
-        functools.partial(scale_kernel, levels, block),
+        functools.partial(scale_kernel, levels),
         in_specs=[smem] * 2 + [hbm] * (2 * many + len(before)),
         out_specs=[hbm] * 2,
-        out_shape=[jax.ShapeDtypeStruct((HALF, 2, ROWS, WIDTH), F32), jax.ShapeDtypeStruct((HALF, 3, ROWS, WIDTH), F32)],
-        scratch_shapes=[buffer, buffer, pltpu.SemaphoreType.DMA((2 * parts,)), pltpu.SemaphoreType.DMA((4 * parts,))],
+        out_shape=OUTPUTS,
+        scratch_shapes=scale_scratch(many),
         input_output_aliases={2 + 2 * many: 0, 3 + 2 * many: 1} if before else {},
         compiler_params=pltpu.CompilerParams(vmem_limit_bytes=62 * MIB),
         name="scale_levels",
@@ -505,8 +531,13 @@
     for target in (to_up, to_dn, to_core):
         pl.semaphore_signal(barrier, inc=1, device_id=target, device_id_type=pl.DeviceIdType.MESH)
     pl.semaphore_wait(barrier, 3)
+    rows = up.shape[1] // SPLIT
+    moves = [(theirs, other, to_core), (message, reply, to_core)]
+    for at in range(SPLIT):
+        part = slice(rows * at, rows * (at + 1))
+        moves += [(up.at[:, part], below.at[:, part], to_up), (dn.at[:, part], above.at[:, part], to_dn)]
     copies = []
-    for source, landing, target in ((up, below, to_up), (dn, above, to_dn), (theirs, other, to_core), (message, reply, to_core)):
+    for source, landing, target in moves:
         copies.append(pltpu.make_async_remote_copy(
             src_ref=source, dst_ref=landing, send_sem=send_sem.at[len(copies)], recv_sem=recv_sem.at[len(copies)],
             device_id=target, device_id_type=pl.DeviceIdType.MESH))
@@ -523,7 +554,7 @@
         in_specs=[any_space] * 4,
         out_specs=[any_space] * 4,
         out_shape=[jax.ShapeDtypeStruct(value.shape, value.dtype) for value in (up, dn, theirs, message)],
-        scratch_shapes=[pltpu.SemaphoreType.DMA((4,)), pltpu.SemaphoreType.DMA((4,))],
+        scratch_shapes=[pltpu.SemaphoreType.DMA((2 + 2 * SPLIT,)), pltpu.SemaphoreType.DMA((2 + 2 * SPLIT,))],
         compiler_params=pltpu.CompilerParams(collective_id=0, has_side_effects=True, vmem_limit_bytes=62 * MIB),
         name="exchange",
     )(up, dn, theirs, message)
@@ -568,9 +599,10 @@
     smooth = functools.partial(smooth_part, velocity=velocity, colop=colop, rowop=rowop)
 
     def full(counts, *_):
-        strips, sums, up, dn, positions, plan = smooth(2, meta, jnp.zeros((16,), I32), cuts=FULL_CUTS)
+        strips, sums, up, dn, positions, plan = smooth(2, meta, meta, cuts=FULL_CUTS)
         below, above = send(up, dn)
-        totals = [finish_level(level, meta, plan, [(positions, strips, FULL_CUTS, below, above)]) for level in range(3)]
+        part = (positions, strips, FULL_CUTS, below, above)
+        totals = finish_levels((0, 1), meta, plan, [part]) + finish_levels((2,), meta, plan, [part])
         totals = [(mine, to_partner(theirs)) for mine, theirs in (sums, *totals)]
         before = scale_levels((3, 0), counts, totals[:2], ())
         return tuple(scale_levels((1, 2), counts, totals[2:], before))
@@ -578,7 +610,7 @@
     def last(counts, mine, other, mean, moment):
         return tuple(scale_levels((2,), counts, [(mine, other)], (mean, moment)))
 
-    strips_a, _, up_a, dn_a, pos_a, plan = smooth(0, meta, jnp.zeros((16,), I32), cuts=FIRST_CUTS)
+    strips_a, _, up_a, dn_a, pos_a, plan = smooth(0, meta, meta, cuts=FIRST_CUTS)
     below_a, above_a = send(up_a, dn_a)
     message = jnp.broadcast_to(jnp.concatenate([own, plan[8:], jnp.zeros((48,), I32)])[None], (8, 128))
     strips_b, sums, up_b, dn_b, pos_b, _ = smooth(1, meta, plan, cuts=REST_CUTS, early=(strips_a[3],))
@@ -586,10 +618,11 @@
     counts = (message, reply)
     over = jnp.max(jnp.maximum(message, reply)[0:1, PHASES:PHASES + 8])
     parts = [(pos_a, strips_a, FIRST_CUTS, below_a, above_a), (pos_b, strips_b, REST_CUTS, [below_b], [above_b])]
-    totals = [finish_level(level, meta, plan, parts) for level in range(3)]
-    totals = [(sums[0], other)] + [(mine, to_partner(theirs)) for mine, theirs in totals]
-    before = scale_levels((3, 0, 1), counts, totals[:3], ())
-    return lax.cond(over <= 0, last, full, counts, *totals[3], *before)
+    totals = finish_levels((0, 1), meta, plan, parts) + finish_levels((2,), meta, plan, parts)
+    totals = [(mine, to_partner(theirs)) for mine, theirs in totals]
+    before = scale_levels((3,), counts, [(sums[0], other)], ())
+    before = scale_levels((0, 1), counts, totals[:2], before)
+    return lax.cond(over <= 0, last, full, counts, *totals[2], *before)
 
 
 def solution(mesh):

time: 146 us -> 146 us (level)
    pallas_call x5, Pallas kernels: 37.9 us -> 35.6 us  [the longest x2 18.4 us: finish_levels(): pl.pallas_call(functools.partial(finish_kernel, levels, cuts), in_specs=[...]
    pallas_call x1, Pallas kernels: 53 us -> 54.5 us  [exchange(): pl.pallas_call(exchange_kernel, in_specs=[any_space] * 4, out_specs=[any_...]
  transfers between devices with their start and end apart: 5 -> 5, of which waited for: 0 -> 0; matrix products, arithmetic and copies ran while one was open for 1% -> 1% of each run, Pallas kernels for 70% -> 66%
where the time goes in v7:
time: 146 us; the launch traced here: 145 us
  Pallas kernels  127 us (87%)
  starting transfers between devices  12.2 us (8%)
  local copies, waits for them, and re-layouts  2.6 us (2%)
  between operations  1.62 us (1%)
  other arithmetic  1.57 us (1%)
    pallas_call x1, Pallas kernels, exchange(): pl.pallas_call(exchange_kernel, in_specs=[any_space] * 4, out_specs=[any_...  54.5 us
    pallas_call x2, Pallas kernels, smooth_part(): pl.pallas_call(functools.partial(smooth_kernel, part, cuts), in_specs=[sm...  37 us
    pallas_call x2, Pallas kernels, finish_levels(): pl.pallas_call(functools.partial(finish_kernel, levels, cuts), in_specs=[...  18.4 us
    pallas_call x3, Pallas kernels, scale_levels(): pl.pallas_call(functools.partial(scale_kernel, levels), in_specs=[smem] *...  17.2 us
    ppermute x1, starting transfers between devices, to_above(): return lax.ppermute(value, 'tile', [(i + 1, i) for i in range(size - 1)])  6.67 us
    ppermute x3, starting transfers between devices, to_partner(): return lax.ppermute(value, 'snap', [(0, 1), (1, 0)])  3.58 us
  transfers between devices with their start and end apart: 5, of which 0 were waited for; matrix products, arithmetic and copies ran while one was open for 1% of the time, Pallas kernels for 66%

profile of v7, /device:TPU:97, one launch (start us, length us, event | category | flops | bytes accessed | tf_op | source)
XLA Modules:
  0.0 145.4 jit_solution(14267783892227247771)
XLA Ops:
  0.6 0.8 slice_bitcast_fusion.1
  1.4 0.7 subtract_remainder_fusion
  2.1 0.0 copy-start.1
  2.1 15.3 %smooth_part.4 = (f32[128,2,2,8,256]{4,3,2,1,0:T(8,128)}, f32[128,2,2,8,256]{4,3,2,1,0:T(8,128)}, f32[128,2,2,8,256]{4,3,2,1,0:T(8,128)}, f32[128,2,2,8,256]{4,3...) custom-call(s32[385]{0:T(512)S(1)} %pad_add_fusion.meta.plan, ...), custom_call_target="tpu_custom_call" | custom-call | tf_op jit(solution)/shard_map/smooth_part/pallas_call | solution.py:307
  17.4 6.7 %collective-permute-start.6 = (f32[2,640,256]{2,1,0:T(8,128)}, f32[2,640,256]{2,1,0:T(8,128)S(1)}, u32[]{:S(2)}, u32[]{:S(2)}) collective-permute-start(f32[2,640,256]{2,1,0:T(8,128)} %get-tuple-element.95), channel_id=1, source_target_pairs={{1,0},{2,1},{3,2},{4,3},{5,4},{6,5},{7,6},{8,7},{9,8},{10,9},{11,1... | collective-permute-start | bytes 3932168 | tf_op jit(solution)/shard_map/ppermute | solution.py:569
  24.1 1.9 %collective-permute-start.7 = (f32[2,640,256]{2,1,0:T(8,128)}, f32[2,640,256]{2,1,0:T(8,128)}, u32[]{:S(2)}, u32[]{:S(2)}) collective-permute-start(f32[2,640,256]{2,1,0:T(8,128)} %get-tuple-element.96), channel_id=1, source_target_pairs={{0,1},{1,2},{2,3},{3,4},{4,5},{5,6},{6,7},{7,8},{8,9},{9,10},{10,1... | collective-permute-start | bytes 3932168 | tf_op jit(solution)/shard_map/ppermute | solution.py:574
  26.0 0.7 slice.14
  26.8 0.0 copy-done.1
  26.8 21.7 %smooth_part.5 = (f32[128,2,2,8,256]{4,3,2,1,0:T(8,128)}, f32[128,2,2,8,256]{4,3,2,1,0:T(8,128)}, f32[128,2,2,8,256]{4,3,2,1,0:T(8,128)}, f32[36,5,2,8,256]{4,3,...) custom-call(s32[385]{0:T(512)S(1)} %pad_add_fusion.meta.plan, ...), custom_call_target="tpu_custom_call" | custom-call | tf_op jit(solution)/shard_map/smooth_part/pallas_call | solution.py:307
  48.5 0.1 convert_reduce_fusion
  48.6 0.1 pad_add_fusion.1
  48.7 54.5 %exchange.1 = (f32[2,1008,256]{2,1,0:T(8,128)}, f32[2,1008,256]{2,1,0:T(8,128)}, f32[36,5,2,8,256]{4,3,2,1,0:T(8,128)}, s32[8,128]{1,0:T(8,128)S(1)}) custom-call(f32[2,1008,256]{2,1,0:T(8,128)} %get-tuple-element.87.up, f32[2,1008,256]{2,1,0:T(8,128)} %get-tuple-element.88.dn, f32[36,5,2,8,256]{4,3,2,1,0:T(8,128)} %get-tuple-element.89.theirs, ...), custom_call_target="tpu_custom_call" | custom-call | tf_op jit(solution)/shard_map/exchange/pallas_call | solution.py:552
  103.2 0.0 collective-permute-done.6.refs_4_.refs_6_
  103.2 0.0 copy-start
  103.2 0.0 collective-permute-done.7.refs_5_.refs_7_
  103.2 1.1 copy-done
  104.3 11.0 %finish_levels.7 = (f32[36,5,2,8,256]{4,3,2,1,0:T(8,128)}, f32[36,5,2,8,256]{4,3,2,1,0:T(8,128)}, f32[36,5,2,8,256]{4,3,2,1,0:T(8,128)}, f32[36,5,2,8,256]{4,3,2,1,0:T(8,128)}) custom-call(s32[385]{0:T(512)S(1)} %pad_add_fusion.meta.plan, s32[16]{0:T(128)} %get-tuple-element.85.plan, s32[768]{0:T(1024)} %get-tuple-element.91.refs_0_, ...), custom_call_target="tpu_custom_call" | custom-call | tf_op jit(solution)/shard_map/finish_levels/pallas_call | solution.py:431
  115.3 3.0 %collective-permute-start.9 = (f32[36,5,2,8,256]{4,3,2,1,0:T(8,128)}, f32[36,5,2,8,256]{4,3,2,1,0:T(8,128)}, u32[]{:S(2)}, u32[]{:S(2)}) collective-permute-start(f32[36,5,2,8,256]{4,3,2,1,0:T(8,128)} %get-tuple-element.107), channel_id=1, source_target_pairs={{0,64},{64,0},{1,65},{65,1},{2,66},{66,2},{3,67},{67,3},{4,68},{68... | collective-permute-start | bytes 8847368 | tf_op jit(solution)/shard_map/ppermute | solution.py:564
  118.3 0.1 collective-permute-start.10
  118.4 7.4 %finish_levels.6 = (f32[36,5,2,8,256]{4,3,2,1,0:T(8,128)}, f32[36,5,2,8,256]{4,3,2,1,0:T(8,128)}) custom-call(s32[385]{0:T(512)S(1)} %pad_add_fusion.meta.plan, s32[16]{0:T(128)} %get-tuple-element.85.plan, s32[768]{0:T(1024)} %get-tuple-element.91.refs_0_, s32[768]{0:T(1024)} %get-tuple-element.92.refs_1_, ...), custom_call_target="tpu_custom_call" | custom-call | tf_op jit(solution)/shard_map/finish_levels/pallas_call | solution.py:431
  125.8 0.5 collective-permute-start.8
  126.3 0.7 slice_reduce_fusion
  127.6 4.8 %scale_levels.8 = (f32[36,2,64,256]{3,2,1,0:T(8,128)}, f32[36,3,64,256]{3,2,1,0:T(8,128)}) custom-call(s32[8,128]{1,0:T(8,128)S(1)} %broadcast_in_dim.16.message, s32[8,128]{1,0:T(8,128)S(1)} %get-tuple-element.90.reply, f32[36,5,2,8,256]{4,3,2,1,0:T(8,128)} %get-tuple-element.109.refs_0_, f32[36,5,2,8,256]{4,3,2,1,0:T(8,128)} %get-tuple-element.110.refs_1_), custom_call_target="tpu_custom_call" | custom-call | tf_op jit(solution)/shard_map/scale_levels/pallas_call | solution.py:512
  132.4 0.0 collective-permute-done.9.refs_2_
  132.5 0.0 collective-permute-done.10.refs_3_
  132.5 7.7 %scale_levels.9 = (f32[36,2,64,256]{3,2,1,0:T(8,128)}, f32[36,3,64,256]{3,2,1,0:T(8,128)}) custom-call(s32[8,128]{1,0:T(8,128)S(1)} %broadcast_in_dim.16.message, s32[8,128]{1,0:T(8,128)S(1)} %get-tuple-element.90.reply, f32[36,5,2,8,256]{4,3,2,1,0:T(8,128)} %get-tuple-element.105.refs_0_, ...), custom_call_target="tpu_custom_call", output_to_operand_aliasing={{0}: (6, {}), {1}: (7, {})} | custom-call | tf_op jit(solution)/shard_map/scale_levels/pallas_call | solution.py:512
  140.1 0.0 collective-permute-done.8
  140.1 5.0 %conditional.1 = ((f32[36,2,64,256]{3,2,1,0:T(8,128)}, f32[36,3,64,256]{3,2,1,0:T(8,128)})) conditional(s32[]{:T(128)} %convert_element_type.7, (s32[385]{0:T(512)S(1)}, f32[128,2,64,256]{3,2,1,0:T(8,128)}, bf16[768,256]{1,0:T(8,128)(2,1)S(1)}, bf16[3,33,112,192]{3,2,1,0:T(8,128)(2,1)}, s32[8,128]{1,0:T(8,128)S(1)}, ...), branch_computations={%region_2.3_spmd, %region_3.4_spmd} | conditional | bytes 98566392 | solution.py:625
  140.4 4.8 %scale_levels.7 = (f32[36,2,64,256]{3,2,1,0:T(8,128)}, f32[36,3,64,256]{3,2,1,0:T(8,128)}) custom-call(s32[8,128]{1,0:T(8,128)S(1)} %get-tuple-element.47.message, s32[8,128]{1,0:T(8,128)S(1)} %get-tuple-element.48.reply, f32[36,5,2,8,256]{4,3,2,1,0:T(8,128)} %get-tuple-element.49.refs_0_, ...), custom_call_target="tpu_custom_call", output_to_operand_aliasing={{0}: (4, {}), {1}: (5, {})} | custom-call | tf_op jit(solution)/shard_map/cond/branch_1_fun/scale_levels/pallas_call | solution.py:512
  (4 shorter events, 0.0 us)
Async XLA Ops:
  2.1 24.7 %copy-start.1 = (bf16[768,256]{1,0:T(8,128)(2,1)S(1)}, bf16[768,256]{1,0:T(8,128)(2,1)}, u32[]{:S(2)}) copy-start(bf16[768,256]{1,0:T(8,128)(2,1)} %constant.28.clone.refs_1_) | copy-start | bytes 1179652
  17.4 85.7 %collective-permute-start.6 = (f32[2,640,256]{2,1,0:T(8,128)}, f32[2,640,256]{2,1,0:T(8,128)S(1)}, u32[]{:S(2)}, u32[]{:S(2)}) collective-permute-start(f32[2,640,256]{2,1,0:T(8,128)} %get-tuple-element.95), channel_id=1, source_target_pairs={{1,0},{2,1},{3,2},{4,3},{5,4},{6,5},{7,6},{8,7},{9,8},{10,9},{11,1... | collective-permute-start | bytes 3932168 | tf_op jit(solution)/shard_map/ppermute | solution.py:569
  24.1 79.1 %collective-permute-start.7 = (f32[2,640,256]{2,1,0:T(8,128)}, f32[2,640,256]{2,1,0:T(8,128)}, u32[]{:S(2)}, u32[]{:S(2)}) collective-permute-start(f32[2,640,256]{2,1,0:T(8,128)} %get-tuple-element.96), channel_id=1, source_target_pairs={{0,1},{1,2},{2,3},{3,4},{4,5},{5,6},{6,7},{7,8},{8,9},{9,10},{10,1... | collective-permute-start | bytes 3932168 | tf_op jit(solution)/shard_map/ppermute | solution.py:574
  103.2 1.1 copy-start
  115.3 17.1 %collective-permute-start.9 = (f32[36,5,2,8,256]{4,3,2,1,0:T(8,128)}, f32[36,5,2,8,256]{4,3,2,1,0:T(8,128)}, u32[]{:S(2)}, u32[]{:S(2)}) collective-permute-start(f32[36,5,2,8,256]{4,3,2,1,0:T(8,128)} %get-tuple-element.107), channel_id=1, source_target_pairs={{0,64},{64,0},{1,65},{65,1},{2,66},{66,2},{3,67},{67,3},{4,68},{68... | collective-permute-start | bytes 8847368 | tf_op jit(solution)/shard_map/ppermute | solution.py:564
  118.3 14.1 %collective-permute-start.10 = (f32[36,5,2,8,256]{4,3,2,1,0:T(8,128)}, f32[36,5,2,8,256]{4,3,2,1,0:T(8,128)}, u32[]{:S(2)}, u32[]{:S(2)}) collective-permute-start(f32[36,5,2,8,256]{4,3,2,1,0:T(8,128)} %get-tuple-element.108), channel_id=1, source_target_pairs={{0,64},{64,0},{1,65},{65,1},{2,66},{66,2},{3,67},{67,3},{4,68},{68... | collective-permute-start | bytes 8847368 | tf_op jit(solution)/shard_map/ppermute | solution.py:564
  125.8 14.3 %collective-permute-start.8 = (f32[36,5,2,8,256]{4,3,2,1,0:T(8,128)}, f32[36,5,2,8,256]{4,3,2,1,0:T(8,128)}, u32[]{:S(2)}, u32[]{:S(2)}) collective-permute-start(f32[36,5,2,8,256]{4,3,2,1,0:T(8,128)} %get-tuple-element.100), channel_id=1, source_target_pairs={{0,64},{64,0},{1,65},{65,1},{2,66},{66,2},{3,67},{67,3},{4,68},{68... | collective-permute-start | bytes 8847368 | tf_op jit(solution)/shard_map/ppermute | solution.py:564

commit v8 on v7

--- a/solution.py
+++ b/solution.py
@@ -20,11 +20,11 @@
 GROUP = 8
 CHUNK = 128
 BLOCK = 18
-SPLIT = 6
+SPLIT = 4
 GAP = 16
 MIB = 1024 * 1024
-FIRST_CUTS = (640,)
-REST_CUTS = (1008,)
+FIRST_CUTS = (576,)
+REST_CUTS = (1024,)
 FULL_CUTS = (3072 + 64,)
 GROUPS = SNAPS // 8
 F32 = jnp.float32
@@ -452,9 +452,13 @@
     parts = [(k, slice(start, start + BLOCK)) for k in range(many) for start in range(0, HALF, BLOCK)]
     loads, stores = [], []
     for at, (k, part) in enumerate(parts):
-        loads.append([pltpu.make_async_copy(mines[k].at[part], a_buf.at[k, part], load_sem.at[2 * at]),
-                      pltpu.make_async_copy(others[k].at[part], b_buf.at[k, part], load_sem.at[2 * at + 1])])
+        loads.append([pltpu.make_async_copy(mines[k].at[part], a_buf.at[k, part], load_sem.at[2 * at])])
+        if others[k] is not None:
+            loads[-1].append(pltpu.make_async_copy(others[k].at[part], b_buf.at[k, part], load_sem.at[2 * at + 1]))
         group = []
+        if moment is None:
+            stores.append([pltpu.make_async_copy(a_buf.at[k, part], mean.at[part], store_sem.at[4 * at])])
+            continue
         for place in range(2):
             first = 8 * levels[k] if place == 0 else ROWS - 8 - 8 * levels[k]
             rows = slice(first, first + 8)
@@ -478,7 +482,8 @@
                 a_buf[k, p] = (a_buf[k, p] + b_buf[k, p]) * (1.0 / jnp.maximum(count, 1.0))
                 return carry
 
-            lax.fori_loop(part.start, part.stop, one, 0, unroll=2)
+            if others[k] is not None:
+                lax.fori_loop(part.start, part.stop, one, 0, unroll=2)
             for copy in stores[at]:
                 copy.start()
 
@@ -499,29 +504,35 @@
 OUTPUTS = [jax.ShapeDtypeStruct((HALF, 2, ROWS, WIDTH), F32), jax.ShapeDtypeStruct((HALF, 3, ROWS, WIDTH), F32)]
 
 
-def scale_kernel(levels, message, reply, *refs):
+def scale_kernel(levels, ready, message, reply, *refs):
     many = len(levels)
-    for step in scale_work(levels, message, reply, refs[:many], refs[many:2 * many], *refs[-6:]):
+    pairs, mines, others = list(refs), [], []
+    for level in levels:
+        mines.append(pairs.pop(0))
+        others.append(None if level == 3 and ready else pairs.pop(0))
+    for step in scale_work(levels, message, reply, mines, others, *refs[-6:]):
         step()
 
 
-def scale_levels(levels, counts, pairs, before):
+def scale_levels(levels, counts, pairs, before, ready=False):
     many = len(levels)
+    sums = [value for pair in pairs for value in pair]
     smem = pl.BlockSpec(memory_space=pltpu.SMEM)
     hbm = pl.BlockSpec(memory_space=pltpu.HBM)
     return pl.pallas_call(
-        functools.partial(scale_kernel, levels),
-        in_specs=[smem] * 2 + [hbm] * (2 * many + len(before)),
+        functools.partial(scale_kernel, levels, ready),
+        in_specs=[smem] * 2 + [hbm] * (len(sums) + len(before)),
         out_specs=[hbm] * 2,
         out_shape=OUTPUTS,
         scratch_shapes=scale_scratch(many),
-        input_output_aliases={2 + 2 * many: 0, 3 + 2 * many: 1} if before else {},
+        input_output_aliases={2 + len(sums): 0, 3 + len(sums): 1} if before else {},
         compiler_params=pltpu.CompilerParams(vmem_limit_bytes=62 * MIB),
         name="scale_levels",
-    )(*counts, *[pair[0] for pair in pairs], *[pair[1] for pair in pairs], *before)
-
-
-def exchange_kernel(up, dn, theirs, message, below, above, other, reply, send_sem, recv_sem):
+    )(*counts, *sums, *before)
+
+
+def exchange_kernel(up, dn, mine, theirs, message, counts, below, above, other, reply, middle, reply_counts, *refs):
+    *scratch, sem, send_sem, recv_sem = refs
     snap, tile = lax.axis_index("snap"), lax.axis_index("tile")
     size = lax.axis_size("tile")
     to_up = (snap, lax.rem(tile + size - 1, size))
@@ -543,21 +554,33 @@
             device_id=target, device_id_type=pl.DeviceIdType.MESH))
     for copy in copies:
         copy.start()
-    for copy in copies:
+    for copy in copies[:2]:
         copy.wait()
-
-
-def exchange(up, dn, theirs, message):
-    any_space = pl.BlockSpec(memory_space=pltpu.HBM)
+    fetch = pltpu.make_async_copy(reply, reply_counts, sem.at[0])
+    fetch.start()
+    fetch.wait()
+    for step in scale_work((3,), counts, reply_counts, [mine], [other], middle, None, *scratch):
+        step()
+    for copy in copies[2:]:
+        copy.wait()
+
+
+def exchange(up, dn, sums, message):
+    hbm = pl.BlockSpec(memory_space=pltpu.HBM)
+    sends = (up, dn, sums[1], message)
     return pl.pallas_call(
         exchange_kernel,
-        in_specs=[any_space] * 4,
-        out_specs=[any_space] * 4,
-        out_shape=[jax.ShapeDtypeStruct(value.shape, value.dtype) for value in (up, dn, theirs, message)],
-        scratch_shapes=[pltpu.SemaphoreType.DMA((2 + 2 * SPLIT,)), pltpu.SemaphoreType.DMA((2 + 2 * SPLIT,))],
+        in_specs=[hbm] * 5 + [pl.BlockSpec(memory_space=pltpu.SMEM)],
+        out_specs=[hbm] * 5,
+        out_shape=[jax.ShapeDtypeStruct(value.shape, value.dtype) for value in (*sends, sums[0])],
+        scratch_shapes=[pltpu.SMEM((8, 128), I32)] + scale_scratch(1) + [
+            pltpu.SemaphoreType.DMA((1,)),
+            pltpu.SemaphoreType.DMA((2 + 2 * SPLIT,)),
+            pltpu.SemaphoreType.DMA((2 + 2 * SPLIT,)),
+        ],
         compiler_params=pltpu.CompilerParams(collective_id=0, has_side_effects=True, vmem_limit_bytes=62 * MIB),
         name="exchange",
-    )(up, dn, theirs, message)
+    )(up, dn, *sums, message, message)
 
 
 def to_partner(value):
@@ -614,14 +637,13 @@
     below_a, above_a = send(up_a, dn_a)
     message = jnp.broadcast_to(jnp.concatenate([own, plan[8:], jnp.zeros((48,), I32)])[None], (8, 128))
     strips_b, sums, up_b, dn_b, pos_b, _ = smooth(1, meta, plan, cuts=REST_CUTS, early=(strips_a[3],))
-    below_b, above_b, other, reply = exchange(up_b[0], dn_b[0], sums[1], message)
+    below_b, above_b, _, reply, middle = exchange(up_b[0], dn_b[0], sums, message)
     counts = (message, reply)
     over = jnp.max(jnp.maximum(message, reply)[0:1, PHASES:PHASES + 8])
     parts = [(pos_a, strips_a, FIRST_CUTS, below_a, above_a), (pos_b, strips_b, REST_CUTS, [below_b], [above_b])]
     totals = finish_levels((0, 1), meta, plan, parts) + finish_levels((2,), meta, plan, parts)
     totals = [(mine, to_partner(theirs)) for mine, theirs in totals]
-    before = scale_levels((3,), counts, [(sums[0], other)], ())
-    before = scale_levels((0, 1), counts, totals[:2], before)
+    before = scale_levels((3, 0, 1), counts, [(middle,), *totals[:2]], (), True)
     return lax.cond(over <= 0, last, full, counts, *totals[2], *before)
 
 

time: 146 us -> 140 us (0.959)
  Pallas kernels: 127 us -> 124 us
  starting transfers between devices: 12.2 us -> 9.83 us
    pallas_call x4 -> x3, Pallas kernels: 71.7 us -> 68.5 us  [the longest x1 54.1 us: exchange(): pl.pallas_call(exchange_kernel, in_specs=[hbm] * 5 + [pl.BlockSpec(memory...]
    ppermute x3, starting transfers between devices: 3.58 us -> 1.23 us  [to_partner(): return lax.ppermute(value, 'snap', [(0, 1), (1, 0)])]
  transfers between devices with their start and end apart: 5 -> 5, of which waited for: 0 -> 1; matrix products, arithmetic and copies ran while one was open for 1% -> 1% of each run, Pallas kernels for 66% -> 67%
where the time goes in v8:
time: 140 us
  Pallas kernels  124 us (89%)
  starting transfers between devices  9.83 us (7%)
  local copies, waits for them, and re-layouts  2.51 us (2%)
  between operations  1.6 us (1%)
  other arithmetic  1.57 us (1%)
    pallas_call x1, Pallas kernels, exchange(): pl.pallas_call(exchange_kernel, in_specs=[hbm] * 5 + [pl.BlockSpec(memory...  54.1 us
    pallas_call x2, Pallas kernels, smooth_part(): pl.pallas_call(functools.partial(smooth_kernel, part, cuts), in_specs=[sm...  37.3 us
    pallas_call x2, Pallas kernels, finish_levels(): pl.pallas_call(functools.partial(finish_kernel, levels, cuts), in_specs=[...  18.5 us
    pallas_call x2, Pallas kernels, scale_levels(): pl.pallas_call(functools.partial(scale_kernel, levels, ready), in_specs=[...  14.5 us
    ppermute x1, starting transfers between devices, to_above(): return lax.ppermute(value, 'tile', [(i + 1, i) for i in range(size - 1)])  6.67 us
  transfers between devices with their start and end apart: 5, of which 1 were waited for; matrix products, arithmetic and copies ran while one was open for 1% of the time, Pallas kernels for 67%

profile of v8, /device:TPU:97, one launch (start us, length us, event | category | flops | bytes accessed | tf_op | source)
XLA Modules:
  0.0 140.2 jit_solution(17053793304907772891)
XLA Ops:
  0.6 0.8 slice_bitcast_fusion.1
  1.4 0.7 subtract_remainder_fusion
  2.1 0.0 copy-start.1
  2.1 14.0 %smooth_part.4 = (f32[128,2,2,8,256]{4,3,2,1,0:T(8,128)}, f32[128,2,2,8,256]{4,3,2,1,0:T(8,128)}, f32[128,2,2,8,256]{4,3,2,1,0:T(8,128)}, f32[128,2,2,8,256]{4,3...) custom-call(s32[385]{0:T(512)S(1)} %pad_add_fusion.meta.plan, ...), custom_call_target="tpu_custom_call" | custom-call | tf_op jit(solution)/shard_map/smooth_part/pallas_call | solution.py:307
  16.1 6.7 %collective-permute-start.6 = (f32[2,576,256]{2,1,0:T(8,128)}, f32[2,576,256]{2,1,0:T(8,128)S(1)}, u32[]{:S(2)}, u32[]{:S(2)}) collective-permute-start(f32[2,576,256]{2,1,0:T(8,128)} %get-tuple-element.94), channel_id=1, source_target_pairs={{1,0},{2,1},{3,2},{4,3},{5,4},{6,5},{7,6},{8,7},{9,8},{10,9},{11,1... | collective-permute-start | bytes 3538952 | tf_op jit(solution)/shard_map/ppermute | solution.py:592
  22.8 1.9 %collective-permute-start.7 = (f32[2,576,256]{2,1,0:T(8,128)}, f32[2,576,256]{2,1,0:T(8,128)}, u32[]{:S(2)}, u32[]{:S(2)}) collective-permute-start(f32[2,576,256]{2,1,0:T(8,128)} %get-tuple-element.95), channel_id=1, source_target_pairs={{0,1},{1,2},{2,3},{3,4},{4,5},{5,6},{6,7},{7,8},{8,9},{9,10},{10,1... | collective-permute-start | bytes 3538952 | tf_op jit(solution)/shard_map/ppermute | solution.py:597
  24.7 0.7 slice.14
  25.4 0.0 copy-done.1
  25.4 23.3 %smooth_part.5 = (f32[128,2,2,8,256]{4,3,2,1,0:T(8,128)}, f32[128,2,2,8,256]{4,3,2,1,0:T(8,128)}, f32[128,2,2,8,256]{4,3,2,1,0:T(8,128)}, f32[36,5,2,8,256]{4,3,...) custom-call(s32[385]{0:T(512)S(1)} %pad_add_fusion.meta.plan, ...), custom_call_target="tpu_custom_call" | custom-call | tf_op jit(solution)/shard_map/smooth_part/pallas_call | solution.py:307
  48.7 0.1 convert_reduce_fusion
  48.8 0.1 pad_add_fusion.1
  48.9 54.1 %exchange.1 = (f32[2,1024,256]{2,1,0:T(8,128)}, f32[2,1024,256]{2,1,0:T(8,128)}, f32[36,5,2,8,256]{4,3,2,1,0:T(8,128)}, s32[8,128]{1,0:T(8,128)S(1)}, f32[36,5,2,8,256]{4,3,2,1,0:T(8,128)}) custom-call(f32[2,1024,256]{2,1,0:T(8,128)} %get-tuple-element.85.up, f32[2,1024,256]{2,1,0:T(8,128)} %get-tuple-element.86.dn, ...), custom_call_target="tpu_custom_call" | custom-call | tf_op jit(solution)/shard_map/exchange/pallas_call | solution.py:571
  102.9 0.0 collective-permute-done.6.refs_4_.refs_6_
  103.0 0.0 copy-start
  103.0 0.0 collective-permute-done.7.refs_5_.refs_7_
  103.0 1.0 copy-done
  104.0 11.1 %finish_levels.7 = (f32[36,5,2,8,256]{4,3,2,1,0:T(8,128)}, f32[36,5,2,8,256]{4,3,2,1,0:T(8,128)}, f32[36,5,2,8,256]{4,3,2,1,0:T(8,128)}, f32[36,5,2,8,256]{4,3,2,1,0:T(8,128)}) custom-call(s32[385]{0:T(512)S(1)} %pad_add_fusion.meta.plan, s32[16]{0:T(128)} %get-tuple-element.83.plan, s32[768]{0:T(1024)} %get-tuple-element.90.refs_0_, ...), custom_call_target="tpu_custom_call" | custom-call | tf_op jit(solution)/shard_map/finish_levels/pallas_call | solution.py:431
  115.1 0.6 collective-permute-start.9
  115.7 0.1 collective-permute-start.10
  115.8 7.4 %finish_levels.6 = (f32[36,5,2,8,256]{4,3,2,1,0:T(8,128)}, f32[36,5,2,8,256]{4,3,2,1,0:T(8,128)}) custom-call(s32[385]{0:T(512)S(1)} %pad_add_fusion.meta.plan, s32[16]{0:T(128)} %get-tuple-element.83.plan, s32[768]{0:T(1024)} %get-tuple-element.90.refs_0_, s32[768]{0:T(1024)} %get-tuple-element.91.refs_1_, ...), custom_call_target="tpu_custom_call" | custom-call | tf_op jit(solution)/shard_map/finish_levels/pallas_call | solution.py:431
  123.2 0.5 collective-permute-start.8
  123.7 0.7 slice_reduce_fusion
  125.1 0.0 collective-permute-done.9.refs_2_
  125.1 0.2 collective-permute-done.10.refs_4_
  125.3 9.7 %scale_levels.7 = (f32[36,2,64,256]{3,2,1,0:T(8,128)}, f32[36,3,64,256]{3,2,1,0:T(8,128)}) custom-call(s32[8,128]{1,0:T(8,128)S(1)} %broadcast_in_dim.16.message.counts, s32[8,128]{1,0:T(8,128)S(1)} %get-tuple-element.89.reply, f32[36,5,2,8,256]{4,3,2,1,0:T(8,128)} %get-tuple-element.100.refs_0_, f32[36,5,2,8,256]{4,3,2,1,0:T(8,128)} %get-tuple-element.105.refs_1_, ...), custom_call_target="tpu_custom_call" | custom-call | tf_op jit(solution)/shard_map/scale_levels/pallas_call | solution.py:522
  134.9 0.0 collective-permute-done.8
  135.0 5.0 %conditional.1 = ((f32[36,2,64,256]{3,2,1,0:T(8,128)}, f32[36,3,64,256]{3,2,1,0:T(8,128)})) conditional(s32[]{:T(128)} %convert_element_type.7, (s32[385]{0:T(512)S(1)}, f32[128,2,64,256]{3,2,1,0:T(8,128)}, bf16[768,256]{1,0:T(8,128)(2,1)S(1)}, bf16[3,33,112,192]{3,2,1,0:T(8,128)(2,1)}, s32[8,128]{1,0:T(8,128)S(1)}, ...), branch_computations={%region_2.3_spmd, %region_3.4_spmd} | conditional | bytes 98566392 | solution.py:647
  135.2 4.8 %scale_levels.6 = (f32[36,2,64,256]{3,2,1,0:T(8,128)}, f32[36,3,64,256]{3,2,1,0:T(8,128)}) custom-call(s32[8,128]{1,0:T(8,128)S(1)} %get-tuple-element.47.message, s32[8,128]{1,0:T(8,128)S(1)} %get-tuple-element.48.reply, f32[36,5,2,8,256]{4,3,2,1,0:T(8,128)} %get-tuple-element.49.refs_0_, ...), custom_call_target="tpu_custom_call", output_to_operand_aliasing={{0}: (4, {}), {1}: (5, {})} | custom-call | tf_op jit(solution)/shard_map/cond/branch_1_fun/scale_levels/pallas_call | solution.py:522
  (4 shorter events, 0.0 us)
Async XLA Ops:
  2.1 23.3 %copy-start.1 = (bf16[768,256]{1,0:T(8,128)(2,1)S(1)}, bf16[768,256]{1,0:T(8,128)(2,1)}, u32[]{:S(2)}) copy-start(bf16[768,256]{1,0:T(8,128)(2,1)} %constant.28.clone.refs_1_) | copy-start | bytes 1179652
  16.1 86.9 %collective-permute-start.6 = (f32[2,576,256]{2,1,0:T(8,128)}, f32[2,576,256]{2,1,0:T(8,128)S(1)}, u32[]{:S(2)}, u32[]{:S(2)}) collective-permute-start(f32[2,576,256]{2,1,0:T(8,128)} %get-tuple-element.94), channel_id=1, source_target_pairs={{1,0},{2,1},{3,2},{4,3},{5,4},{6,5},{7,6},{8,7},{9,8},{10,9},{11,1... | collective-permute-start | bytes 3538952 | tf_op jit(solution)/shard_map/ppermute | solution.py:592
  22.8 80.2 %collective-permute-start.7 = (f32[2,576,256]{2,1,0:T(8,128)}, f32[2,576,256]{2,1,0:T(8,128)}, u32[]{:S(2)}, u32[]{:S(2)}) collective-permute-start(f32[2,576,256]{2,1,0:T(8,128)} %get-tuple-element.95), channel_id=1, source_target_pairs={{0,1},{1,2},{2,3},{3,4},{4,5},{5,6},{6,7},{7,8},{8,9},{9,10},{10,1... | collective-permute-start | bytes 3538952 | tf_op jit(solution)/shard_map/ppermute | solution.py:597
  103.0 1.1 copy-start
  115.1 10.0 %collective-permute-start.9 = (f32[36,5,2,8,256]{4,3,2,1,0:T(8,128)}, f32[36,5,2,8,256]{4,3,2,1,0:T(8,128)}, u32[]{:S(2)}, u32[]{:S(2)}) collective-permute-start(f32[36,5,2,8,256]{4,3,2,1,0:T(8,128)} %get-tuple-element.106), channel_id=1, source_target_pairs={{0,64},{64,0},{1,65},{65,1},{2,66},{66,2},{3,67},{67,3},{4,68},{68... | collective-permute-start | bytes 8847368 | tf_op jit(solution)/shard_map/ppermute | solution.py:587
  115.7 9.6 %collective-permute-start.10 = (f32[36,5,2,8,256]{4,3,2,1,0:T(8,128)}, f32[36,5,2,8,256]{4,3,2,1,0:T(8,128)}, u32[]{:S(2)}, u32[]{:S(2)}) collective-permute-start(f32[36,5,2,8,256]{4,3,2,1,0:T(8,128)} %get-tuple-element.108), channel_id=1, source_target_pairs={{0,64},{64,0},{1,65},{65,1},{2,66},{66,2},{3,67},{67,3},{4,68},{68... | collective-permute-start | bytes 8847368 | tf_op jit(solution)/shard_map/ppermute | solution.py:587
  123.2 11.7 %collective-permute-start.8 = (f32[36,5,2,8,256]{4,3,2,1,0:T(8,128)}, f32[36,5,2,8,256]{4,3,2,1,0:T(8,128)}, u32[]{:S(2)}, u32[]{:S(2)}) collective-permute-start(f32[36,5,2,8,256]{4,3,2,1,0:T(8,128)} %get-tuple-element.99), channel_id=1, source_target_pairs={{0,64},{64,0},{1,65},{65,1},{2,66},{66,2},{3,67},{67,3},{4,68},{68... | collective-permute-start | bytes 8847368 | tf_op jit(solution)/shard_map/ppermute | solution.py:587
